TPU v7x, 512 devices: a whole 4x4x16 slice. The times are simulated.
512 devices in a mesh: section: 2 (over x_hi), blk: 128 (over y, x_lo, z), sta: 2 (over core).
Axes of the slice: x: 4 (x_hi: 2, x_lo: 2; x = x_hi * 2 + x_lo), y: 4, z: 16, core: 2. Of those that a mesh axis runs over, the one named last changes fastest.
Arguments:
- raw_traces: bfloat16 [1200, 327680], P(('section', 'sta'), 'blk'), may hold values from -600 to 600
- fir_taps: bfloat16 [60], replicated, may hold values from -0.75 to 0.75
- templates: bfloat16 [128, 1200, 256], P('blk', ('section', 'sta')), may hold values from -600 to 600
- start_offsets: int32 [128], P('blk'), may hold values from 0 to 128, as said below
- channel_mask: int32 [128, 1200], P('blk', ('section', 'sta')), may hold values from 0 to 1, as said below
- station_shifts: int32 [400], P(('section', 'sta')), may hold values from 0 to 64, as said below
Outputs:
- detection: float32 [128, 65536], P(('section', 'sta'), 'blk')
Inputs may be any that keep to these rules, and one draw needn't show every extreme that they name: `start_offsets`: some template starts at the last possible sample. `channel_mask`: every template uses at least one channel. `station_shifts`: some station has the shift 64.
All inputs are finite; a program needn't handle non-finite values.
Results may differ from a plain program's by a relative error of at most 0.0029.
Values may be sent and summed in bfloat16 or wider, within the bound.
No kernel may reach another device: no remote copies, remote signals or barrier semaphores. Data moves between devices by JAX's collectives and lax.ppermute only.
A program may use at most 128 MiB of HBM per device.

v0:
```python
import math

import jax
import jax.numpy as jnp
from jax import lax
from jax.sharding import PartitionSpec as P

TLEN = 128
NTAP = 60
DECIM = 5
SHIFT_MAX = 64


def from_behind(value, axis, steps):
    count = lax.axis_size(axis)
    initial, last = (max(0, -steps), min(count, count - steps))
    return lax.ppermute(value, axis, [(source, source + steps) for source in range(initial, last)])


def tap_matrix(fir_taps, block_len):
    padding = jnp.zeros((DECIM * block_len,), fir_taps.dtype)
    pattern = jnp.concatenate([fir_taps, padding])
    window_len = DECIM * block_len + NTAP - DECIM
    flat_taps = jnp.tile(pattern, block_len)[: block_len * window_len]
    return flat_taps.reshape(block_len, window_len)


def decimate(raw_window, fir_taps, out_len):
    block_len = math.gcd(out_len, 128)
    blocks = out_len // block_len
    channels = raw_window.shape[0]
    stride = DECIM * block_len
    needed = stride * (blocks + 1)
    padded = jnp.pad(raw_window, ((0, 0), (0, needed - raw_window.shape[1])))
    leading = padded[:, : stride * blocks].reshape(channels, blocks, stride)
    trailing = padded[:, stride:].reshape(channels, blocks, stride)[:, :, : NTAP - DECIM]
    windows = jnp.concatenate([leading, trailing], axis=2)
    weights = tap_matrix(fir_taps, block_len)
    result = jnp.einsum("cnw,bw->cnb", windows, weights, preferred_element_type=jnp.float32)
    return result.reshape(channels, out_len)


def skew_sum(product, lag_count):
    groups, taps_len, span_len = product.shape
    flat_vals = product.reshape(groups, taps_len * span_len)
    cut_at = (taps_len - 1) * (span_len + 1)
    lead_rows = flat_vals[:, :cut_at].reshape(groups, taps_len - 1, span_len + 1)[:, :, :lag_count]
    last_row = flat_vals[:, cut_at : cut_at + lag_count]
    return jnp.sum(lead_rows, axis=1) + last_row


def correlate(panel_rows, shifted, lag_count):
    total_rows = panel_rows.shape[0]
    group_size = math.gcd(total_rows, 8)
    grouped = panel_rows.reshape((total_rows // group_size, group_size) + panel_rows.shape[1:])

    def one_group(members):
        product = jnp.einsum("gck,cw->gkw", members, shifted, preferred_element_type=jnp.float32)
        return skew_sum(product, lag_count)

    lag_sums = lax.map(one_group, grouped)
    return lag_sums.reshape(total_rows, lag_count)


def cut_one(stored, begin_at, keep_flags):
    window = lax.dynamic_slice_in_dim(stored, begin_at, TLEN, axis=1)
    return window * keep_flags.astype(jnp.bfloat16)[:, None]


def apply_shifts(extended, chan_shift, span_len):
    current = extended
    for bit_pos in range(SHIFT_MAX.bit_length()):
        step_len = 1 << bit_pos
        moved = jnp.pad(current[:, step_len:], ((0, 0), (0, step_len)))
        taken = chan_shift // step_len % 2 == 1
        current = jnp.where(taken[:, None], moved, current)
    return current[:, :span_len]


def local(raw_traces, fir_taps, templates, start_offsets, channel_mask, station_shifts):
    channels, raw_len = raw_traces.shape
    lag_count = raw_len // DECIM
    rim_len = TLEN - 1 + SHIFT_MAX
    tap_rim = NTAP - DECIM
    following = from_behind(raw_traces[:, :tap_rim], "blk", -1)
    extended_raw = jnp.concatenate([raw_traces, following], axis=1)
    decimated = decimate(extended_raw, fir_taps, lag_count)
    powers = lax.psum(jnp.sum(decimated * decimated, axis=1), "blk")
    window_len = lag_count * lax.axis_size("blk")
    root_power = jnp.sqrt(powers / window_len + 1e-06)
    trace_rows = (decimated / root_power[:, None]).astype(jnp.bfloat16)
    trace_rim = from_behind(trace_rows[:, :rim_len], "blk", -1)
    extended = jnp.concatenate([trace_rows, trace_rim], axis=1)
    chan_shift = jnp.repeat(station_shifts, 3)
    span_len = lag_count + TLEN - 1
    shifted = apply_shifts(extended, chan_shift, span_len)
    panels = jax.vmap(cut_one)(templates, start_offsets, channel_mask)
    arrived = lax.all_gather(panels, "blk", axis=0, tiled=True)
    piece_sums = correlate(arrived, shifted, lag_count)
    piece_norms = jnp.sum(jnp.square(arrived.astype(jnp.float32)), axis=(1, 2))
    owned_sums, owned_norms = (
        lax.psum_scatter(piece_sums, ("section", "sta"), scatter_dimension=0, tiled=True),
        lax.psum_scatter(piece_norms, ("section", "sta"), scatter_dimension=0, tiled=True),
    )
    return owned_sums / jnp.sqrt(owned_norms + 1e-05)[:, None]


def solution(mesh):
    return jax.shard_map(
        local,
        mesh=mesh,
        in_specs=(
            P(("section", "sta"), "blk"),
            P(),
            P("blk", ("section", "sta"), None),
            P("blk"),
            P("blk", ("section", "sta")),
            P(("section", "sta")),
        ),
        out_specs=P(("section", "sta"), "blk"),
        check_vma=False,
    )
```

profile of v0, /device:TPU:1, one launch (start us, length us, event | category | flops | bytes accessed | tf_op | source)
XLA Modules:
  0.0 793.4 jit_solution(1413016920918277426)
XLA Ops:
  12.8 3.0 reshape.284
  20.8 2.2 multiply_reduce_fusion.1
  23.4 268.9 %psum.7 = f32[300]{0:T(512)S(1)} all-reduce(f32[300]{0:T(512)S(1)} %get-tuple-element.55), channel_id=1, replica_groups=mesh['section'=2,'blk'=128,'sta'=2] {'blk'}, use_global_device_ids=true, to_apply=%region_1.2 | all-reduce | flops 300 | bytes 2400 | tf_op jit(solution)/shard_map/psum | solution.py:88
  293.9 5.2 collective-permute-done.1
  301.8 236.6 %all-gather.2.cloned.1.call-done = bf16[128,300,128]{2,1,0:T(8,128)(2,1)} async-done(((bf16[1,300,128]{2,1,0:T(8,128)(2,1)}), bf16[128,300,128]{2,1,0:T(8,128)(2,1)}) %all-gather.2.cloned.1.call-update) | async-done | bytes 9830416 | tf_op jit(solution)/shard_map/all_gather | solution.py:98
  538.4 129.0 %while.11 = (s32[]{:T(128)}, f32[16,8,512]{2,1,0:T(8,128)}, bf16[16,8,300,128]{3,2,1,0:T(8,128)(2,1)}, bf16[300,639]{1,0:T(8,128)(2,1)S(1)}, s32[]{:T(128)}) while((s32[]{:T(128)}, f32[16,8,512]{2,1,0:T(8,128)}, bf16[16,8,300,128]{3,2,1,0:T(8,128)(2,1)}, bf16[300,639]{1,0:T(8,128)(2,1)S(1)}, s32[]{:T(128)}) %tuple.37), condition=%wide.region_4.5_spmd, body=%wide.region_2.4_spmd.sunk | while | flops 393121792 | bytes 29277720 | solution.py:61
  538.4 2.0 fusion.44
  540.4 2.9 reshape.319
  546.5 2.0 fusion.44
  548.5 2.9 reshape.319
  556.6 2.9 reshape.319
  564.6 2.9 reshape.319
  572.7 2.9 reshape.319
  580.8 2.9 reshape.319
  586.8 2.0 fusion.44
  588.8 2.9 reshape.319
  596.9 2.9 reshape.319
  602.9 2.0 fusion.44
  604.9 2.9 reshape.319
  611.0 2.0 fusion.44
  613.0 2.9 reshape.319
  621.1 2.9 reshape.319
  629.1 2.9 reshape.319
  635.2 2.0 fusion.44
  637.2 2.9 reshape.319
  645.3 2.9 reshape.319
  653.3 2.9 reshape.319
  659.3 2.0 fusion.44
  661.4 2.9 reshape.319
  667.4 6.8 multiply_reduce_fusion
  674.2 91.1 %all-reduce.9 = f32[128]{0:T(128)S(1)} all-reduce(f32[128]{0:T(128)S(1)} %multiply_reduce_fusion), channel_id=3, replica_groups=mesh['section'=2,'blk'=128,'sta'=2] {'section','sta'}, use_global_device_ids=true, to_apply=%region_7.8.clone | all-reduce | flops 128 | bytes 1024
  765.4 19.6 %reduce-scatter.2.cloned.1.call-done = f32[32,512]{1,0:T(8,128)} async-done(((f32[128,512]{1,0:T(8,128)}), f32[32,512]{1,0:T(8,128)}) %reduce-scatter.2.cloned.1.call-update) | async-done | bytes 65552 | tf_op jit(solution)/shard_map/reduce_scatter | solution.py:102
  (157 shorter events, 84.4 us)
Async XLA Ops:
  6.5 531.9 %all-gather.2.cloned.1.call-start = ((), (), s32[]{:S(2)}) async-start(), calls=%async_computation.1 | async-start | bytes 10039296 | tf_op jit(solution)/shard_map/all_gather | solution.py:98
  9.6 775.4 %reduce-scatter.2.cloned.1.call-start = ((), (), s32[]{:S(2)}) async-start(), calls=%async_computation.2 | async-start | bytes 327680 | tf_op jit(solution)/shard_map/reduce_scatter | solution.py:102
  10.5 9.4 %collective-permute-start = (bf16[300,55]{1,0:T(8,128)(2,1)S(1)}, bf16[300,55]{1,0:T(8,128)(2,1)S(1)}, u32[]{:S(2)}, u32[]{:S(2)}) collective-permute-start(bf16[300,55]{1,0:T(8,128)(2,1)S(1)} %slice.50), channel_id=1, source_target_pairs={{2,0},{4,2},{6,4},{8,6},{10,8},{12,10},{14,12},{16,14},{18,16},{20... | collective-permute-start | bytes 99008 | tf_op jit(solution)/shard_map/ppermute | solution.py:17
  12.8 4.4 copy-start.2
  15.8 4.2 copy-start.1
  292.4 6.7 collective-permute-start.1
  543.3 2.5 copy-start
  551.4 1.7 slice-start
  551.4 2.5 copy-start
  559.5 1.7 slice-start
  559.5 2.5 copy-start
  567.5 2.5 copy-start
  575.6 1.7 slice-start
  575.6 2.5 copy-start
  583.7 1.7 slice-start
  583.7 2.5 copy-start
  591.7 2.5 copy-start
  599.8 2.5 copy-start
  607.8 1.7 slice-start
  607.8 2.5 copy-start
  615.9 1.7 slice-start
  615.9 2.5 copy-start
  624.0 2.5 copy-start
  632.0 1.7 slice-start
  632.0 2.5 copy-start
  640.1 1.7 slice-start
  640.1 2.5 copy-start
  648.2 1.7 slice-start
  648.2 2.5 copy-start
  656.2 1.7 slice-start
  656.2 2.5 copy-start
  664.3 2.5 copy-start
  (6 other events, 10.4 us)
Sparse Core Ops, SparseCore 0:
  9.7 528.6 all-gather.1
  667.6 117.4 reduce-scatter.1
where the time goes:
time: 795 us; the launch traced here: 793 us
  blocking collectives  360 us (45%)
  waiting for transfers between devices  261 us (33%)
  local copies, waits for them, and re-layouts  94.3 us (12%)
  matrix products  34.7 us (4%)
  other arithmetic  25.1 us (3%)
  between operations  15 us (2%)
    psum x1, blocking collectives, local(): powers = lax.psum(jnp.sum(decimated * decimated, axis=1), 'blk')  269 us
    all_gather x1, waiting for transfers between devices, local(): arrived = lax.all_gather(panels, 'blk', axis=0, tiled=True)  237 us
    unnamed x1, blocking collectives  91.1 us
    reshape x16, local copies, waits for them, and re-layouts, skew_sum(): flat_vals = product.reshape(groups, taps_len * span_len)  46.3 us
    dot_general x16, matrix products, one_group(): jnp.einsum('gck,cw->gkw', members, shifted, preferred_element_type=jnp.fl...  32.5 us
    slice x32, local copies, waits for them, and re-layouts, skew_sum(): flat_vals[:, :cut_at].reshape(groups, taps_len - 1, span_len + 1)  27.7 us
    reduce_scatter x1, waiting for transfers between devices, local(): lax.psum_scatter(piece_sums, ('section', 'sta'), scatter_dimension=0, til...  19.6 us
  transfers between devices with their start and end apart: 4, of which 3 were waited for; matrix products, arithmetic and copies ran while one was open for 3% of the time, Pallas kernels for 0%

commit v1 on v0

v1 whole, which is shorter than its diff:
```python
import functools

import jax
import jax.numpy as jnp
import numpy as np
from jax import lax
from jax.experimental import pallas as pl
from jax.experimental.pallas import tpu as pltpu
from jax.sharding import Mesh, PartitionSpec as P

TLEN = 128
NTAP = 60
DECIM = 5
SHIFT_MAX = 64
LANES = 128
SUB = 16
ROWS = TLEN // SUB
PAIR = 2
WIDE = 640
GROUPS = 8
GROUP = 40
BLK = ("y", "xl", "zq", "zp")


def vmem():
    return pl.BlockSpec(memory_space=pltpu.VMEM)


def params(mib):
    return pltpu.CompilerParams(vmem_limit_bytes=mib << 20)


def from_next_block(value):
    count = 128
    return lax.ppermute(value, BLK, [(i + 1, i) for i in range(count - 1)])


def tap_matrix(fir_taps):
    depth = DECIM * LANES + LANES
    pattern = jnp.concatenate([fir_taps, jnp.zeros((depth + DECIM - NTAP,), fir_taps.dtype)])
    flat = jnp.tile(pattern, LANES)[: LANES * depth]
    return flat.reshape(LANES, depth)


def decimate_kernel(raw_ref, rim_ref, weights_ref, out_ref):
    step = DECIM * LANES
    blocks = out_ref.shape[1] // LANES
    dims = (((1,), (1,)), ((), ()))
    for i in range(blocks):
        if i < blocks - 1:
            part = lax.dot_general(
                raw_ref[:, i * step : i * step + step + LANES], weights_ref[...], dims,
                preferred_element_type=jnp.float32,
            )
        else:
            part = lax.dot_general(
                raw_ref[:, i * step :], weights_ref[:, :step], dims,
                preferred_element_type=jnp.float32,
            ) + lax.dot_general(
                rim_ref[...], weights_ref[:, step:], dims,
                preferred_element_type=jnp.float32,
            )
        out_ref[:, i * LANES : (i + 1) * LANES] = part


def shift_kernel(dec_ref, rim_ref, root_ref, shift_ref, out_ref):
    channels = dec_ref.shape[0]
    rows = jnp.concatenate([dec_ref[...], rim_ref[...]], axis=1)
    rows = (rows / root_ref[...]).astype(jnp.bfloat16).astype(jnp.float32)
    shift = shift_ref[...]
    width = rows.shape[1]
    for bit in range(SHIFT_MAX.bit_length()):
        step = 1 << bit
        moved = pltpu.roll(rows, width - step, 1)
        rows = jnp.where((shift & step) != 0, moved, rows)
    rows = rows[:, :WIDE]
    tail = jnp.zeros((out_ref.shape[0] - channels, WIDE), jnp.float32)
    out_ref[...] = jnp.concatenate([rows, tail], axis=0).astype(jnp.bfloat16)


def corr_kernel(panel_ref, first_ref, second_ref, trace_ref, out_ref, mixed, panels, shifted):
    chunks = panel_ref.shape[0] // LANES
    lags = out_ref.shape[-1]
    depth = PAIR * SUB * GROUP
    count = ROWS // PAIR

    @pl.when(pl.program_id(0) == 0)
    def _():
        for i in range(chunks):
            part = jnp.dot(
                first_ref[...], panel_ref[i * LANES : (i + 1) * LANES, :],
                preferred_element_type=jnp.float32,
            ).astype(jnp.bfloat16)
            for r in range(ROWS):
                mixed[r, i * SUB : (i + 1) * SUB, :] = part[r * SUB : (r + 1) * SUB, :]
        for r in range(ROWS):
            part = jnp.dot(
                second_ref[...], mixed[r], preferred_element_type=jnp.float32
            ).astype(jnp.bfloat16)
            a, h = divmod(r, PAIR)
            panels[a * LANES : (a + 1) * LANES, h * WIDE : (h + 1) * WIDE] = part

    pieces = trace_ref.shape[0]
    for t in range(pieces):
        trace = trace_ref[t].astype(jnp.float32)
        for j in range(PAIR * SUB // 2):
            low = trace if j == 0 else pltpu.roll(trace, WIDE - 2 * j, 1)
            high = pltpu.roll(trace, WIDE - 2 * j - 1, 1)
            both = jnp.concatenate([low, high], axis=0).astype(jnp.bfloat16)
            shifted[j * 2 * GROUP : (j + 1) * 2 * GROUP, t * WIDE : (t + 1) * WIDE] = both
    sums = jnp.dot(panels[...], shifted[...], preferred_element_type=jnp.float32)
    for t in range(pieces):
        total = sums[:LANES, t * WIDE : t * WIDE + lags]
        for a in range(1, count):
            part = sums[a * LANES : (a + 1) * LANES, t * WIDE : (t + 1) * WIDE]
            total = total + pltpu.roll(part, WIDE - a * PAIR * SUB, 1)[:, :lags]
        for c in range(2):
            for x in range(2):
                g = c * 2 + x
                out_ref[c, x, t] = total[g * 32 : (g + 1) * 32, :]


def orders():
    first = np.zeros((LANES, LANES), np.float32)
    for src in range(SUB):
        for r in range(ROWS):
            first[r * SUB + src, src * ROWS + r] = 1
    second = np.zeros((LANES, LANES), np.float32)
    for zq in range(8):
        for y in range(4):
            for xl in range(2):
                for zp in range(2):
                    source = ((zq * 4 + y) * 2 + xl) * 2 + zp
                    x, c = divmod(y, 2)
                    target = (((c * 2 + x) * 2 + xl) * 8 + zq) * 2 + zp
                    second[target, source] = 1
    return jnp.asarray(first, jnp.bfloat16), jnp.asarray(second, jnp.bfloat16)


def correlate(gathered, traces, lags):
    first, second = orders()
    pieces = 2
    depth = PAIR * SUB * GROUP
    whole = lambda shape: pl.BlockSpec(shape, lambda i: (0,) * len(shape))
    flops = 2 * ROWS // PAIR * LANES * depth * WIDE * GROUPS
    return pl.pallas_call(
        corr_kernel,
        grid=(GROUPS // pieces,),
        in_specs=[
            whole(gathered.shape),
            whole(first.shape),
            whole(second.shape),
            pl.BlockSpec((pieces, GROUP, WIDE), lambda i: (i, 0, 0)),
        ],
        out_specs=pl.BlockSpec((2, 2, pieces, 32, lags), lambda i: (0, 0, i, 0, 0)),
        out_shape=jax.ShapeDtypeStruct((2, 2, GROUPS, 32, lags), jnp.float32),
        scratch_shapes=[
            pltpu.VMEM((ROWS, LANES, WIDE), jnp.bfloat16),
            pltpu.VMEM((ROWS // PAIR * LANES, depth), jnp.bfloat16),
            pltpu.VMEM((depth, pieces * WIDE), jnp.bfloat16),
        ],
        compiler_params=params(48),
        cost_estimate=pl.CostEstimate(flops=flops, bytes_accessed=4 << 20, transcendentals=0),
    )(gathered, first, second, traces)


def local(raw_traces, fir_taps, templates, start_offsets, channel_mask, station_shifts):
    channels, raw_len = raw_traces.shape
    lags = raw_len // DECIM
    blocks = lax.axis_size(BLK)
    raw_rim = from_next_block(raw_traces[:, :LANES])

    window = lax.dynamic_slice_in_dim(templates[0], start_offsets[0], TLEN, axis=1)
    panel = window * channel_mask[0].astype(jnp.bfloat16)[:, None]
    own_norm = jnp.sum(jnp.square(panel.astype(jnp.float32)))
    padded = jnp.pad(panel, ((0, GROUPS * GROUP - channels), (0, 0)))
    message = padded.reshape(GROUPS, GROUP, ROWS, SUB).transpose(0, 2, 3, 1)
    message = message.reshape(GROUPS, 1, ROWS, SUB * GROUP)
    message = jnp.broadcast_to(message, (GROUPS, 2, ROWS, SUB * GROUP))
    message = message.reshape(2 * GROUPS, ROWS, SUB * GROUP)
    exchanged = lax.all_to_all(message, ("y", "xl", "zp"), 0, 0, tiled=True)
    gathered = lax.all_gather(exchanged, "zq", axis=0, tiled=True)
    gathered = gathered.reshape(blocks * ROWS, SUB * GROUP)

    decimated = pl.pallas_call(
        decimate_kernel,
        in_specs=[vmem()] * 3,
        out_specs=vmem(),
        out_shape=jax.ShapeDtypeStruct((channels, lags), jnp.float32),
        compiler_params=params(32),
    )(raw_traces, raw_rim, tap_matrix(fir_taps))
    rim = from_next_block(decimated[:, : 2 * LANES])
    own_power = jnp.sum(decimated * decimated, axis=1)
    own_facts = jnp.concatenate([own_power, own_norm[None], jnp.zeros((3,), jnp.float32)])
    facts = lax.all_to_all(
        jnp.broadcast_to(own_facts[None], (blocks, own_facts.shape[0])), BLK, 0, 0, tiled=True
    )
    powers = jnp.sum(facts[:, :channels], axis=0)
    root_power = jnp.sqrt(powers / (lags * blocks) + 1e-06)
    part_norms = facts[:, channels].reshape(4, 32)
    norms = jnp.sum(lax.all_to_all(part_norms, ("xh", "core"), 0, 0, tiled=True), axis=0)

    traces = pl.pallas_call(
        shift_kernel,
        in_specs=[vmem()] * 4,
        out_specs=vmem(),
        out_shape=jax.ShapeDtypeStruct((GROUPS * GROUP, WIDE), jnp.bfloat16),
        compiler_params=params(32),
    )(decimated, rim, root_power[:, None], jnp.repeat(station_shifts, 3)[:, None])
    traces = lax.all_to_all(
        traces.reshape(GROUPS, GROUP, WIDE), ("y", "xl"), 0, 0, tiled=True
    )

    sums = correlate(gathered, traces, lags)
    sums = jnp.sum(lax.all_to_all(sums, "core", 0, 0, tiled=True), axis=0)
    sums = sums.reshape(2 * GROUPS, 32, lags)
    sums = jnp.sum(lax.all_to_all(sums, ("xh", "y", "xl"), 0, 0, tiled=True), axis=0)
    return sums / jnp.sqrt(norms + 1e-05)[:, None]


def solution(mesh):
    fine = Mesh(
        mesh.devices.reshape(2, 4, 2, 8, 2, 2), ("xh", "y", "xl", "zq", "zp", "core")
    )
    parts = ("xh", "core")
    return jax.shard_map(
        local,
        mesh=fine,
        in_specs=(P(parts, BLK), P(), P(BLK, parts, None), P(BLK), P(BLK, parts), P(parts)),
        out_specs=P(parts, BLK),
        check_vma=False,
    )
```

time: 795 us -> 153 us (0.19)
  the two profiles are of different devices: /device:TPU:1 before, /device:TPU:224 now
where the time goes in v1:
time: 153 us; the launch traced here: 152 us
  waiting for transfers between devices  63.2 us (41%)
  starting transfers between devices  32.8 us (21%)
  blocking collectives  18.3 us (12%)
  between operations  14.4 us (9%)
  Pallas kernels  13.7 us (9%)
  other arithmetic  5.47 us (4%)
  local copies, waits for them, and re-layouts  4.55 us (3%)
    ppermute x2, waiting for transfers between devices, from_next_block(): return lax.ppermute(value, BLK, [(i + 1, i) for i in range(count - 1)])  19.4 us
    all_to_all x1, waiting for transfers between devices, local(): lax.all_to_all(sums, ('xh', 'y', 'xl'), 0, 0, tiled=True)  17.5 us
    all_to_all x1, waiting for transfers between devices, local(): lax.all_to_all(jnp.broadcast_to(own_facts[None], (blocks, own_facts.shape...  15 us
    all_to_all x1, starting transfers between devices, local(): lax.all_to_all(jnp.broadcast_to(own_facts[None], (blocks, own_facts.shape...  13.7 us
    all_to_all x1, blocking collectives, local(): exchanged = lax.all_to_all(message, ('y', 'xl', 'zp'), 0, 0, tiled=True)  12.9 us
    pallas_call x1, Pallas kernels, correlate(): pl.pallas_call(corr_kernel, grid=(GROUPS // pieces,), in_specs=[whole(gat...  10.4 us
    all_to_all x1, waiting for transfers between devices, local(): lax.all_to_all(traces.reshape(GROUPS, GROUP, WIDE), ('y', 'xl'), 0, 0, ti...  7.39 us
    all_to_all x1, starting transfers between devices, local(): lax.all_to_all(traces.reshape(GROUPS, GROUP, WIDE), ('y', 'xl'), 0, 0, ti...  5.84 us
  transfers between devices with their start and end apart: 7, of which 6 were waited for; matrix products, arithmetic and copies ran while one was open for 3% of the time, Pallas kernels for 2%

profile of v1, /device:TPU:224, one launch (start us, length us, event | category | flops | bytes accessed | tf_op | source)
XLA Modules:
  0.0 152.5 jit_solution(11644115677259041507)
XLA Ops:
  7.3 0.7 convert_reduce_fusion
  8.0 1.7 %multiply_reduce_fusion.1 = (f32[]{:T(128)}, bf16[300,128]{1,0:T(8,128)(2,1)S(1)}) fusion(bf16[300]{0:T(512)(128)(2,1)S(1)} %convert_reduce_fusion, bf16[1,300,256]{2,1,0:T(8,128)(2,1)} %param.10, s32[]{:T(128)S(6)} %select_n.3), kind=kLoop, calls=%fused_computation.2 | loop fusion | flops 268799 | bytes 154208 | tf_op jit(solution)/shard_map/reduce_sum | solution.py:175
  9.8 0.2 reshape.59
  10.1 0.3 broadcast_in_dim.10
  10.4 12.9 %all_to_all.38 = bf16[16,8,640]{2,1,0:T(8,128)(2,1)} all-to-all(bf16[16,8,640]{2,1,0:T(8,128)(2,1)S(1)} %bitcast.21), channel_id=1, replica_groups=mesh['xh'=2,'y'=4,'xl'=2,'zq'=8,'zp'=2,'core'=2] {'y','xl','zp'}, dimensions={0} | all-to-all | bytes 327680 | tf_op jit(solution)/shard_map/all_to_all | solution.py:181
  23.4 3.2 %collective-permute-start = (bf16[300,128]{1,0:T(8,128)(2,1)S(1)}, bf16[300,128]{1,0:T(8,128)(2,1)S(1)}, u32[]{:S(2)}, u32[]{:S(2)}) collective-permute-start(bf16[300,128]{1,0:T(8,128)(2,1)S(1)} %slice.15), channel_id=1, source_target_pairs={{2,0},{4,2},{6,4},{8,6},{10,8},{12,10},{14,12},{16,14},{18,16},{20... | collective-permute-start | bytes 230408 | tf_op jit(solution)/shard_map/ppermute | solution.py:35
  26.6 0.4 tile.10
  27.0 0.2 reshape.62.weights_ref
  27.2 3.8 %collective-permute-done.rim_ref = bf16[300,128]{1,0:T(8,128)(2,1)S(1)} collective-permute-done((bf16[300,128]{1,0:T(8,128)(2,1)S(1)}, bf16[300,128]{1,0:T(8,128)(2,1)S(1)}, u32[]{:S(2)}, u32[]{:S(2)}) %collective-permute-start) | collective-permute-done | bytes 76832 | tf_op jit(solution)/shard_map/ppermute | solution.py:35
  31.0 0.7 shard_map.82.dec_ref
  31.7 0.2 multiply_reduce_fusion
  31.9 0.7 pad_maximum_fusion
  32.6 0.8 broadcast_in_dim.26
  33.4 13.7 %all-to-all-start.1 = ((f32[128,1,304]{2,1,0:T(1,128)}), f32[128,1,304]{2,1,0:T(1,128)S(1)}, u32[]{:S(2)}, u32[]{:S(2)}) async-start(f32[128,1,304]{2,1,0:T(1,128)} %broadcast_in_dim.26), calls=%async_computation.1 | async-start | bytes 393216 | tf_op jit(solution)/shard_map/all_to_all | solution.py:195
  47.4 2.5 %collective-permute-start.1 = (f32[300,256]{1,0:T(8,128)S(1)}, f32[300,256]{1,0:T(8,128)S(1)}, u32[]{:S(2)}, u32[]{:S(2)}) collective-permute-start(f32[300,256]{1,0:T(8,128)S(1)} %slice.21), channel_id=1, source_target_pairs={{2,0},{4,2},{6,4},{8,6},{10,8},{12,10},{14,12},{16,14},{18,16},{20... | collective-permute-start | bytes 921608 | tf_op jit(solution)/shard_map/ppermute | solution.py:35
  49.9 15.0 %all-to-all-done.1 = f32[128,1,304]{2,1,0:T(1,128)S(1)} async-done(((f32[128,1,304]{2,1,0:T(1,128)}), f32[128,1,304]{2,1,0:T(1,128)S(1)}, u32[]{:S(2)}, u32[]{:S(2)}) %all-to-all-start.1) | async-done | bytes 155680 | tf_op jit(solution)/shard_map/all_to_all | solution.py:195
  64.9 0.1 copy.29
  65.0 0.1 slice_reduce_fusion
  65.3 15.6 %collective-permute-done.1.rim_ref = f32[300,256]{1,0:T(8,128)S(1)} collective-permute-done((f32[300,256]{1,0:T(8,128)S(1)}, f32[300,256]{1,0:T(8,128)S(1)}, u32[]{:S(2)}, u32[]{:S(2)}) %collective-permute-start.1) | collective-permute-done | bytes 307232 | tf_op jit(solution)/shard_map/ppermute | solution.py:35
  80.9 2.6 %shard_map.83 = bf16[320,640]{1,0:T(8,128)(2,1)} custom-call(f32[300,512]{1,0:T(8,128)S(1)} %shard_map.82.dec_ref, f32[300,256]{1,0:T(8,128)S(1)} %collective-permute-done.1.rim_ref, f32[300,1]{1,0:T(8,128)S(1)} %sqrt.23.root_ref, s32[300,1]{1,0:T(8,128)S(1)} %broadcast_in_dim_reshape.4.shift_ref), custom_call_target="tpu_custom_call" | custom-call | tf_op jit(solution)/shard_map/pallas_call | solution.py:203
  83.5 5.8 %all-to-all-start.2 = ((bf16[8,40,640]{2,1,0:T(8,128)(2,1)}), bf16[8,40,640]{2,1,0:T(8,128)(2,1)S(1)}, u32[]{:S(2)}, u32[]{:S(2)}) async-start(bf16[8,40,640]{2,1,0:T(8,128)(2,1)} %bitcast.7), calls=%async_computation.2 | async-start | bytes 819200 | tf_op jit(solution)/shard_map/all_to_all | solution.py:210
  89.3 0.7 all_to_all.30
  90.0 7.4 %all-to-all-done.2.trace_ref = bf16[8,40,640]{2,1,0:T(8,128)(2,1)S(1)} async-done(((bf16[8,40,640]{2,1,0:T(8,128)(2,1)}), bf16[8,40,640]{2,1,0:T(8,128)(2,1)S(1)}, u32[]{:S(2)}, u32[]{:S(2)}) %all-to-all-start.2) | async-done | bytes 409632 | tf_op jit(solution)/shard_map/all_to_all | solution.py:210
  97.4 1.3 copy-done.1
  98.7 10.4 %shard_map.84 = f32[2,2,8,32,512]{4,3,2,1,0:T(8,128)S(1)} custom-call(bf16[1024,640]{1,0:T(8,128)(2,1)S(1)} %bitcast.19, bf16[128,128]{1,0:T(8,128)(2,1)S(1)} %copy-done.3, bf16[128,128]{1,0:T(8,128)(2,1)S(1)} %copy-done.2, bf16[8,40,640]{2,1,0:T(8,128)(2,1)S(1)} %all-to-all-done.2.trace_ref), custom_call_target="tpu_custom_call" | custom-call | flops 6710886400 | bytes 4194304 | tf_op jit(solution)/shard_map/pallas_call | solution.py:146
  109.1 5.4 %all_to_all.39 = f32[2,2,8,32,512]{4,3,2,1,0:T(8,128)S(1)} all-to-all(f32[2,2,8,32,512]{4,3,2,1,0:T(8,128)S(1)} %shard_map.84), channel_id=1, replica_groups=mesh['xh'=2,'y'=4,'xl'=2,'zq'=8,'zp'=2,'core'=2] {'core'}, dimensions={0} | all-to-all | bytes 4194304 | tf_op jit(solution)/shard_map/all_to_all | solution.py:215
  114.6 3.9 %all-to-all-start.5 = ((f32[4,1,32]{2,1,0:T(1,128)}), f32[4,1,32]{2,1,0:T(1,128)S(1)}, u32[]{:S(2)}, u32[]{:S(2)}) async-start(f32[4,1,32]{2,1,0:T(1,128)} %bitcast.9), calls=%async_computation.5 | async-start | bytes 4096 | tf_op jit(solution)/shard_map/all_to_all | solution.py:201
  118.5 1.3 reduce_sum.57
  119.8 3.9 %all-to-all-done.5 = f32[4,1,32]{2,1,0:T(1,128)S(1)} async-done(((f32[4,1,32]{2,1,0:T(1,128)}), f32[4,1,32]{2,1,0:T(1,128)S(1)}, u32[]{:S(2)}, u32[]{:S(2)}) %all-to-all-start.5) | async-done | bytes 544 | tf_op jit(solution)/shard_map/all_to_all | solution.py:201
  123.7 3.7 %all-to-all-start.4 = ((f32[16,32,512]{2,1,0:T(8,128)}), f32[16,32,512]{2,1,0:T(8,128)S(1)}, u32[]{:S(2)}, u32[]{:S(2)}) async-start(f32[16,32,512]{2,1,0:T(8,128)} %bitcast.8), calls=%async_computation.4 | async-start | bytes 2097152 | tf_op jit(solution)/shard_map/all_to_all | solution.py:217
  127.4 17.5 %all-to-all-done.4 = f32[16,32,512]{2,1,0:T(8,128)S(1)} async-done(((f32[16,32,512]{2,1,0:T(8,128)}), f32[16,32,512]{2,1,0:T(8,128)S(1)}, u32[]{:S(2)}, u32[]{:S(2)}) %all-to-all-start.4) | async-done | bytes 1048608 | tf_op jit(solution)/shard_map/all_to_all | solution.py:217
  144.9 0.7 broadcast_divide_fusion
  (32 shorter events, 0.7 us)
Async XLA Ops:
  6.5 16.8 %copy-start = (bf16[300,2560]{1,0:T(8,128)(2,1)S(1)}, bf16[300,2560]{1,0:T(8,128)(2,1)}, u32[]{:S(2)}) copy-start(bf16[300,2560]{1,0:T(8,128)(2,1)} %raw_ref.1) | copy-start | bytes 4608004
  6.5 20.0 %copy-start.5 = (bf16[60]{0:T(256)(128)(2,1)S(1)}, bf16[60]{0:T(256)(128)(2,1)}, u32[]{:S(2)}) copy-start(bf16[60]{0:T(256)(128)(2,1)} %param.9) | copy-start | bytes 364
  6.5 90.9 %all-gather.2.cloned.1.call-start = ((), (), s32[]{:S(2)}) async-start(), calls=%async_computation.6 | async-start | bytes 1474560 | tf_op jit(solution)/shard_map/all_gather | solution.py:182
  23.4 7.6 %collective-permute-start = (bf16[300,128]{1,0:T(8,128)(2,1)S(1)}, bf16[300,128]{1,0:T(8,128)(2,1)S(1)}, u32[]{:S(2)}, u32[]{:S(2)}) collective-permute-start(bf16[300,128]{1,0:T(8,128)(2,1)S(1)} %slice.15), channel_id=1, source_target_pairs={{2,0},{4,2},{6,4},{8,6},{10,8},{12,10},{14,12},{16,14},{18,16},{20... | collective-permute-start | bytes 230408 | tf_op jit(solution)/shard_map/ppermute | solution.py:35
  27.0 20.1 %copy-start.4 = (s32[100]{0:T(128)S(1)}, s32[100]{0:T(128)}, u32[]{:S(2)}) copy-start(s32[100]{0:T(128)} %param.13) | copy-start | bytes 1204
  33.4 31.5 %all-to-all-start.1 = ((f32[128,1,304]{2,1,0:T(1,128)}), f32[128,1,304]{2,1,0:T(1,128)S(1)}, u32[]{:S(2)}, u32[]{:S(2)}) async-start(f32[128,1,304]{2,1,0:T(1,128)} %broadcast_in_dim.26), calls=%async_computation.1 | async-start | bytes 393216 | tf_op jit(solution)/shard_map/all_to_all | solution.py:195
  47.1 50.3 %copy-start.2 = (bf16[128,128]{1,0:T(8,128)(2,1)S(1)}, bf16[128,128]{1,0:T(8,128)(2,1)}, u32[]{:S(2)}) copy-start(bf16[128,128]{1,0:T(8,128)(2,1)} %constant.23.clone.second_ref) | copy-start | bytes 98308
  47.1 50.3 %copy-start.3 = (bf16[128,128]{1,0:T(8,128)(2,1)S(1)}, bf16[128,128]{1,0:T(8,128)(2,1)}, u32[]{:S(2)}) copy-start(bf16[128,128]{1,0:T(8,128)(2,1)} %constant.22.clone.first_ref) | copy-start | bytes 98308
  47.4 33.5 %collective-permute-start.1 = (f32[300,256]{1,0:T(8,128)S(1)}, f32[300,256]{1,0:T(8,128)S(1)}, u32[]{:S(2)}, u32[]{:S(2)}) collective-permute-start(f32[300,256]{1,0:T(8,128)S(1)} %slice.21), channel_id=1, source_target_pairs={{2,0},{4,2},{6,4},{8,6},{10,8},{12,10},{14,12},{16,14},{18,16},{20... | collective-permute-start | bytes 921608 | tf_op jit(solution)/shard_map/ppermute | solution.py:35
  83.5 13.9 %all-to-all-start.2 = ((bf16[8,40,640]{2,1,0:T(8,128)(2,1)}), bf16[8,40,640]{2,1,0:T(8,128)(2,1)S(1)}, u32[]{:S(2)}, u32[]{:S(2)}) async-start(bf16[8,40,640]{2,1,0:T(8,128)(2,1)} %bitcast.7), calls=%async_computation.2 | async-start | bytes 819200 | tf_op jit(solution)/shard_map/all_to_all | solution.py:210
  97.4 1.3 copy-start.1
  114.6 9.1 %all-to-all-start.5 = ((f32[4,1,32]{2,1,0:T(1,128)}), f32[4,1,32]{2,1,0:T(1,128)S(1)}, u32[]{:S(2)}, u32[]{:S(2)}) async-start(f32[4,1,32]{2,1,0:T(1,128)} %bitcast.9), calls=%async_computation.5 | async-start | bytes 4096 | tf_op jit(solution)/shard_map/all_to_all | solution.py:201
  123.7 21.2 %all-to-all-start.4 = ((f32[16,32,512]{2,1,0:T(8,128)}), f32[16,32,512]{2,1,0:T(8,128)S(1)}, u32[]{:S(2)}, u32[]{:S(2)}) async-start(f32[16,32,512]{2,1,0:T(8,128)} %bitcast.8), calls=%async_computation.4 | async-start | bytes 2097152 | tf_op jit(solution)/shard_map/all_to_all | solution.py:217
Sparse Core Ops, SparseCore 0:
  23.5 59.4 all-gather.1

commit v2 on v1

v2 whole, which is shorter than its diff:
```python
import jax
import jax.numpy as jnp
import numpy as np
from jax import lax
from jax.experimental import pallas as pl
from jax.experimental.pallas import tpu as pltpu
from jax.sharding import Mesh, PartitionSpec as P

TLEN = 128
NTAP = 60
DECIM = 5
SHIFT_MAX = 64
LANES = 128
SUB = 16
ROWS = TLEN // SUB
PAIR = 2
WIDE = 640
GROUPS = 8
GROUP = 40
USED = 38
RIM = 1024
PIECES = 2
BLK = ("y", "xl", "zq", "zp")


def vmem():
    return pl.BlockSpec(memory_space=pltpu.VMEM)


def params(mib):
    return pltpu.CompilerParams(vmem_limit_bytes=mib << 20)


def from_next_block(value):
    count = 128
    return lax.ppermute(value, BLK, [(i + 1, i) for i in range(count - 1)])


def tap_matrix(fir_taps):
    depth = DECIM * LANES + LANES
    pattern = jnp.concatenate([fir_taps, jnp.zeros((depth + DECIM - NTAP,), fir_taps.dtype)])
    flat = jnp.tile(pattern, LANES)[: LANES * depth]
    return flat.reshape(LANES, depth)


def trace_kernel(norm_ref, raw_ref, rim_ref, weights_ref, shift_ref, out_ref):
    channels = raw_ref.shape[0]
    step = DECIM * LANES
    own = raw_ref.shape[1] // step
    dims = (((1,), (1,)), ((), ()))

    def product(left, right):
        return lax.dot_general(left, right, dims, preferred_element_type=jnp.float32)

    blocks = []
    for i in range(own - 1):
        blocks.append(product(raw_ref[:, i * step : i * step + step + LANES], weights_ref[...]))
    blocks.append(
        product(raw_ref[:, (own - 1) * step :], weights_ref[:, :step])
        + product(rim_ref[:, :LANES], weights_ref[:, step:])
    )
    blocks.append(product(rim_ref[:, : step + LANES], weights_ref[...]))
    blocks.append(product(rim_ref[:, step:], weights_ref[:, : RIM - step]))
    squares = blocks[0] * blocks[0]
    for block in blocks[1:own]:
        squares = squares + block * block
    power = jnp.sum(squares, axis=1, keepdims=True)

    rows = jnp.concatenate(blocks, axis=1)
    shift = shift_ref[...]
    width = rows.shape[1]
    for bit in range(SHIFT_MAX.bit_length()):
        hop = 1 << bit
        moved = pltpu.roll(rows, width - hop, 1)
        rows = jnp.where((shift & hop) != 0, moved, rows)
    rows = rows[:, :WIDE]
    lane = lax.broadcasted_iota(jnp.int32, rows.shape, 1)
    rows = jnp.where(lane == WIDE - 1, power, rows)
    spare = GROUP - USED
    side = lax.broadcasted_iota(jnp.int32, (spare, WIDE), 0)
    side = jnp.where(side == 0, norm_ref[0], 0.0)
    for g in range(GROUPS):
        first, last = g * USED, min((g + 1) * USED, channels)
        pieces = [rows[first:last]]
        if last - first < USED:
            pieces.append(jnp.zeros((USED - last + first, WIDE), jnp.float32))
        out_ref[g] = jnp.concatenate(pieces + [side], axis=0)


def spread_kernel(trace_ref, root_ref, out_ref):
    pieces = trace_ref.shape[0]
    for t in range(pieces):
        trace = (trace_ref[t] / root_ref[...]).astype(jnp.bfloat16).astype(jnp.float32)
        for j in range(PAIR * SUB // 2):
            low = trace if j == 0 else pltpu.roll(trace, WIDE - 2 * j, 1)
            high = pltpu.roll(trace, WIDE - 2 * j - 1, 1)
            both = jnp.concatenate([low, high], axis=0).astype(jnp.bfloat16)
            out_ref[0, j * 2 * GROUP : (j + 1) * 2 * GROUP, t * WIDE : (t + 1) * WIDE] = both


def corr_kernel(panel_ref, first_ref, second_ref, shifted_ref, out_ref, mixed, panels):
    chunks = panel_ref.shape[0] // LANES
    lags = out_ref.shape[-1]
    count = ROWS // PAIR

    @pl.when(pl.program_id(0) == 0)
    def _():
        for i in range(chunks):
            part = jnp.dot(
                first_ref[...], panel_ref[i * LANES : (i + 1) * LANES, :],
                preferred_element_type=jnp.float32,
            ).astype(jnp.bfloat16)
            for r in range(ROWS):
                mixed[r, i * SUB : (i + 1) * SUB, :] = part[r * SUB : (r + 1) * SUB, :]
        for r in range(ROWS):
            part = jnp.dot(
                second_ref[...], mixed[r], preferred_element_type=jnp.float32
            ).astype(jnp.bfloat16)
            a, h = divmod(r, PAIR)
            panels[a * LANES : (a + 1) * LANES, h * WIDE : (h + 1) * WIDE] = part

    pieces = out_ref.shape[2]
    sums = jnp.dot(panels[...], shifted_ref[0], preferred_element_type=jnp.float32)
    for t in range(pieces):
        total = sums[:LANES, t * WIDE : t * WIDE + lags]
        for a in range(1, count):
            part = sums[a * LANES : (a + 1) * LANES, t * WIDE : (t + 1) * WIDE]
            total = total + pltpu.roll(part, WIDE - a * PAIR * SUB, 1)[:, :lags]
        for c in range(2):
            for x in range(2):
                g = c * 2 + x
                out_ref[c, x, t] = total[g * 32 : (g + 1) * 32, :]


def orders():
    first = np.zeros((LANES, LANES), np.float32)
    for src in range(SUB):
        for r in range(ROWS):
            first[r * SUB + src, src * ROWS + r] = 1
    second = np.zeros((LANES, LANES), np.float32)
    for zq in range(8):
        for y in range(4):
            for xl in range(2):
                for zp in range(2):
                    source = ((zq * 4 + y) * 2 + xl) * 2 + zp
                    x, c = divmod(y, 2)
                    target = (((c * 2 + x) * 2 + xl) * 8 + zq) * 2 + zp
                    second[target, source] = 1
    return jnp.asarray(first, jnp.bfloat16), jnp.asarray(second, jnp.bfloat16)


def whole(shape):
    return pl.BlockSpec(shape, lambda i: (0,) * len(shape))


def spread(traces, root_power):
    depth = PAIR * SUB * GROUP
    return pl.pallas_call(
        spread_kernel,
        grid=(GROUPS // PIECES,),
        in_specs=[
            pl.BlockSpec((PIECES, GROUP, WIDE), lambda i: (i, 0, 0)),
            whole(root_power.shape),
        ],
        out_specs=pl.BlockSpec((1, depth, PIECES * WIDE), lambda i: (i, 0, 0)),
        out_shape=jax.ShapeDtypeStruct((GROUPS // PIECES, depth, PIECES * WIDE), jnp.bfloat16),
        compiler_params=params(32),
        cost_estimate=pl.CostEstimate(flops=20 << 20, bytes_accessed=14 << 20, transcendentals=0),
    )(traces, root_power)


def correlate(gathered, shifted, lags):
    first, second = orders()
    depth = PAIR * SUB * GROUP
    flops = 2 * ROWS // PAIR * LANES * depth * WIDE * GROUPS
    return pl.pallas_call(
        corr_kernel,
        grid=(GROUPS // PIECES,),
        in_specs=[
            whole(gathered.shape),
            whole(first.shape),
            whole(second.shape),
            pl.BlockSpec((1,) + shifted.shape[1:], lambda i: (i, 0, 0)),
        ],
        out_specs=pl.BlockSpec((2, 2, PIECES, 32, lags), lambda i: (0, 0, i, 0, 0)),
        out_shape=jax.ShapeDtypeStruct((2, 2, GROUPS, 32, lags), jnp.float32),
        scratch_shapes=[
            pltpu.VMEM((ROWS, LANES, WIDE), jnp.bfloat16),
            pltpu.VMEM((ROWS // PAIR * LANES, depth), jnp.bfloat16),
        ],
        compiler_params=params(48),
        cost_estimate=pl.CostEstimate(flops=flops, bytes_accessed=17 << 20, transcendentals=0),
    )(gathered, first, second, shifted)


def local(raw_traces, fir_taps, templates, start_offsets, channel_mask, station_shifts):
    channels, raw_len = raw_traces.shape
    lags = raw_len // DECIM
    blocks = lax.axis_size(BLK)
    raw_rim = from_next_block(raw_traces[:, :RIM])

    window = lax.dynamic_slice_in_dim(templates[0], start_offsets[0], TLEN, axis=1)
    panel = window * channel_mask[0].astype(jnp.bfloat16)[:, None]
    norm = jnp.sum(jnp.square(panel.astype(jnp.float32)))[None]
    padded = jnp.pad(panel, ((0, GROUPS * USED - channels), (0, 0)))
    padded = jnp.pad(padded.reshape(GROUPS, USED, TLEN), ((0, 0), (0, GROUP - USED), (0, 0)))
    message = padded.reshape(GROUPS, GROUP, ROWS, SUB).transpose(0, 2, 3, 1)
    message = message.reshape(GROUPS, 1, ROWS, SUB * GROUP)
    message = jnp.broadcast_to(message, (GROUPS, 2, ROWS, SUB * GROUP))
    message = message.reshape(2 * GROUPS, ROWS, SUB * GROUP)
    exchanged = lax.all_to_all(message, ("y", "xl", "zp"), 0, 0, tiled=True)
    gathered = lax.all_gather(exchanged, "zq", axis=0, tiled=True)
    gathered = gathered.reshape(blocks * ROWS, SUB * GROUP)

    norm = norm + lax.ppermute(norm, "core", [(0, 1), (1, 0)])
    norm = norm + lax.ppermute(norm, "xh", [(0, 1), (1, 0)])

    traces = pl.pallas_call(
        trace_kernel,
        in_specs=[pl.BlockSpec(memory_space=pltpu.SMEM)] + [vmem()] * 4,
        out_specs=vmem(),
        out_shape=jax.ShapeDtypeStruct((GROUPS, GROUP, WIDE), jnp.float32),
        compiler_params=params(32),
        cost_estimate=pl.CostEstimate(flops=400 << 20, bytes_accessed=4 << 20, transcendentals=0),
    )(norm, raw_traces, raw_rim, tap_matrix(fir_taps), jnp.repeat(station_shifts, 3)[:, None])
    traces = lax.all_to_all(traces, ("y", "xl"), 0, 0, tiled=True)

    powers = jnp.sum(traces[:, :, WIDE - 1], axis=0)
    norms = traces[:, USED, 0]
    facts = jnp.concatenate([powers, norms, jnp.zeros((LANES - GROUP - GROUPS,), jnp.float32)])
    along = lax.axis_size(("zq", "zp"))
    facts = jnp.broadcast_to(facts[None], (along, LANES))
    facts = lax.all_to_all(facts, ("zq", "zp"), 0, 0, tiled=True)
    powers = jnp.sum(facts[:, :GROUP], axis=0)
    root_power = jnp.sqrt(powers / (lags * blocks) + 1e-06)
    norms = facts[:, GROUP : GROUP + GROUPS].T.reshape(4, 2 * along)
    norms = lax.dynamic_index_in_dim(norms, lax.axis_index(("xh", "core")), 0, keepdims=False)

    shifted = spread(traces, root_power[:, None])
    sums = correlate(gathered, shifted, lags)
    sums = jnp.sum(lax.all_to_all(sums, "core", 0, 0, tiled=True), axis=0)
    sums = sums.reshape(2 * GROUPS, 32, lags)
    sums = jnp.sum(lax.all_to_all(sums, ("xh", "y", "xl"), 0, 0, tiled=True), axis=0)
    return sums / jnp.sqrt(norms + 1e-05)[:, None]


def solution(mesh):
    fine = Mesh(
        mesh.devices.reshape(2, 4, 2, 8, 2, 2), ("xh", "y", "xl", "zq", "zp", "core")
    )
    parts = ("xh", "core")
    return jax.shard_map(
        local,
        mesh=fine,
        in_specs=(P(parts, BLK), P(), P(BLK, parts, None), P(BLK), P(BLK, parts), P(parts)),
        out_specs=P(parts, BLK),
        check_vma=False,
    )
```

time: 153 us -> 153 us (level)
  the two profiles are of different devices: /device:TPU:224 before, /device:TPU:1 now
where the time goes in v2:
time: 153 us
  blocking collectives  70.9 us (46%)
  waiting for transfers between devices  19 us (12%)
  Pallas kernels  18.6 us (12%)
  between operations  16.4 us (11%)
  starting transfers between devices  14.3 us (9%)
  local copies, waits for them, and re-layouts  8.71 us (6%)
  other arithmetic  4.73 us (3%)
    all_to_all x1, blocking collectives, local(): traces = lax.all_to_all(traces, ('y', 'xl'), 0, 0, tiled=True)  21.6 us
    all_to_all x1, blocking collectives, local(): sums = jnp.sum(lax.all_to_all(sums, 'core', 0, 0, tiled=True), axis=0)  18.4 us
    all_to_all x1, blocking collectives, local(): facts = lax.all_to_all(facts, ('zq', 'zp'), 0, 0, tiled=True)  17.4 us
    all_to_all x1, waiting for transfers between devices, local(): lax.all_to_all(sums, ('xh', 'y', 'xl'), 0, 0, tiled=True)  16.2 us
    all_to_all x1, blocking collectives, local(): exchanged = lax.all_to_all(message, ('y', 'xl', 'zp'), 0, 0, tiled=True)  13.5 us
    pallas_call x1, Pallas kernels, correlate(): pl.pallas_call(corr_kernel, grid=(GROUPS // PIECES,), in_specs=[whole(gat...  11.2 us
    unnamed x15, local copies, waits for them, and re-layouts  6.18 us
    ppermute x1, starting transfers between devices, local(): norm = norm + lax.ppermute(norm, 'core', [(0, 1), (1, 0)])  5.88 us
  transfers between devices with their start and end apart: 5, of which 3 were waited for; matrix products, arithmetic and copies ran while one was open for 2% of the time, Pallas kernels for 5%

profile of v2, /device:TPU:1, one launch (start us, length us, event | category | flops | bytes accessed | tf_op | source)
XLA Modules:
  0.0 152.5 jit_solution(13004100285791954578)
XLA Ops:
  7.3 0.7 convert_reduce_fusion
  8.0 1.7 %multiply_reduce_fusion = (f32[]{:T(128)}, bf16[300,128]{1,0:T(8,128)(2,1)S(1)}) fusion(bf16[300]{0:T(512)(128)(2,1)S(1)} %convert_reduce_fusion, bf16[1,300,256]{2,1,0:T(8,128)(2,1)} %param.10, s32[]{:T(128)S(6)} %select_n.7), kind=kLoop, calls=%fused_computation.1 | loop fusion | flops 268799 | bytes 154208 | tf_op jit(solution)/shard_map/reduce_sum | solution.py:204
  9.7 0.2 copy.21
  10.0 0.3 broadcast_in_dim.12
  10.3 13.5 %all_to_all.29 = bf16[16,8,640]{2,1,0:T(8,128)(2,1)} all-to-all(bf16[16,8,640]{2,1,0:T(8,128)(2,1)S(1)} %bitcast.25), channel_id=1, replica_groups=mesh['xh'=2,'y'=4,'xl'=2,'zq'=8,'zp'=2,'core'=2] {'y','xl','zp'}, dimensions={0} | all-to-all | bytes 327680 | tf_op jit(solution)/shard_map/all_to_all | solution.py:211
  23.8 0.9 slice.18
  24.7 1.3 collective-permute-start.2
  26.0 5.9 %collective-permute-start = (f32[1]{0:T(128)}, f32[1]{0:T(128)}, u32[]{:S(2)}, u32[]{:S(2)}) collective-permute-start(f32[1]{0:T(128)} %bitcast.6), channel_id=1, source_target_pairs={{0,1},{1,0},{2,3},{3,2},{4,5},{5,4},{6,7},{7,6},{8,9},{9,8},{10,11... | collective-permute-start | bytes 20 | tf_op jit(solution)/shard_map/ppermute | solution.py:215
  31.9 0.1 broadcast_in_dim.29
  32.0 0.1 broadcast_in_dim_reshape.4.shift_ref
  32.1 0.4 tile.10
  32.5 0.2 reshape.68.weights_ref
  32.7 0.1 collective-permute-done
  34.1 3.2 %collective-permute-start.1 = (f32[1]{0:T(128)}, f32[1]{0:T(128)}, u32[]{:S(2)}, u32[]{:S(2)}) collective-permute-start(f32[1]{0:T(128)} %add.48), channel_id=1, source_target_pairs={{0,256},{256,0},{1,257},{257,1},{2,258},{258,2},{3,259},{259,3},{4... | collective-permute-start | bytes 20 | tf_op jit(solution)/shard_map/ppermute | solution.py:216
  37.3 2.7 %collective-permute-done.1 = f32[1]{0:T(128)} collective-permute-done((f32[1]{0:T(128)}, f32[1]{0:T(128)}, u32[]{:S(2)}, u32[]{:S(2)}) %collective-permute-start.1) | collective-permute-done | bytes 36 | tf_op jit(solution)/shard_map/ppermute | solution.py:216
  40.7 3.0 %shard_map.82 = f32[8,40,640]{2,1,0:T(8,128)S(1)} custom-call(f32[1]{0:T(128)S(6)} %add.49.norm_ref, bf16[300,2560]{1,0:T(8,128)(2,1)S(1)} %copy-done.1, bf16[300,1024]{1,0:T(8,128)(2,1)S(1)} %collective-permute-done.2.rim_ref, bf16[128,768]{1,0:T(8,128)(2,1)S(1)} %reshape.68.weights_ref, s32[300,1]{1,0:T(8,128)S(1)} %broadcast_in_dim_reshape.4.shift_ref), custom_call_target="tpu_custom_call" | custom-call | flops 419430400 | bytes 4194304 | tf_op jit(solution)/shard_map/pallas_call | solution.py:218
  43.8 21.6 %all_to_all.30.trace_ref = f32[8,40,640]{2,1,0:T(8,128)S(1)} all-to-all(f32[8,40,640]{2,1,0:T(8,128)S(1)} %shard_map.82), channel_id=1, replica_groups=mesh['xh'=2,'y'=4,'xl'=2,'zq'=8,'zp'=2,'core'=2] {'y','xl'}, dimensions={0} | all-to-all | bytes 1638400 | tf_op jit(solution)/shard_map/all_to_all | solution.py:226
  65.4 0.1 slice_reduce_fusion.2
  65.5 0.2 slice_reduce_fusion
  65.7 0.1 pad_maximum_fusion
  65.8 17.4 %all_to_all.31 = f32[16,1,128]{2,1,0:T(1,128)S(1)} all-to-all(f32[16,1,128]{2,1,0:T(1,128)S(1)} %broadcast_in_dim.31), channel_id=1, replica_groups=mesh['xh'=2,'y'=4,'xl'=2,'zq'=8,'zp'=2,'core'=2] {'zq','zp'}, dimensions={0} | all-to-all | bytes 16384 | tf_op jit(solution)/shard_map/all_to_all | solution.py:233
  83.2 0.1 copy.19.root_ref
  83.3 4.3 %shard_map.83.shifted_ref = bf16[4,1280,1280]{2,1,0:T(8,128)(2,1)S(1)} custom-call(f32[8,40,640]{2,1,0:T(8,128)S(1)} %all_to_all.30.trace_ref, f32[40,1]{1,0:T(8,128)S(1)} %copy.19.root_ref), custom_call_target="tpu_custom_call" | custom-call | flops 20971520 | bytes 14680064 | tf_op jit(solution)/shard_map/pallas_call | solution.py:158
  87.7 4.7 %copy-done = bf16[4,1280,1280]{2,1,0:T(8,128)(2,1)} copy-done((bf16[4,1280,1280]{2,1,0:T(8,128)(2,1)}, bf16[4,1280,1280]{2,1,0:T(8,128)(2,1)S(1)}, u32[]{:S(2)}) %copy-start) | copy-done | bytes 13107224
  92.4 1.3 copy-done.2
  93.7 11.2 %shard_map.84 = f32[2,2,8,32,512]{4,3,2,1,0:T(8,128)S(1)} custom-call(bf16[1024,640]{1,0:T(8,128)(2,1)S(1)} %bitcast.23, bf16[128,128]{1,0:T(8,128)(2,1)S(1)} %copy-done.4, bf16[128,128]{1,0:T(8,128)(2,1)S(1)} %copy-done.3, bf16[4,1280,1280]{2,1,0:T(8,128)(2,1)} %copy-done), custom_call_target="tpu_custom_call" | custom-call | flops 6710886400 | bytes 17825792 | tf_op jit(solution)/shard_map/pallas_call | solution.py:176
  104.9 18.4 %all_to_all.32 = f32[2,2,8,32,512]{4,3,2,1,0:T(8,128)S(1)} all-to-all(f32[2,2,8,32,512]{4,3,2,1,0:T(8,128)S(1)} %shard_map.84), channel_id=1, replica_groups=mesh['xh'=2,'y'=4,'xl'=2,'zq'=8,'zp'=2,'core'=2] {'core'}, dimensions={0} | all-to-all | bytes 4194304 | tf_op jit(solution)/shard_map/all_to_all | solution.py:241
  123.3 1.3 reduce_sum.48
  124.6 3.9 %all-to-all-start.4 = ((f32[16,32,512]{2,1,0:T(8,128)}), f32[16,32,512]{2,1,0:T(8,128)S(1)}, u32[]{:S(2)}, u32[]{:S(2)}) async-start(f32[16,32,512]{2,1,0:T(8,128)} %bitcast.9), calls=%async_computation.4 | async-start | bytes 2097152 | tf_op jit(solution)/shard_map/all_to_all | solution.py:243
  128.6 0.1 reshape.70
  128.7 16.2 %all-to-all-done.4 = f32[16,32,512]{2,1,0:T(8,128)S(1)} async-done(((f32[16,32,512]{2,1,0:T(8,128)}), f32[16,32,512]{2,1,0:T(8,128)S(1)}, u32[]{:S(2)}, u32[]{:S(2)}) %all-to-all-start.4) | async-done | bytes 1048608 | tf_op jit(solution)/shard_map/all_to_all | solution.py:243
  144.9 0.7 broadcast_divide_fusion
  (31 shorter events, 0.5 us)
Async XLA Ops:
  6.5 17.2 %copy-start.1 = (bf16[300,2560]{1,0:T(8,128)(2,1)S(1)}, bf16[300,2560]{1,0:T(8,128)(2,1)}, u32[]{:S(2)}) copy-start(bf16[300,2560]{1,0:T(8,128)(2,1)} %raw_ref.1) | copy-start | bytes 4608004
  6.5 25.3 %copy-start.6 = (bf16[60]{0:T(256)(128)(2,1)S(1)}, bf16[60]{0:T(256)(128)(2,1)}, u32[]{:S(2)}) copy-start(bf16[60]{0:T(256)(128)(2,1)} %param.9) | copy-start | bytes 364
  6.5 25.3 %copy-start.5 = (s32[100]{0:T(128)S(1)}, s32[100]{0:T(128)}, u32[]{:S(2)}) copy-start(s32[100]{0:T(128)} %param.13) | copy-start | bytes 1204
  6.5 85.8 %all-gather.2.cloned.1.call-start = ((), (), s32[]{:S(2)}) async-start(), calls=%async_computation.5 | async-start | bytes 1474560 | tf_op jit(solution)/shard_map/all_gather | solution.py:212
  24.7 16.0 %collective-permute-start.2 = (bf16[300,1024]{1,0:T(8,128)(2,1)}, bf16[300,1024]{1,0:T(8,128)(2,1)S(1)}, u32[]{:S(2)}, u32[]{:S(2)}) collective-permute-start(bf16[300,1024]{1,0:T(8,128)(2,1)} %slice.18), channel_id=1, source_target_pairs={{2,0},{4,2},{6,4},{8,6},{10,8},{12,10},{14,12},{16,14},{18,16},{20... | collective-permute-start | bytes 1843208 | tf_op jit(solution)/shard_map/ppermute | solution.py:36
  26.0 6.8 %collective-permute-start = (f32[1]{0:T(128)}, f32[1]{0:T(128)}, u32[]{:S(2)}, u32[]{:S(2)}) collective-permute-start(f32[1]{0:T(128)} %bitcast.6), channel_id=1, source_target_pairs={{0,1},{1,0},{2,3},{3,2},{4,5},{5,4},{6,7},{7,6},{8,9},{9,8},{10,11... | collective-permute-start | bytes 20 | tf_op jit(solution)/shard_map/ppermute | solution.py:215
  34.1 5.9 %collective-permute-start.1 = (f32[1]{0:T(128)}, f32[1]{0:T(128)}, u32[]{:S(2)}, u32[]{:S(2)}) collective-permute-start(f32[1]{0:T(128)} %add.48), channel_id=1, source_target_pairs={{0,256},{256,0},{1,257},{257,1},{2,258},{258,2},{3,259},{259,3},{4... | collective-permute-start | bytes 20 | tf_op jit(solution)/shard_map/ppermute | solution.py:216
  83.3 9.0 %copy-start.3 = (bf16[128,128]{1,0:T(8,128)(2,1)S(1)}, bf16[128,128]{1,0:T(8,128)(2,1)}, u32[]{:S(2)}) copy-start(bf16[128,128]{1,0:T(8,128)(2,1)} %constant.38.clone.second_ref) | copy-start | bytes 98308
  83.3 9.0 %copy-start.4 = (bf16[128,128]{1,0:T(8,128)(2,1)S(1)}, bf16[128,128]{1,0:T(8,128)(2,1)}, u32[]{:S(2)}) copy-start(bf16[128,128]{1,0:T(8,128)(2,1)} %constant.37.clone.first_ref) | copy-start | bytes 98308
  87.7 4.7 %copy-start = (bf16[4,1280,1280]{2,1,0:T(8,128)(2,1)}, bf16[4,1280,1280]{2,1,0:T(8,128)(2,1)S(1)}, u32[]{:S(2)}) copy-start(bf16[4,1280,1280]{2,1,0:T(8,128)(2,1)S(1)} %shard_map.83.shifted_ref) | copy-start | bytes 39321604
  92.4 1.3 copy-start.2
  124.6 20.3 %all-to-all-start.4 = ((f32[16,32,512]{2,1,0:T(8,128)}), f32[16,32,512]{2,1,0:T(8,128)S(1)}, u32[]{:S(2)}, u32[]{:S(2)}) async-start(f32[16,32,512]{2,1,0:T(8,128)} %bitcast.9), calls=%async_computation.4 | async-start | bytes 2097152 | tf_op jit(solution)/shard_map/all_to_all | solution.py:243
Sparse Core Ops, SparseCore 0:
  23.9 55.9 all-gather.1

commit v3 on v2

--- a/solution.py
+++ b/solution.py
@@ -87,18 +87,9 @@
         out_ref[g] = jnp.concatenate(pieces + [side], axis=0)
 
 
-def spread_kernel(trace_ref, root_ref, out_ref):
-    pieces = trace_ref.shape[0]
-    for t in range(pieces):
-        trace = (trace_ref[t] / root_ref[...]).astype(jnp.bfloat16).astype(jnp.float32)
-        for j in range(PAIR * SUB // 2):
-            low = trace if j == 0 else pltpu.roll(trace, WIDE - 2 * j, 1)
-            high = pltpu.roll(trace, WIDE - 2 * j - 1, 1)
-            both = jnp.concatenate([low, high], axis=0).astype(jnp.bfloat16)
-            out_ref[0, j * 2 * GROUP : (j + 1) * 2 * GROUP, t * WIDE : (t + 1) * WIDE] = both
-
-
-def corr_kernel(panel_ref, first_ref, second_ref, shifted_ref, out_ref, mixed, panels):
+def corr_kernel(
+    panel_ref, first_ref, second_ref, trace_ref, root_ref, out_ref, mixed, panels, shifted
+):
     chunks = panel_ref.shape[0] // LANES
     lags = out_ref.shape[-1]
     count = ROWS // PAIR
@@ -119,8 +110,15 @@
             a, h = divmod(r, PAIR)
             panels[a * LANES : (a + 1) * LANES, h * WIDE : (h + 1) * WIDE] = part
 
-    pieces = out_ref.shape[2]
-    sums = jnp.dot(panels[...], shifted_ref[0], preferred_element_type=jnp.float32)
+    pieces = trace_ref.shape[0]
+    for t in range(pieces):
+        trace = (trace_ref[t] / root_ref[...]).astype(jnp.bfloat16).astype(jnp.float32)
+        for j in range(PAIR * SUB // 2):
+            low = trace if j == 0 else pltpu.roll(trace, WIDE - 2 * j, 1)
+            high = pltpu.roll(trace, WIDE - 2 * j - 1, 1)
+            both = jnp.concatenate([low, high], axis=0).astype(jnp.bfloat16)
+            shifted[j * 2 * GROUP : (j + 1) * 2 * GROUP, t * WIDE : (t + 1) * WIDE] = both
+    sums = jnp.dot(panels[...], shifted[...], preferred_element_type=jnp.float32)
     for t in range(pieces):
         total = sums[:LANES, t * WIDE : t * WIDE + lags]
         for a in range(1, count):
@@ -153,23 +151,7 @@
     return pl.BlockSpec(shape, lambda i: (0,) * len(shape))
 
 
-def spread(traces, root_power):
-    depth = PAIR * SUB * GROUP
-    return pl.pallas_call(
-        spread_kernel,
-        grid=(GROUPS // PIECES,),
-        in_specs=[
-            pl.BlockSpec((PIECES, GROUP, WIDE), lambda i: (i, 0, 0)),
-            whole(root_power.shape),
-        ],
-        out_specs=pl.BlockSpec((1, depth, PIECES * WIDE), lambda i: (i, 0, 0)),
-        out_shape=jax.ShapeDtypeStruct((GROUPS // PIECES, depth, PIECES * WIDE), jnp.bfloat16),
-        compiler_params=params(32),
-        cost_estimate=pl.CostEstimate(flops=20 << 20, bytes_accessed=14 << 20, transcendentals=0),
-    )(traces, root_power)
-
-
-def correlate(gathered, shifted, lags):
+def correlate(gathered, traces, root_power, lags):
     first, second = orders()
     depth = PAIR * SUB * GROUP
     flops = 2 * ROWS // PAIR * LANES * depth * WIDE * GROUPS
@@ -180,17 +162,19 @@
             whole(gathered.shape),
             whole(first.shape),
             whole(second.shape),
-            pl.BlockSpec((1,) + shifted.shape[1:], lambda i: (i, 0, 0)),
+            pl.BlockSpec((PIECES, GROUP, WIDE), lambda i: (i, 0, 0)),
+            whole(root_power.shape),
         ],
         out_specs=pl.BlockSpec((2, 2, PIECES, 32, lags), lambda i: (0, 0, i, 0, 0)),
         out_shape=jax.ShapeDtypeStruct((2, 2, GROUPS, 32, lags), jnp.float32),
         scratch_shapes=[
             pltpu.VMEM((ROWS, LANES, WIDE), jnp.bfloat16),
             pltpu.VMEM((ROWS // PAIR * LANES, depth), jnp.bfloat16),
+            pltpu.VMEM((depth, PIECES * WIDE), jnp.bfloat16),
         ],
         compiler_params=params(48),
-        cost_estimate=pl.CostEstimate(flops=flops, bytes_accessed=17 << 20, transcendentals=0),
-    )(gathered, first, second, shifted)
+        cost_estimate=pl.CostEstimate(flops=flops, bytes_accessed=4 << 20, transcendentals=0),
+    )(gathered, first, second, traces, root_power)
 
 
 def local(raw_traces, fir_taps, templates, start_offsets, channel_mask, station_shifts):
@@ -209,6 +193,7 @@
     message = jnp.broadcast_to(message, (GROUPS, 2, ROWS, SUB * GROUP))
     message = message.reshape(2 * GROUPS, ROWS, SUB * GROUP)
     exchanged = lax.all_to_all(message, ("y", "xl", "zp"), 0, 0, tiled=True)
+    exchanged, raw_rim = lax.optimization_barrier((exchanged, raw_rim))
     gathered = lax.all_gather(exchanged, "zq", axis=0, tiled=True)
     gathered = gathered.reshape(blocks * ROWS, SUB * GROUP)
 
@@ -236,11 +221,11 @@
     norms = facts[:, GROUP : GROUP + GROUPS].T.reshape(4, 2 * along)
     norms = lax.dynamic_index_in_dim(norms, lax.axis_index(("xh", "core")), 0, keepdims=False)
 
-    shifted = spread(traces, root_power[:, None])
-    sums = correlate(gathered, shifted, lags)
+    sums = correlate(gathered, traces, root_power[:, None], lags)
     sums = jnp.sum(lax.all_to_all(sums, "core", 0, 0, tiled=True), axis=0)
-    sums = sums.reshape(2 * GROUPS, 32, lags)
-    sums = jnp.sum(lax.all_to_all(sums, ("xh", "y", "xl"), 0, 0, tiled=True), axis=0)
+    sums = sums.astype(jnp.bfloat16).reshape(2 * GROUPS, 32, lags)
+    sums = lax.all_to_all(sums, ("xh", "y", "xl"), 0, 0, tiled=True)
+    sums = jnp.sum(sums.astype(jnp.float32), axis=0)
     return sums / jnp.sqrt(norms + 1e-05)[:, None]
 
 

time: 153 us -> 142 us (0.928)
  blocking collectives: 70.9 us -> 49.7 us
  starting transfers between devices: 14.3 us -> 24.3 us
  waiting for transfers between devices: 19 us -> 27.9 us
  Pallas kernels: 18.6 us -> 13.8 us
  local copies, waits for them, and re-layouts: 8.71 us -> 4.73 us
    all_to_all x1 -> x0, blocking collectives: 13.5 us -> none  [local(): exchanged = lax.all_to_all(message, ('y', 'xl', 'zp'), 0, 0, tiled=True)]
    ppermute x1, waiting for transfers between devices: 0.01 us -> 11.2 us  [from_next_block(): return lax.ppermute(value, BLK, [(i + 1, i) for i in range(count - 1)])]
    all_to_all x1 -> x2, starting transfers between devices: 3.89 us -> 13.8 us  [the longest x1 7.41 us: local(): exchanged = lax.all_to_all(message, ('y', 'xl', 'zp'), 0, 0, tiled=True)]
    all_to_all x1, blocking collectives: 18.4 us -> 8.84 us  [local(): sums = jnp.sum(lax.all_to_all(sums, 'core', 0, 0, tiled=True), axis=0)]
    unnamed x15, local copies, waits for them, and re-layouts: 6.18 us -> 1.54 us
    pallas_call x1 -> x0, Pallas kernels: 4.35 us -> none  [spread(): pl.pallas_call(spread_kernel, grid=(GROUPS // PIECES,), in_specs=[pl.Bloc...]
    all_to_all x1 -> x2, waiting for transfers between devices: 16.2 us -> 14.4 us  [the longest x1 10.5 us: local(): sums = lax.all_to_all(sums, ('xh', 'y', 'xl'), 0, 0, tiled=True)]
  transfers between devices with their start and end apart: 5 -> 6, of which waited for: 3 -> 6; matrix products, arithmetic and copies ran while one was open for 2% -> 2% of each run, Pallas kernels for 5% -> 2%
where the time goes in v3:
time: 142 us; the launch traced here: 141 us
  blocking collectives  49.7 us (35%)
  waiting for transfers between devices  27.9 us (20%)
  starting transfers between devices  24.3 us (17%)
  between operations  16.2 us (11%)
  Pallas kernels  13.8 us (10%)
  local copies, waits for them, and re-layouts  4.73 us (3%)
  other arithmetic  4.59 us (3%)
    all_to_all x1, blocking collectives, local(): traces = lax.all_to_all(traces, ('y', 'xl'), 0, 0, tiled=True)  22.1 us
    all_to_all x1, blocking collectives, local(): facts = lax.all_to_all(facts, ('zq', 'zp'), 0, 0, tiled=True)  18.7 us
    ppermute x1, waiting for transfers between devices, from_next_block(): return lax.ppermute(value, BLK, [(i + 1, i) for i in range(count - 1)])  11.2 us
    pallas_call x1, Pallas kernels, correlate(): pl.pallas_call(corr_kernel, grid=(GROUPS // PIECES,), in_specs=[whole(gat...  10.7 us
    all_to_all x1, waiting for transfers between devices, local(): sums = lax.all_to_all(sums, ('xh', 'y', 'xl'), 0, 0, tiled=True)  10.5 us
    all_to_all x1, blocking collectives, local(): sums = jnp.sum(lax.all_to_all(sums, 'core', 0, 0, tiled=True), axis=0)  8.84 us
    all_to_all x1, starting transfers between devices, local(): exchanged = lax.all_to_all(message, ('y', 'xl', 'zp'), 0, 0, tiled=True)  7.41 us
    all_to_all x1, starting transfers between devices, local(): sums = lax.all_to_all(sums, ('xh', 'y', 'xl'), 0, 0, tiled=True)  6.42 us
  transfers between devices with their start and end apart: 6, of which 6 were waited for; matrix products, arithmetic and copies ran while one was open for 2% of the time, Pallas kernels for 2%

profile of v3, /device:TPU:1, one launch (start us, length us, event | category | flops | bytes accessed | tf_op | source)
XLA Modules:
  0.0 141.2 jit_solution(72276986471611570)
XLA Ops:
  7.3 0.7 convert_reduce_fusion.1
  8.0 1.7 %multiply_reduce_fusion = (f32[]{:T(128)}, bf16[300,128]{1,0:T(8,128)(2,1)S(1)}) fusion(bf16[300]{0:T(512)(128)(2,1)S(1)} %convert_reduce_fusion.1, bf16[1,300,256]{2,1,0:T(8,128)(2,1)} %param.10, s32[]{:T(128)S(6)} %select_n.7), kind=kLoop, calls=%fused_computation.2 | loop fusion | flops 268799 | bytes 154208 | tf_op jit(solution)/shard_map/reduce_sum | solution.py:188
  9.7 0.2 copy.21
  10.0 0.3 broadcast_in_dim.12
  10.2 0.7 broadcast_in_dim.13
  10.9 7.4 %all-to-all-start = ((bf16[16,8,640]{2,1,0:T(8,128)(2,1)}), bf16[16,8,640]{2,1,0:T(8,128)(2,1)S(1)}, u32[]{:S(2)}, u32[]{:S(2)}) async-start(bf16[16,8,640]{2,1,0:T(8,128)(2,1)} %bitcast.4), calls=%async_computation | async-start | bytes 327680 | tf_op jit(solution)/shard_map/all_to_all | solution.py:195
  18.4 0.9 slice.18
  19.3 1.3 collective-permute-start
  20.6 3.9 %all-to-all-done = bf16[16,8,640]{2,1,0:T(8,128)(2,1)S(1)} async-done(((bf16[16,8,640]{2,1,0:T(8,128)(2,1)}), bf16[16,8,640]{2,1,0:T(8,128)(2,1)S(1)}, u32[]{:S(2)}, u32[]{:S(2)}) %all-to-all-start) | async-done | bytes 163872 | tf_op jit(solution)/shard_map/all_to_all | solution.py:195
  24.5 11.2 %collective-permute-done.rim_ref = bf16[300,1024]{1,0:T(8,128)(2,1)S(1)} collective-permute-done((bf16[300,1024]{1,0:T(8,128)(2,1)}, bf16[300,1024]{1,0:T(8,128)(2,1)S(1)}, u32[]{:S(2)}, u32[]{:S(2)}) %collective-permute-start) | collective-permute-done | bytes 614432 | tf_op jit(solution)/shard_map/ppermute | solution.py:36
  35.7 4.9 %collective-permute-start.1 = (f32[1]{0:T(128)}, f32[1]{0:T(128)}, u32[]{:S(2)}, u32[]{:S(2)}) collective-permute-start(f32[1]{0:T(128)} %bitcast.6), channel_id=1, source_target_pairs={{0,1},{1,0},{2,3},{3,2},{4,5},{5,4},{6,7},{7,6},{8,9},{9,8},{10,11... | collective-permute-start | bytes 20 | tf_op jit(solution)/shard_map/ppermute | solution.py:200
  40.8 0.1 broadcast_in_dim_reshape.4.shift_ref
  40.9 0.4 tile.10
  41.3 0.2 reshape.68.weights_ref
  41.5 0.2 collective-permute-done.1
  43.0 4.2 %collective-permute-start.2 = (f32[1]{0:T(128)}, f32[1]{0:T(128)}, u32[]{:S(2)}, u32[]{:S(2)}) collective-permute-start(f32[1]{0:T(128)} %add.48), channel_id=1, source_target_pairs={{0,256},{256,0},{1,257},{257,1},{2,258},{258,2},{3,259},{259,3},{4... | collective-permute-start | bytes 20 | tf_op jit(solution)/shard_map/ppermute | solution.py:201
  47.2 1.6 %collective-permute-done.2 = f32[1]{0:T(128)} collective-permute-done((f32[1]{0:T(128)}, f32[1]{0:T(128)}, u32[]{:S(2)}, u32[]{:S(2)}) %collective-permute-start.2) | collective-permute-done | bytes 36 | tf_op jit(solution)/shard_map/ppermute | solution.py:201
  49.4 3.1 %shard_map.82 = f32[8,40,640]{2,1,0:T(8,128)S(1)} custom-call(f32[1]{0:T(128)S(6)} %add.49.norm_ref, bf16[300,2560]{1,0:T(8,128)(2,1)S(1)} %copy-done, bf16[300,1024]{1,0:T(8,128)(2,1)S(1)} %collective-permute-done.rim_ref, bf16[128,768]{1,0:T(8,128)(2,1)S(1)} %reshape.68.weights_ref, s32[300,1]{1,0:T(8,128)S(1)} %broadcast_in_dim_reshape.4.shift_ref), custom_call_target="tpu_custom_call" | custom-call | flops 419430400 | bytes 4194304 | tf_op jit(solution)/shard_map/pallas_call | solution.py:203
  52.5 22.1 %all_to_all.29.trace_ref = f32[8,40,640]{2,1,0:T(8,128)S(1)} all-to-all(f32[8,40,640]{2,1,0:T(8,128)S(1)} %shard_map.82), channel_id=1, replica_groups=mesh['xh'=2,'y'=4,'xl'=2,'zq'=8,'zp'=2,'core'=2] {'y','xl'}, dimensions={0} | all-to-all | bytes 1638400 | tf_op jit(solution)/shard_map/all_to_all | solution.py:211
  74.6 0.1 slice_reduce_fusion.2
  74.8 0.2 slice_reduce_fusion
  75.1 18.7 %all_to_all.30 = f32[16,1,128]{2,1,0:T(1,128)S(1)} all-to-all(f32[16,1,128]{2,1,0:T(1,128)S(1)} %broadcast_in_dim.31), channel_id=1, replica_groups=mesh['xh'=2,'y'=4,'xl'=2,'zq'=8,'zp'=2,'core'=2] {'zq','zp'}, dimensions={0} | all-to-all | bytes 16384 | tf_op jit(solution)/shard_map/all_to_all | solution.py:218
  93.8 0.1 copy.19.root_ref
  93.9 0.6 all-gather.2.cloned.1.call-done
  94.4 1.3 copy-done.1
  95.8 10.7 %shard_map.83 = f32[2,2,8,32,512]{4,3,2,1,0:T(8,128)S(1)} custom-call(bf16[1024,640]{1,0:T(8,128)(2,1)S(1)} %bitcast.23, bf16[128,128]{1,0:T(8,128)(2,1)S(1)} %copy-done.3, bf16[128,128]{1,0:T(8,128)(2,1)S(1)} %copy-done.2, f32[8,40,640]{2,1,0:T(8,128)S(1)} %all_to_all.29.trace_ref, f32[40,1]{1,0:T(8,128)S(1)} %copy.19.root_ref), custom_call_target="tpu_custom_call" | custom-call | flops 6710886400 | bytes 4194304 | tf_op jit(solution)/shard_map/pallas_call | solution.py:158
  106.5 8.8 %all_to_all.31 = f32[2,2,8,32,512]{4,3,2,1,0:T(8,128)S(1)} all-to-all(f32[2,2,8,32,512]{4,3,2,1,0:T(8,128)S(1)} %shard_map.83), channel_id=1, replica_groups=mesh['xh'=2,'y'=4,'xl'=2,'zq'=8,'zp'=2,'core'=2] {'core'}, dimensions={0} | all-to-all | bytes 4194304 | tf_op jit(solution)/shard_map/all_to_all | solution.py:225
  115.3 1.1 reduce_sum.48
  116.5 6.4 %all-to-all-start.4 = ((bf16[16,32,512]{2,1,0:T(8,128)(2,1)}), bf16[16,32,512]{2,1,0:T(8,128)(2,1)S(1)}, u32[]{:S(2)}, u32[]{:S(2)}) async-start(bf16[16,32,512]{2,1,0:T(8,128)(2,1)} %bitcast.9), calls=%async_computation.4 | async-start | bytes 1048576 | tf_op jit(solution)/shard_map/all_to_all | solution.py:227
  123.0 0.1 reshape.69
  123.1 10.5 %all-to-all-done.4 = bf16[16,32,512]{2,1,0:T(8,128)(2,1)S(1)} async-done(((bf16[16,32,512]{2,1,0:T(8,128)(2,1)}), bf16[16,32,512]{2,1,0:T(8,128)(2,1)S(1)}, u32[]{:S(2)}, u32[]{:S(2)}) %all-to-all-start.4) | async-done | bytes 524320 | tf_op jit(solution)/shard_map/all_to_all | solution.py:227
  133.7 0.7 broadcast_divide_fusion
  (31 shorter events, 0.7 us)
Async XLA Ops:
  6.5 11.8 %copy-start = (bf16[300,2560]{1,0:T(8,128)(2,1)S(1)}, bf16[300,2560]{1,0:T(8,128)(2,1)}, u32[]{:S(2)}) copy-start(bf16[300,2560]{1,0:T(8,128)(2,1)} %raw_ref.1) | copy-start | bytes 4608004
  6.5 34.1 %copy-start.6 = (bf16[60]{0:T(256)(128)(2,1)S(1)}, bf16[60]{0:T(256)(128)(2,1)}, u32[]{:S(2)}) copy-start(bf16[60]{0:T(256)(128)(2,1)} %param.9) | copy-start | bytes 364
  6.5 34.1 %copy-start.5 = (s32[100]{0:T(128)S(1)}, s32[100]{0:T(128)}, u32[]{:S(2)}) copy-start(s32[100]{0:T(128)} %param.13) | copy-start | bytes 1204
  10.9 13.6 %all-to-all-start = ((bf16[16,8,640]{2,1,0:T(8,128)(2,1)}), bf16[16,8,640]{2,1,0:T(8,128)(2,1)S(1)}, u32[]{:S(2)}, u32[]{:S(2)}) async-start(bf16[16,8,640]{2,1,0:T(8,128)(2,1)} %bitcast.4), calls=%async_computation | async-start | bytes 327680 | tf_op jit(solution)/shard_map/all_to_all | solution.py:195
  18.3 76.1 %all-gather.2.cloned.1.call-start = ((), (), s32[]{:S(2)}) async-start(), calls=%async_computation.5 | async-start | bytes 1474560 | tf_op jit(solution)/shard_map/all_gather | solution.py:197
  19.3 16.4 %collective-permute-start = (bf16[300,1024]{1,0:T(8,128)(2,1)}, bf16[300,1024]{1,0:T(8,128)(2,1)S(1)}, u32[]{:S(2)}, u32[]{:S(2)}) collective-permute-start(bf16[300,1024]{1,0:T(8,128)(2,1)} %slice.18), channel_id=1, source_target_pairs={{2,0},{4,2},{6,4},{8,6},{10,8},{12,10},{14,12},{16,14},{18,16},{20... | collective-permute-start | bytes 1843208 | tf_op jit(solution)/shard_map/ppermute | solution.py:36
  24.5 11.2 %copy-start.4 = (bf16[16,8,640]{2,1,0:T(8,128)(2,1)}, bf16[16,8,640]{2,1,0:T(8,128)(2,1)S(1)}, u32[]{:S(2)}) copy-start(bf16[16,8,640]{2,1,0:T(8,128)(2,1)S(1)} %all-to-all-done) | copy-start | bytes 491524
  35.7 6.0 %collective-permute-start.1 = (f32[1]{0:T(128)}, f32[1]{0:T(128)}, u32[]{:S(2)}, u32[]{:S(2)}) collective-permute-start(f32[1]{0:T(128)} %bitcast.6), channel_id=1, source_target_pairs={{0,1},{1,0},{2,3},{3,2},{4,5},{5,4},{6,7},{7,6},{8,9},{9,8},{10,11... | collective-permute-start | bytes 20 | tf_op jit(solution)/shard_map/ppermute | solution.py:200
  43.0 5.7 %collective-permute-start.2 = (f32[1]{0:T(128)}, f32[1]{0:T(128)}, u32[]{:S(2)}, u32[]{:S(2)}) collective-permute-start(f32[1]{0:T(128)} %add.48), channel_id=1, source_target_pairs={{0,256},{256,0},{1,257},{257,1},{2,258},{258,2},{3,259},{259,3},{4... | collective-permute-start | bytes 20 | tf_op jit(solution)/shard_map/ppermute | solution.py:201
  49.4 45.1 %copy-start.2 = (bf16[128,128]{1,0:T(8,128)(2,1)S(1)}, bf16[128,128]{1,0:T(8,128)(2,1)}, u32[]{:S(2)}) copy-start(bf16[128,128]{1,0:T(8,128)(2,1)} %constant.38.clone.second_ref) | copy-start | bytes 98308
  49.4 45.1 %copy-start.3 = (bf16[128,128]{1,0:T(8,128)(2,1)S(1)}, bf16[128,128]{1,0:T(8,128)(2,1)}, u32[]{:S(2)}) copy-start(bf16[128,128]{1,0:T(8,128)(2,1)} %constant.37.clone.first_ref) | copy-start | bytes 98308
  94.4 1.3 copy-start.1
  116.5 17.1 %all-to-all-start.4 = ((bf16[16,32,512]{2,1,0:T(8,128)(2,1)}), bf16[16,32,512]{2,1,0:T(8,128)(2,1)S(1)}, u32[]{:S(2)}, u32[]{:S(2)}) async-start(bf16[16,32,512]{2,1,0:T(8,128)(2,1)} %bitcast.9), calls=%async_computation.4 | async-start | bytes 1048576 | tf_op jit(solution)/shard_map/all_to_all | solution.py:227
Sparse Core Ops, SparseCore 0:
  35.8 58.5 all-gather.1

commit v4 on v3

--- a/solution.py
+++ b/solution.py
@@ -18,7 +18,7 @@
 GROUPS = 8
 GROUP = 40
 USED = 38
-RIM = 1024
+RIM = 192
 PIECES = 2
 BLK = ("y", "xl", "zq", "zp")
 
@@ -43,24 +43,33 @@
     return flat.reshape(LANES, depth)
 
 
+def product(left, right):
+    dims = (((1,), (1,)), ((), ()))
+    return lax.dot_general(left, right, dims, preferred_element_type=jnp.float32)
+
+
+def rim_kernel(raw_ref, weights_ref, out_ref):
+    step = DECIM * LANES
+    out_ref[:, :LANES] = product(raw_ref[:, : step + LANES], weights_ref[...])
+    later = product(raw_ref[:, step : 2 * step + LANES], weights_ref[...])
+    raw = pltpu.roll(raw_ref[:, :LANES].astype(jnp.float32), RIM % LANES, 1)
+    lane = lax.broadcasted_iota(jnp.int32, raw.shape, 1)
+    out_ref[:, LANES:] = jnp.where(lane < RIM % LANES, later, raw)
+
+
 def trace_kernel(norm_ref, raw_ref, rim_ref, weights_ref, shift_ref, out_ref):
     channels = raw_ref.shape[0]
     step = DECIM * LANES
     own = raw_ref.shape[1] // step
-    dims = (((1,), (1,)), ((), ()))
-
-    def product(left, right):
-        return lax.dot_general(left, right, dims, preferred_element_type=jnp.float32)
-
     blocks = []
     for i in range(own - 1):
         blocks.append(product(raw_ref[:, i * step : i * step + step + LANES], weights_ref[...]))
+    raw_rim = pltpu.roll(rim_ref[:, LANES:], LANES - RIM % LANES, 1).astype(jnp.bfloat16)
     blocks.append(
         product(raw_ref[:, (own - 1) * step :], weights_ref[:, :step])
-        + product(rim_ref[:, :LANES], weights_ref[:, step:])
+        + product(raw_rim, weights_ref[:, step:])
     )
-    blocks.append(product(rim_ref[:, : step + LANES], weights_ref[...]))
-    blocks.append(product(rim_ref[:, step:], weights_ref[:, : RIM - step]))
+    blocks.append(rim_ref[...])
     squares = blocks[0] * blocks[0]
     for block in blocks[1:own]:
         squares = squares + block * block
@@ -181,7 +190,16 @@
     channels, raw_len = raw_traces.shape
     lags = raw_len // DECIM
     blocks = lax.axis_size(BLK)
-    raw_rim = from_next_block(raw_traces[:, :RIM])
+    weights = tap_matrix(fir_taps)
+    rim = pl.pallas_call(
+        rim_kernel,
+        in_specs=[vmem()] * 2,
+        out_specs=vmem(),
+        out_shape=jax.ShapeDtypeStruct((channels, 2 * LANES), jnp.float32),
+        compiler_params=params(32),
+        cost_estimate=pl.CostEstimate(flops=128 << 20, bytes_accessed=2 << 20, transcendentals=0),
+    )(raw_traces[:, : 2 * DECIM * LANES + LANES], weights)
+    rim = from_next_block(rim)
 
     window = lax.dynamic_slice_in_dim(templates[0], start_offsets[0], TLEN, axis=1)
     panel = window * channel_mask[0].astype(jnp.bfloat16)[:, None]
@@ -193,12 +211,11 @@
     message = jnp.broadcast_to(message, (GROUPS, 2, ROWS, SUB * GROUP))
     message = message.reshape(2 * GROUPS, ROWS, SUB * GROUP)
     exchanged = lax.all_to_all(message, ("y", "xl", "zp"), 0, 0, tiled=True)
-    exchanged, raw_rim = lax.optimization_barrier((exchanged, raw_rim))
+    norm = norm + lax.ppermute(norm, "core", [(0, 1), (1, 0)])
+    norm = norm + lax.ppermute(norm, "xh", [(0, 1), (1, 0)])
+    exchanged, rim, norm = lax.optimization_barrier((exchanged, rim, norm))
     gathered = lax.all_gather(exchanged, "zq", axis=0, tiled=True)
     gathered = gathered.reshape(blocks * ROWS, SUB * GROUP)
-
-    norm = norm + lax.ppermute(norm, "core", [(0, 1), (1, 0)])
-    norm = norm + lax.ppermute(norm, "xh", [(0, 1), (1, 0)])
 
     traces = pl.pallas_call(
         trace_kernel,
@@ -207,7 +224,7 @@
         out_shape=jax.ShapeDtypeStruct((GROUPS, GROUP, WIDE), jnp.float32),
         compiler_params=params(32),
         cost_estimate=pl.CostEstimate(flops=400 << 20, bytes_accessed=4 << 20, transcendentals=0),
-    )(norm, raw_traces, raw_rim, tap_matrix(fir_taps), jnp.repeat(station_shifts, 3)[:, None])
+    )(norm, raw_traces, rim, weights, jnp.repeat(station_shifts, 3)[:, None])
     traces = lax.all_to_all(traces, ("y", "xl"), 0, 0, tiled=True)
 
     powers = jnp.sum(traces[:, :, WIDE - 1], axis=0)

time: 142 us -> 140 us (0.986)
    all_gather x1, waiting for transfers between devices: 0.58 us -> 12.2 us  [local(): gathered = lax.all_gather(exchanged, 'zq', axis=0, tiled=True)]
    ppermute x1, waiting for transfers between devices: 11.2 us -> 0.01 us  [from_next_block(): return lax.ppermute(value, BLK, [(i + 1, i) for i in range(count - 1)])]
    all_to_all x1, waiting for transfers between devices: 3.91 us -> 0.01 us  [local(): exchanged = lax.all_to_all(message, ('y', 'xl', 'zp'), 0, 0, tiled=True)]
    all_to_all x1, blocking collectives: 22.1 us -> 24.6 us  [local(): traces = lax.all_to_all(traces, ('y', 'xl'), 0, 0, tiled=True)]
    all_to_all x1, blocking collectives: 18.7 us -> 16.7 us  [local(): facts = lax.all_to_all(facts, ('zq', 'zp'), 0, 0, tiled=True)]
    all_to_all x1, blocking collectives: 8.84 us -> 7.25 us  [local(): sums = jnp.sum(lax.all_to_all(sums, 'core', 0, 0, tiled=True), axis=0)]
  transfers between devices with their start and end apart: 6 -> 6, of which waited for: 6 -> 4; matrix products, arithmetic and copies ran while one was open for 2% -> 1% of each run, Pallas kernels for 2% -> 2%
where the time goes in v4:
time: 140 us; the launch traced here: 139 us
  blocking collectives  48.5 us (35%)
  waiting for transfers between devices  26.6 us (19%)
  starting transfers between devices  24.5 us (18%)
  between operations  16.3 us (12%)
  Pallas kernels  14.1 us (10%)
  other arithmetic  4.59 us (3%)
  local copies, waits for them, and re-layouts  4.54 us (3%)
    all_to_all x1, blocking collectives, local(): traces = lax.all_to_all(traces, ('y', 'xl'), 0, 0, tiled=True)  24.6 us
    all_to_all x1, blocking collectives, local(): facts = lax.all_to_all(facts, ('zq', 'zp'), 0, 0, tiled=True)  16.7 us
    all_gather x1, waiting for transfers between devices, local(): gathered = lax.all_gather(exchanged, 'zq', axis=0, tiled=True)  12.2 us
    pallas_call x1, Pallas kernels, correlate(): pl.pallas_call(corr_kernel, grid=(GROUPS // PIECES,), in_specs=[whole(gat...  10.7 us
    all_to_all x1, waiting for transfers between devices, local(): sums = lax.all_to_all(sums, ('xh', 'y', 'xl'), 0, 0, tiled=True)  10.5 us
    all_to_all x1, starting transfers between devices, local(): sums = lax.all_to_all(sums, ('xh', 'y', 'xl'), 0, 0, tiled=True)  7.81 us
    all_to_all x1, starting transfers between devices, local(): exchanged = lax.all_to_all(message, ('y', 'xl', 'zp'), 0, 0, tiled=True)  7.38 us
    all_to_all x1, blocking collectives, local(): sums = jnp.sum(lax.all_to_all(sums, 'core', 0, 0, tiled=True), axis=0)  7.25 us
  transfers between devices with their start and end apart: 6, of which 4 were waited for; matrix products, arithmetic and copies ran while one was open for 1% of the time, Pallas kernels for 2%

profile of v4, /device:TPU:1, one launch (start us, length us, event | category | flops | bytes accessed | tf_op | source)
XLA Modules:
  0.0 139.1 jit_solution(2900091595176862371)
XLA Ops:
  7.3 0.7 convert_reduce_fusion.1
  8.0 1.7 %multiply_reduce_fusion = (f32[]{:T(128)}, bf16[300,128]{1,0:T(8,128)(2,1)S(1)}) fusion(bf16[300]{0:T(512)(128)(2,1)S(1)} %convert_reduce_fusion.1, bf16[1,300,256]{2,1,0:T(8,128)(2,1)} %param.10, s32[]{:T(128)S(6)} %select_n.7), kind=kLoop, calls=%fused_computation.2 | loop fusion | flops 268799 | bytes 154208 | tf_op jit(solution)/shard_map/reduce_sum | solution.py:206
  9.7 0.2 copy.21
  10.0 0.3 broadcast_in_dim.12
  10.2 0.7 broadcast_in_dim.13
  10.9 7.4 %all-to-all-start = ((bf16[16,8,640]{2,1,0:T(8,128)(2,1)}), bf16[16,8,640]{2,1,0:T(8,128)(2,1)S(1)}, u32[]{:S(2)}, u32[]{:S(2)}) async-start(bf16[16,8,640]{2,1,0:T(8,128)(2,1)} %bitcast.4), calls=%async_computation | async-start | bytes 327680 | tf_op jit(solution)/shard_map/all_to_all | solution.py:213
  18.4 0.4 tile.10
  18.8 0.2 reshape.67.weights_ref
  19.1 0.4 shard_map.82
  19.5 1.3 collective-permute-start
  20.8 4.9 %collective-permute-start.1 = (f32[1]{0:T(128)}, f32[1]{0:T(128)}, u32[]{:S(2)}, u32[]{:S(2)}) collective-permute-start(f32[1]{0:T(128)} %bitcast.5), channel_id=1, source_target_pairs={{0,1},{1,0},{2,3},{3,2},{4,5},{5,4},{6,7},{7,6},{8,9},{9,8},{10,11... | collective-permute-start | bytes 20 | tf_op jit(solution)/shard_map/ppermute | solution.py:214
  25.7 0.9 collective-permute-done.1
  27.9 3.0 %collective-permute-start.2 = (f32[1]{0:T(128)}, f32[1]{0:T(128)}, u32[]{:S(2)}, u32[]{:S(2)}) collective-permute-start(f32[1]{0:T(128)} %add.48), channel_id=1, source_target_pairs={{0,256},{256,0},{1,257},{257,1},{2,258},{258,2},{3,259},{259,3},{4... | collective-permute-start | bytes 20 | tf_op jit(solution)/shard_map/ppermute | solution.py:215
  30.9 2.9 %collective-permute-done.2 = f32[1]{0:T(128)} collective-permute-done((f32[1]{0:T(128)}, f32[1]{0:T(128)}, u32[]{:S(2)}, u32[]{:S(2)}) %collective-permute-start.2) | collective-permute-done | bytes 36 | tf_op jit(solution)/shard_map/ppermute | solution.py:215
  34.5 0.7 copy-done.4
  35.2 0.1 broadcast_in_dim_reshape.4.shift_ref
  35.4 3.0 %shard_map.83 = f32[8,40,640]{2,1,0:T(8,128)S(1)} custom-call(f32[1]{0:T(128)S(6)} %add.49.norm_ref, bf16[300,2560]{1,0:T(8,128)(2,1)S(1)} %copy-done, f32[300,256]{1,0:T(8,128)S(1)} %collective-permute-done.rim_ref, bf16[128,768]{1,0:T(8,128)(2,1)S(1)} %reshape.67.weights_ref, s32[300,1]{1,0:T(8,128)S(1)} %broadcast_in_dim_reshape.4.shift_ref), custom_call_target="tpu_custom_call" | custom-call | flops 419430400 | bytes 4194304 | tf_op jit(solution)/shard_map/pallas_call | solution.py:220
  38.4 24.6 %all_to_all.29.trace_ref = f32[8,40,640]{2,1,0:T(8,128)S(1)} all-to-all(f32[8,40,640]{2,1,0:T(8,128)S(1)} %shard_map.83), channel_id=1, replica_groups=mesh['xh'=2,'y'=4,'xl'=2,'zq'=8,'zp'=2,'core'=2] {'y','xl'}, dimensions={0} | all-to-all | bytes 1638400 | tf_op jit(solution)/shard_map/all_to_all | solution.py:228
  63.0 0.1 slice_reduce_fusion.2
  63.1 0.2 slice_reduce_fusion
  63.3 0.1 pad_maximum_fusion
  63.4 16.7 %all_to_all.30 = f32[16,1,128]{2,1,0:T(1,128)S(1)} all-to-all(f32[16,1,128]{2,1,0:T(1,128)S(1)} %broadcast_in_dim.31), channel_id=1, replica_groups=mesh['xh'=2,'y'=4,'xl'=2,'zq'=8,'zp'=2,'core'=2] {'zq','zp'}, dimensions={0} | all-to-all | bytes 16384 | tf_op jit(solution)/shard_map/all_to_all | solution.py:235
  80.1 0.1 copy.19.root_ref
  80.2 12.2 %all-gather.2.cloned.1.call-done = bf16[128,8,640]{2,1,0:T(8,128)(2,1)} async-done(((bf16[16,8,640]{2,1,0:T(8,128)(2,1)}), bf16[128,8,640]{2,1,0:T(8,128)(2,1)}) %all-gather.2.cloned.1.call-update) | async-done | bytes 1310736 | tf_op jit(solution)/shard_map/all_gather | solution.py:217
  92.5 1.3 copy-done.1
  93.8 10.7 %shard_map.84 = f32[2,2,8,32,512]{4,3,2,1,0:T(8,128)S(1)} custom-call(bf16[1024,640]{1,0:T(8,128)(2,1)S(1)} %bitcast.23, bf16[128,128]{1,0:T(8,128)(2,1)S(1)} %copy-done.3, bf16[128,128]{1,0:T(8,128)(2,1)S(1)} %copy-done.2, f32[8,40,640]{2,1,0:T(8,128)S(1)} %all_to_all.29.trace_ref, f32[40,1]{1,0:T(8,128)S(1)} %copy.19.root_ref), custom_call_target="tpu_custom_call" | custom-call | flops 6710886400 | bytes 4194304 | tf_op jit(solution)/shard_map/pallas_call | solution.py:167
  104.5 7.3 %all_to_all.31 = f32[2,2,8,32,512]{4,3,2,1,0:T(8,128)S(1)} all-to-all(f32[2,2,8,32,512]{4,3,2,1,0:T(8,128)S(1)} %shard_map.84), channel_id=1, replica_groups=mesh['xh'=2,'y'=4,'xl'=2,'zq'=8,'zp'=2,'core'=2] {'core'}, dimensions={0} | all-to-all | bytes 4194304 | tf_op jit(solution)/shard_map/all_to_all | solution.py:242
  111.8 1.1 reduce_sum.48
  112.9 7.8 %all-to-all-start.4 = ((bf16[16,32,512]{2,1,0:T(8,128)(2,1)}), bf16[16,32,512]{2,1,0:T(8,128)(2,1)S(1)}, u32[]{:S(2)}, u32[]{:S(2)}) async-start(bf16[16,32,512]{2,1,0:T(8,128)(2,1)} %bitcast.9), calls=%async_computation.4 | async-start | bytes 1048576 | tf_op jit(solution)/shard_map/all_to_all | solution.py:244
  120.9 0.1 reshape.69
  121.0 10.5 %all-to-all-done.4 = bf16[16,32,512]{2,1,0:T(8,128)(2,1)S(1)} async-done(((bf16[16,32,512]{2,1,0:T(8,128)(2,1)}), bf16[16,32,512]{2,1,0:T(8,128)(2,1)S(1)}, u32[]{:S(2)}, u32[]{:S(2)}) %all-to-all-start.4) | async-done | bytes 524320 | tf_op jit(solution)/shard_map/all_to_all | solution.py:244
  131.5 0.7 broadcast_divide_fusion
  (32 shorter events, 0.6 us)
Async XLA Ops:
  6.5 11.8 %copy-start.6 = (bf16[60]{0:T(256)(128)(2,1)S(1)}, bf16[60]{0:T(256)(128)(2,1)}, u32[]{:S(2)}) copy-start(bf16[60]{0:T(256)(128)(2,1)} %param.9) | copy-start | bytes 364
  6.5 12.5 %copy-start = (bf16[300,2560]{1,0:T(8,128)(2,1)S(1)}, bf16[300,2560]{1,0:T(8,128)(2,1)}, u32[]{:S(2)}) copy-start(bf16[300,2560]{1,0:T(8,128)(2,1)} %raw_ref.1) | copy-start | bytes 4608004
  10.9 23.6 %all-to-all-start = ((bf16[16,8,640]{2,1,0:T(8,128)(2,1)}), bf16[16,8,640]{2,1,0:T(8,128)(2,1)S(1)}, u32[]{:S(2)}, u32[]{:S(2)}) async-start(bf16[16,8,640]{2,1,0:T(8,128)(2,1)} %bitcast.4), calls=%async_computation | async-start | bytes 327680 | tf_op jit(solution)/shard_map/all_to_all | solution.py:213
  18.3 74.2 %all-gather.2.cloned.1.call-start = ((), (), s32[]{:S(2)}) async-start(), calls=%async_computation.5 | async-start | bytes 1474560 | tf_op jit(solution)/shard_map/all_gather | solution.py:217
  18.8 16.4 %copy-start.5 = (s32[100]{0:T(128)S(1)}, s32[100]{0:T(128)}, u32[]{:S(2)}) copy-start(s32[100]{0:T(128)} %param.13) | copy-start | bytes 1204
  19.5 15.0 %collective-permute-start = (f32[300,256]{1,0:T(8,128)S(1)}, f32[300,256]{1,0:T(8,128)S(1)}, u32[]{:S(2)}, u32[]{:S(2)}) collective-permute-start(f32[300,256]{1,0:T(8,128)S(1)} %shard_map.82), channel_id=1, source_target_pairs={{2,0},{4,2},{6,4},{8,6},{10,8},{12,10},{14,12},{16,14},{18,16},{20... | collective-permute-start | bytes 921608 | tf_op jit(solution)/shard_map/ppermute | solution.py:36
  20.8 5.9 %collective-permute-start.1 = (f32[1]{0:T(128)}, f32[1]{0:T(128)}, u32[]{:S(2)}, u32[]{:S(2)}) collective-permute-start(f32[1]{0:T(128)} %bitcast.5), channel_id=1, source_target_pairs={{0,1},{1,0},{2,3},{3,2},{4,5},{5,4},{6,7},{7,6},{8,9},{9,8},{10,11... | collective-permute-start | bytes 20 | tf_op jit(solution)/shard_map/ppermute | solution.py:214
  27.9 5.9 %collective-permute-start.2 = (f32[1]{0:T(128)}, f32[1]{0:T(128)}, u32[]{:S(2)}, u32[]{:S(2)}) collective-permute-start(f32[1]{0:T(128)} %add.48), channel_id=1, source_target_pairs={{0,256},{256,0},{1,257},{257,1},{2,258},{258,2},{3,259},{259,3},{4... | collective-permute-start | bytes 20 | tf_op jit(solution)/shard_map/ppermute | solution.py:215
  34.5 0.7 copy-start.4
  35.4 57.1 %copy-start.2 = (bf16[128,128]{1,0:T(8,128)(2,1)S(1)}, bf16[128,128]{1,0:T(8,128)(2,1)}, u32[]{:S(2)}) copy-start(bf16[128,128]{1,0:T(8,128)(2,1)} %constant.38.clone.second_ref) | copy-start | bytes 98308
  35.4 57.1 %copy-start.3 = (bf16[128,128]{1,0:T(8,128)(2,1)S(1)}, bf16[128,128]{1,0:T(8,128)(2,1)}, u32[]{:S(2)}) copy-start(bf16[128,128]{1,0:T(8,128)(2,1)} %constant.37.clone.first_ref) | copy-start | bytes 98308
  92.5 1.3 copy-start.1
  112.9 18.5 %all-to-all-start.4 = ((bf16[16,32,512]{2,1,0:T(8,128)(2,1)}), bf16[16,32,512]{2,1,0:T(8,128)(2,1)S(1)}, u32[]{:S(2)}, u32[]{:S(2)}) async-start(bf16[16,32,512]{2,1,0:T(8,128)(2,1)} %bitcast.9), calls=%async_computation.4 | async-start | bytes 1048576 | tf_op jit(solution)/shard_map/all_to_all | solution.py:244
Sparse Core Ops, SparseCore 0:
  35.3 57.1 all-gather.1

commit v5 on v4

--- a/solution.py
+++ b/solution.py
@@ -211,9 +211,7 @@
     message = jnp.broadcast_to(message, (GROUPS, 2, ROWS, SUB * GROUP))
     message = message.reshape(2 * GROUPS, ROWS, SUB * GROUP)
     exchanged = lax.all_to_all(message, ("y", "xl", "zp"), 0, 0, tiled=True)
-    norm = norm + lax.ppermute(norm, "core", [(0, 1), (1, 0)])
-    norm = norm + lax.ppermute(norm, "xh", [(0, 1), (1, 0)])
-    exchanged, rim, norm = lax.optimization_barrier((exchanged, rim, norm))
+    exchanged, rim = lax.optimization_barrier((exchanged, rim))
     gathered = lax.all_gather(exchanged, "zq", axis=0, tiled=True)
     gathered = gathered.reshape(blocks * ROWS, SUB * GROUP)
 
@@ -235,8 +233,9 @@
     facts = lax.all_to_all(facts, ("zq", "zp"), 0, 0, tiled=True)
     powers = jnp.sum(facts[:, :GROUP], axis=0)
     root_power = jnp.sqrt(powers / (lags * blocks) + 1e-06)
-    norms = facts[:, GROUP : GROUP + GROUPS].T.reshape(4, 2 * along)
-    norms = lax.dynamic_index_in_dim(norms, lax.axis_index(("xh", "core")), 0, keepdims=False)
+    norms = facts[:, GROUP : GROUP + GROUPS].T.reshape(4, 1, 2 * along)
+    norms = jnp.sum(lax.all_to_all(norms, ("xh", "core"), 0, 0, tiled=True), axis=(0, 1))
+    root_power, norms = lax.optimization_barrier((root_power, norms))
 
     sums = correlate(gathered, traces, root_power[:, None], lags)
     sums = jnp.sum(lax.all_to_all(sums, "core", 0, 0, tiled=True), axis=0)

time: 140 us -> 136 us (0.971)
  waiting for transfers between devices: 26.6 us -> 23.6 us
  between operations: 16.3 us -> 14.4 us
  blocking collectives: 48.5 us -> 47 us
    all_gather x1, waiting for transfers between devices: 12.2 us -> 0.01 us  [local(): gathered = lax.all_gather(exchanged, 'zq', axis=0, tiled=True)]
    all_to_all x0 -> x1, starting transfers between devices: none -> 8.88 us  [local(): lax.all_to_all(norms, ('xh', 'core'), 0, 0, tiled=True)]
    ppermute x1, waiting for transfers between devices: 0.01 us -> 8.21 us  [from_next_block(): return lax.ppermute(value, BLK, [(i + 1, i) for i in range(count - 1)])]
    ppermute x2 -> x0, starting transfers between devices: 7.93 us -> none  [the longest x1 4.93 us: local(): norm = norm + lax.ppermute(norm, 'core', [(0, 1), (1, 0)])]
    all_to_all x0 -> x1, waiting for transfers between devices: none -> 4.67 us  [local(): lax.all_to_all(norms, ('xh', 'core'), 0, 0, tiled=True)]
    ppermute x2 -> x0, waiting for transfers between devices: 3.82 us -> none  [the longest x1 2.89 us: local(): norm = norm + lax.ppermute(norm, 'xh', [(0, 1), (1, 0)])]
    all_to_all x1, blocking collectives: 24.6 us -> 22.2 us  [local(): traces = lax.all_to_all(traces, ('y', 'xl'), 0, 0, tiled=True)]
    all_to_all x1, blocking collectives: 16.7 us -> 19 us  [local(): facts = lax.all_to_all(facts, ('zq', 'zp'), 0, 0, tiled=True)]
  transfers between devices with their start and end apart: 6 -> 5, of which waited for: 4 -> 3; matrix products, arithmetic and copies ran while one was open for 1% -> 2% of each run, Pallas kernels for 2% -> 3%
where the time goes in v5:
time: 136 us; the launch traced here: 135 us
  blocking collectives  47 us (35%)
  starting transfers between devices  25.9 us (19%)
  waiting for transfers between devices  23.6 us (17%)
  Pallas kernels  14.7 us (11%)
  between operations  14.4 us (11%)
  local copies, waits for them, and re-layouts  5.11 us (4%)
  other arithmetic  4.6 us (3%)
    all_to_all x1, blocking collectives, local(): traces = lax.all_to_all(traces, ('y', 'xl'), 0, 0, tiled=True)  22.2 us
    all_to_all x1, blocking collectives, local(): facts = lax.all_to_all(facts, ('zq', 'zp'), 0, 0, tiled=True)  19 us
    pallas_call x1, Pallas kernels, correlate(): pl.pallas_call(corr_kernel, grid=(GROUPS // PIECES,), in_specs=[whole(gat...  10.7 us
    all_to_all x1, waiting for transfers between devices, local(): sums = lax.all_to_all(sums, ('xh', 'y', 'xl'), 0, 0, tiled=True)  10.7 us
    all_to_all x1, starting transfers between devices, local(): lax.all_to_all(norms, ('xh', 'core'), 0, 0, tiled=True)  8.88 us
    all_to_all x1, starting transfers between devices, local(): sums = lax.all_to_all(sums, ('xh', 'y', 'xl'), 0, 0, tiled=True)  8.31 us
    ppermute x1, waiting for transfers between devices, from_next_block(): return lax.ppermute(value, BLK, [(i + 1, i) for i in range(count - 1)])  8.21 us
    all_to_all x1, starting transfers between devices, local(): exchanged = lax.all_to_all(message, ('y', 'xl', 'zp'), 0, 0, tiled=True)  7.41 us
  transfers between devices with their start and end apart: 5, of which 3 were waited for; matrix products, arithmetic and copies ran while one was open for 2% of the time, Pallas kernels for 3%

profile of v5, /device:TPU:1, one launch (start us, length us, event | category | flops | bytes accessed | tf_op | source)
XLA Modules:
  0.0 135.4 jit_solution(7660091023447765402)
XLA Ops:
  7.3 0.7 convert_reduce_fusion.1
  8.0 1.7 %multiply_reduce_fusion = (f32[]{:T(128)}, bf16[300,128]{1,0:T(8,128)(2,1)S(1)}) fusion(bf16[300]{0:T(512)(128)(2,1)S(1)} %convert_reduce_fusion.1, bf16[1,300,256]{2,1,0:T(8,128)(2,1)} %param.10, s32[]{:T(128)S(6)} %select_n.3), kind=kLoop, calls=%fused_computation.2 | loop fusion | flops 268799 | bytes 154208 | tf_op jit(solution)/shard_map/reduce_sum | solution.py:206
  9.7 0.2 copy.23
  10.0 0.3 broadcast_in_dim.28
  10.2 0.7 broadcast_in_dim.29
  10.9 7.4 %all-to-all-start = ((bf16[16,8,640]{2,1,0:T(8,128)(2,1)}), bf16[16,8,640]{2,1,0:T(8,128)(2,1)S(1)}, u32[]{:S(2)}, u32[]{:S(2)}) async-start(bf16[16,8,640]{2,1,0:T(8,128)(2,1)} %bitcast.4), calls=%async_computation | async-start | bytes 327680 | tf_op jit(solution)/shard_map/all_to_all | solution.py:213
  18.4 0.4 tile.10
  18.8 0.2 reshape.41.weights_ref
  19.1 0.4 shard_map.82
  19.5 1.3 collective-permute-start
  20.8 8.2 %collective-permute-done.rim_ref = f32[300,256]{1,0:T(8,128)S(1)} collective-permute-done((f32[300,256]{1,0:T(8,128)S(1)}, f32[300,256]{1,0:T(8,128)S(1)}, u32[]{:S(2)}, u32[]{:S(2)}) %collective-permute-start) | collective-permute-done | bytes 307232 | tf_op jit(solution)/shard_map/ppermute | solution.py:36
  29.0 0.7 copy-done.4
  29.7 0.1 broadcast_in_dim.31
  29.8 0.1 broadcast_in_dim_reshape.4.shift_ref
  29.9 3.6 %shard_map.83 = f32[8,40,640]{2,1,0:T(8,128)S(1)} custom-call(f32[1]{0:T(128)} %bitcast.6.norm_ref, bf16[300,2560]{1,0:T(8,128)(2,1)S(1)} %copy-done, f32[300,256]{1,0:T(8,128)S(1)} %collective-permute-done.rim_ref, bf16[128,768]{1,0:T(8,128)(2,1)S(1)} %reshape.41.weights_ref, s32[300,1]{1,0:T(8,128)S(1)} %broadcast_in_dim_reshape.4.shift_ref), custom_call_target="tpu_custom_call" | custom-call | flops 419430400 | bytes 4194304 | tf_op jit(solution)/shard_map/pallas_call | solution.py:218
  33.6 22.2 %all_to_all.34.trace_ref = f32[8,40,640]{2,1,0:T(8,128)S(1)} all-to-all(f32[8,40,640]{2,1,0:T(8,128)S(1)} %shard_map.83), channel_id=1, replica_groups=mesh['xh'=2,'y'=4,'xl'=2,'zq'=8,'zp'=2,'core'=2] {'y','xl'}, dimensions={0} | all-to-all | bytes 1638400 | tf_op jit(solution)/shard_map/all_to_all | solution.py:226
  55.8 0.1 slice_reduce_fusion.2
  56.0 0.2 slice_reduce_fusion
  56.2 0.1 pad_maximum_fusion
  56.3 19.0 %all_to_all.35 = f32[16,1,128]{2,1,0:T(1,128)S(1)} all-to-all(f32[16,1,128]{2,1,0:T(1,128)S(1)} %broadcast_in_dim.33), channel_id=1, replica_groups=mesh['xh'=2,'y'=4,'xl'=2,'zq'=8,'zp'=2,'core'=2] {'zq','zp'}, dimensions={0} | all-to-all | bytes 16384 | tf_op jit(solution)/shard_map/all_to_all | solution.py:233
  75.4 0.7 reshape.43
  76.1 8.9 %all-to-all-start.3 = ((f32[4,1,32]{2,1,0:T(1,128)}), f32[4,1,32]{2,1,0:T(1,128)S(1)}, u32[]{:S(2)}, u32[]{:S(2)}) async-start(f32[4,1,32]{2,1,0:T(1,128)} %bitcast.9), calls=%async_computation.3 | async-start | bytes 4096 | tf_op jit(solution)/shard_map/all_to_all | solution.py:237
  85.0 4.7 %all-to-all-done.3 = f32[4,1,32]{2,1,0:T(1,128)S(1)} async-done(((f32[4,1,32]{2,1,0:T(1,128)}), f32[4,1,32]{2,1,0:T(1,128)S(1)}, u32[]{:S(2)}, u32[]{:S(2)}) %all-to-all-start.3) | async-done | bytes 544 | tf_op jit(solution)/shard_map/all_to_all | solution.py:237
  89.7 0.1 copy.22.root_ref
  89.8 1.3 copy-done.1
  91.1 10.7 %shard_map.84 = f32[2,2,8,32,512]{4,3,2,1,0:T(8,128)S(1)} custom-call(bf16[1024,640]{1,0:T(8,128)(2,1)S(1)} %bitcast.21, bf16[128,128]{1,0:T(8,128)(2,1)S(1)} %copy-done.3, bf16[128,128]{1,0:T(8,128)(2,1)S(1)} %copy-done.2, f32[8,40,640]{2,1,0:T(8,128)S(1)} %all_to_all.34.trace_ref, f32[40,1]{1,0:T(8,128)S(1)} %copy.22.root_ref), custom_call_target="tpu_custom_call" | custom-call | flops 6710886400 | bytes 4194304 | tf_op jit(solution)/shard_map/pallas_call | solution.py:167
  101.8 5.8 %all_to_all.36 = f32[2,2,8,32,512]{4,3,2,1,0:T(8,128)S(1)} all-to-all(f32[2,2,8,32,512]{4,3,2,1,0:T(8,128)S(1)} %shard_map.84), channel_id=1, replica_groups=mesh['xh'=2,'y'=4,'xl'=2,'zq'=8,'zp'=2,'core'=2] {'core'}, dimensions={0} | all-to-all | bytes 4194304 | tf_op jit(solution)/shard_map/all_to_all | solution.py:241
  107.6 1.1 reduce_sum.58
  108.7 8.3 %all-to-all-start.5 = ((bf16[16,32,512]{2,1,0:T(8,128)(2,1)}), bf16[16,32,512]{2,1,0:T(8,128)(2,1)S(1)}, u32[]{:S(2)}, u32[]{:S(2)}) async-start(bf16[16,32,512]{2,1,0:T(8,128)(2,1)} %bitcast.11), calls=%async_computation.5 | async-start | bytes 1048576 | tf_op jit(solution)/shard_map/all_to_all | solution.py:243
  117.0 10.7 %all-to-all-done.5 = bf16[16,32,512]{2,1,0:T(8,128)(2,1)S(1)} async-done(((bf16[16,32,512]{2,1,0:T(8,128)(2,1)}), bf16[16,32,512]{2,1,0:T(8,128)(2,1)S(1)}, u32[]{:S(2)}, u32[]{:S(2)}) %all-to-all-start.5) | async-done | bytes 524320 | tf_op jit(solution)/shard_map/all_to_all | solution.py:243
  127.7 0.1 convert_reduce_fusion
  127.8 0.7 broadcast_divide_fusion
  (31 shorter events, 0.5 us)
Async XLA Ops:
  6.5 11.8 %copy-start.6 = (bf16[60]{0:T(256)(128)(2,1)S(1)}, bf16[60]{0:T(256)(128)(2,1)}, u32[]{:S(2)}) copy-start(bf16[60]{0:T(256)(128)(2,1)} %param.9) | copy-start | bytes 364
  6.5 12.5 %copy-start = (bf16[300,2560]{1,0:T(8,128)(2,1)S(1)}, bf16[300,2560]{1,0:T(8,128)(2,1)}, u32[]{:S(2)}) copy-start(bf16[300,2560]{1,0:T(8,128)(2,1)} %raw_ref.1) | copy-start | bytes 4608004
  10.9 18.1 %all-to-all-start = ((bf16[16,8,640]{2,1,0:T(8,128)(2,1)}), bf16[16,8,640]{2,1,0:T(8,128)(2,1)S(1)}, u32[]{:S(2)}, u32[]{:S(2)}) async-start(bf16[16,8,640]{2,1,0:T(8,128)(2,1)} %bitcast.4), calls=%async_computation | async-start | bytes 327680 | tf_op jit(solution)/shard_map/all_to_all | solution.py:213
  18.3 71.4 %all-gather.2.cloned.1.call-start = ((), (), s32[]{:S(2)}) async-start(), calls=%async_computation.6 | async-start | bytes 1474560 | tf_op jit(solution)/shard_map/all_gather | solution.py:215
  18.8 10.9 %copy-start.5 = (s32[100]{0:T(128)S(1)}, s32[100]{0:T(128)}, u32[]{:S(2)}) copy-start(s32[100]{0:T(128)} %param.13) | copy-start | bytes 1204
  19.5 9.5 %collective-permute-start = (f32[300,256]{1,0:T(8,128)S(1)}, f32[300,256]{1,0:T(8,128)S(1)}, u32[]{:S(2)}, u32[]{:S(2)}) collective-permute-start(f32[300,256]{1,0:T(8,128)S(1)} %shard_map.82), channel_id=1, source_target_pairs={{2,0},{4,2},{6,4},{8,6},{10,8},{12,10},{14,12},{16,14},{18,16},{20... | collective-permute-start | bytes 921608 | tf_op jit(solution)/shard_map/ppermute | solution.py:36
  29.0 0.7 copy-start.4
  29.9 59.9 %copy-start.2 = (bf16[128,128]{1,0:T(8,128)(2,1)S(1)}, bf16[128,128]{1,0:T(8,128)(2,1)}, u32[]{:S(2)}) copy-start(bf16[128,128]{1,0:T(8,128)(2,1)} %constant.23.clone.second_ref) | copy-start | bytes 98308
  29.9 59.9 %copy-start.3 = (bf16[128,128]{1,0:T(8,128)(2,1)S(1)}, bf16[128,128]{1,0:T(8,128)(2,1)}, u32[]{:S(2)}) copy-start(bf16[128,128]{1,0:T(8,128)(2,1)} %constant.22.clone.first_ref) | copy-start | bytes 98308
  76.1 13.6 %all-to-all-start.3 = ((f32[4,1,32]{2,1,0:T(1,128)}), f32[4,1,32]{2,1,0:T(1,128)S(1)}, u32[]{:S(2)}, u32[]{:S(2)}) async-start(f32[4,1,32]{2,1,0:T(1,128)} %bitcast.9), calls=%async_computation.3 | async-start | bytes 4096 | tf_op jit(solution)/shard_map/all_to_all | solution.py:237
  89.8 1.3 copy-start.1
  108.7 19.0 %all-to-all-start.5 = ((bf16[16,32,512]{2,1,0:T(8,128)(2,1)}), bf16[16,32,512]{2,1,0:T(8,128)(2,1)S(1)}, u32[]{:S(2)}, u32[]{:S(2)}) async-start(bf16[16,32,512]{2,1,0:T(8,128)(2,1)} %bitcast.11), calls=%async_computation.5 | async-start | bytes 1048576 | tf_op jit(solution)/shard_map/all_to_all | solution.py:243
Sparse Core Ops, SparseCore 0:
  29.8 59.3 all-gather.1

commit v6 on v5

--- a/solution.py
+++ b/solution.py
@@ -19,7 +19,7 @@
 GROUP = 40
 USED = 38
 RIM = 192
-PIECES = 2
+PIECES = 4
 BLK = ("y", "xl", "zq", "zp")
 
 
@@ -48,13 +48,43 @@
     return lax.dot_general(left, right, dims, preferred_element_type=jnp.float32)
 
 
-def rim_kernel(raw_ref, weights_ref, out_ref):
+def front_kernel(
+    start_ref, template_ref, mask_ref, order_ref, raw_ref, weights_ref,
+    message_ref, rim_ref, norm_ref,
+):
     step = DECIM * LANES
-    out_ref[:, :LANES] = product(raw_ref[:, : step + LANES], weights_ref[...])
+    rim_ref[:, :LANES] = product(raw_ref[:, : step + LANES], weights_ref[...])
     later = product(raw_ref[:, step : 2 * step + LANES], weights_ref[...])
     raw = pltpu.roll(raw_ref[:, :LANES].astype(jnp.float32), RIM % LANES, 1)
     lane = lax.broadcasted_iota(jnp.int32, raw.shape, 1)
-    out_ref[:, LANES:] = jnp.where(lane < RIM % LANES, later, raw)
+    rim_ref[:, LANES:] = jnp.where(lane < RIM % LANES, later, raw)
+
+    stored = template_ref[0].astype(jnp.float32)
+    channels, width = stored.shape
+    window = pltpu.roll(stored, lax.rem(width - start_ref[0], width), 1)[:, :TLEN]
+    rest = jnp.zeros((mask_ref.shape[1] - channels, TLEN), jnp.float32)
+    panel = jnp.concatenate([window, rest], axis=0).T * mask_ref[...].astype(jnp.float32)
+    norm = jnp.sum(jnp.sum(panel * panel, axis=0, keepdims=True), axis=1, keepdims=True)
+    norm_ref[...] = jnp.broadcast_to(norm, norm_ref.shape)
+
+    mixed = jnp.dot(
+        order_ref[...], panel.astype(jnp.bfloat16), preferred_element_type=jnp.float32
+    )
+    lane = lax.broadcasted_iota(jnp.int32, (ROWS, WIDE), 1)
+    empty = jnp.zeros((ROWS, WIDE), jnp.float32)
+    messages = [empty] * GROUPS
+    for s in range(SUB):
+        row = mixed[s * ROWS : (s + 1) * ROWS]
+        row = jnp.concatenate([row, empty[:, row.shape[1] :]], axis=1)
+        place = (lane >= s * GROUP) & (lane < s * GROUP + USED)
+        for g in range(GROUPS):
+            hop = (s * GROUP - g * USED) % WIDE
+            moved = row if hop == 0 else pltpu.roll(row, hop, 1)
+            messages[g] = jnp.where(place, moved, messages[g])
+    for g in range(GROUPS):
+        message = messages[g].astype(jnp.bfloat16)
+        message_ref[2 * g] = message
+        message_ref[2 * g + 1] = message
 
 
 def trace_kernel(norm_ref, raw_ref, rim_ref, weights_ref, shift_ref, out_ref):
@@ -87,7 +117,7 @@
     rows = jnp.where(lane == WIDE - 1, power, rows)
     spare = GROUP - USED
     side = lax.broadcasted_iota(jnp.int32, (spare, WIDE), 0)
-    side = jnp.where(side == 0, norm_ref[0], 0.0)
+    side = jnp.where(side == 0, jnp.broadcast_to(norm_ref[:, :1], side.shape), 0.0)
     for g in range(GROUPS):
         first, last = g * USED, min((g + 1) * USED, channels)
         pieces = [rows[first:last]]
@@ -191,25 +221,26 @@
     lags = raw_len // DECIM
     blocks = lax.axis_size(BLK)
     weights = tap_matrix(fir_taps)
-    rim = pl.pallas_call(
-        rim_kernel,
-        in_specs=[vmem()] * 2,
-        out_specs=vmem(),
-        out_shape=jax.ShapeDtypeStruct((channels, 2 * LANES), jnp.float32),
+    order = np.zeros((TLEN, TLEN), np.float32)
+    for r in range(ROWS):
+        for s in range(SUB):
+            order[s * ROWS + r, r * SUB + s] = 1
+    message, rim, norm = pl.pallas_call(
+        front_kernel,
+        in_specs=[pl.BlockSpec(memory_space=pltpu.SMEM)] + [vmem()] * 5,
+        out_specs=[vmem()] * 3,
+        out_shape=[
+            jax.ShapeDtypeStruct((2 * GROUPS, ROWS, WIDE), jnp.bfloat16),
+            jax.ShapeDtypeStruct((channels, 2 * LANES), jnp.float32),
+            jax.ShapeDtypeStruct((1, LANES), jnp.float32),
+        ],
         compiler_params=params(32),
         cost_estimate=pl.CostEstimate(flops=128 << 20, bytes_accessed=2 << 20, transcendentals=0),
-    )(raw_traces[:, : 2 * DECIM * LANES + LANES], weights)
+    )(
+        start_offsets, templates, jnp.pad(channel_mask, ((0, 0), (0, -channels % LANES))),
+        jnp.asarray(order, jnp.bfloat16), raw_traces[:, : 2 * DECIM * LANES + LANES], weights,
+    )
     rim = from_next_block(rim)
-
-    window = lax.dynamic_slice_in_dim(templates[0], start_offsets[0], TLEN, axis=1)
-    panel = window * channel_mask[0].astype(jnp.bfloat16)[:, None]
-    norm = jnp.sum(jnp.square(panel.astype(jnp.float32)))[None]
-    padded = jnp.pad(panel, ((0, GROUPS * USED - channels), (0, 0)))
-    padded = jnp.pad(padded.reshape(GROUPS, USED, TLEN), ((0, 0), (0, GROUP - USED), (0, 0)))
-    message = padded.reshape(GROUPS, GROUP, ROWS, SUB).transpose(0, 2, 3, 1)
-    message = message.reshape(GROUPS, 1, ROWS, SUB * GROUP)
-    message = jnp.broadcast_to(message, (GROUPS, 2, ROWS, SUB * GROUP))
-    message = message.reshape(2 * GROUPS, ROWS, SUB * GROUP)
     exchanged = lax.all_to_all(message, ("y", "xl", "zp"), 0, 0, tiled=True)
     exchanged, rim = lax.optimization_barrier((exchanged, rim))
     gathered = lax.all_gather(exchanged, "zq", axis=0, tiled=True)
@@ -217,7 +248,7 @@
 
     traces = pl.pallas_call(
         trace_kernel,
-        in_specs=[pl.BlockSpec(memory_space=pltpu.SMEM)] + [vmem()] * 4,
+        in_specs=[vmem()] * 5,
         out_specs=vmem(),
         out_shape=jax.ShapeDtypeStruct((GROUPS, GROUP, WIDE), jnp.float32),
         compiler_params=params(32),

time: 136 us -> 133 us (0.978)
  other arithmetic: 4.6 us -> 2.25 us
    reduce_sum x1 -> x0, other arithmetic: 1.65 us -> none  [local(): norm = jnp.sum(jnp.square(panel.astype(jnp.float32)))[None]]
    pallas_call x1, Pallas kernels: 10.7 us -> 9.25 us  [correlate(): pl.pallas_call(corr_kernel, grid=(GROUPS // PIECES,), in_specs=[whole(gat...]
  transfers between devices with their start and end apart: 5 -> 5, of which waited for: 3 -> 3; matrix products, arithmetic and copies ran while one was open for 2% -> 1% of each run, Pallas kernels for 3% -> 2%
where the time goes in v6:
time: 133 us
  blocking collectives  48.1 us (36%)
  starting transfers between devices  25.1 us (19%)
  waiting for transfers between devices  23.5 us (18%)
  between operations  14.3 us (11%)
  Pallas kernels  13.6 us (10%)
  local copies, waits for them, and re-layouts  5.85 us (4%)
  other arithmetic  2.25 us (2%)
    all_to_all x1, blocking collectives, local(): traces = lax.all_to_all(traces, ('y', 'xl'), 0, 0, tiled=True)  22.2 us
    all_to_all x1, blocking collectives, local(): facts = lax.all_to_all(facts, ('zq', 'zp'), 0, 0, tiled=True)  19.2 us
    all_to_all x1, waiting for transfers between devices, local(): sums = lax.all_to_all(sums, ('xh', 'y', 'xl'), 0, 0, tiled=True)  10.7 us
    pallas_call x1, Pallas kernels, correlate(): pl.pallas_call(corr_kernel, grid=(GROUPS // PIECES,), in_specs=[whole(gat...  9.25 us
    all_to_all x1, starting transfers between devices, local(): lax.all_to_all(norms, ('xh', 'core'), 0, 0, tiled=True)  8.98 us
    ppermute x1, waiting for transfers between devices, from_next_block(): return lax.ppermute(value, BLK, [(i + 1, i) for i in range(count - 1)])  8.21 us
    all_to_all x1, starting transfers between devices, local(): exchanged = lax.all_to_all(message, ('y', 'xl', 'zp'), 0, 0, tiled=True)  7.4 us
    all_to_all x1, starting transfers between devices, local(): sums = lax.all_to_all(sums, ('xh', 'y', 'xl'), 0, 0, tiled=True)  7.39 us
  transfers between devices with their start and end apart: 5, of which 3 were waited for; matrix products, arithmetic and copies ran while one was open for 1% of the time, Pallas kernels for 2%

profile of v6, /device:TPU:1, one launch (start us, length us, event | category | flops | bytes accessed | tf_op | source)
XLA Modules:
  0.0 132.7 jit_solution(18064464239685439657)
XLA Ops:
  7.2 0.7 concatenate.6
  7.9 0.4 tile.10
  8.3 0.2 reshape.20.weights_ref
  8.5 1.3 %slice.18.raw_ref = bf16[300,1408]{1,0:T(8,128)(2,1)S(1)} slice(bf16[300,2560]{1,0:T(8,128)(2,1)} %raw_ref.1), slice={[0:300], [0:1408]} | slice | bytes 1689600 | tf_op jit(solution)/shard_map/slice | solution.py:241
  9.9 1.3 %shard_map.91 = (bf16[16,8,640]{2,1,0:T(8,128)(2,1)}, f32[300,256]{1,0:T(8,128)S(1)}, f32[1,128]{1,0:T(1,128)S(1)}) custom-call(s32[1]{0:T(128)S(6)} %copy.21.start_ref, bf16[1,300,256]{2,1,0:T(8,128)(2,1)S(1)} %copy-done.1, s32[1,384]{1,0:T(1,128)S(1)} %pad.5.mask_ref, bf16[128,128]{1,0:T(8,128)(2,1)S(1)} %copy-done.2, ...), custom_call_target="tpu_custom_call" | custom-call | flops 134217728 | bytes 2097152 | tf_op jit(solution)/shard_map/pallas_call | solution.py:228
  11.2 7.4 %all-to-all-start = ((bf16[16,8,640]{2,1,0:T(8,128)(2,1)}), bf16[16,8,640]{2,1,0:T(8,128)(2,1)S(1)}, u32[]{:S(2)}, u32[]{:S(2)}) async-start(bf16[16,8,640]{2,1,0:T(8,128)(2,1)} %get-tuple-element.12), calls=%async_computation | async-start | bytes 327680 | tf_op jit(solution)/shard_map/all_to_all | solution.py:244
  18.6 0.0 all-gather.2.cloned.1.call-start
  18.7 1.3 collective-permute-start
  20.0 8.2 %collective-permute-done.rim_ref = f32[300,256]{1,0:T(8,128)S(1)} collective-permute-done((f32[300,256]{1,0:T(8,128)S(1)}, f32[300,256]{1,0:T(8,128)S(1)}, u32[]{:S(2)}, u32[]{:S(2)}) %collective-permute-start) | collective-permute-done | bytes 307232 | tf_op jit(solution)/shard_map/ppermute | solution.py:36
  28.2 0.7 copy-done.6
  28.9 0.1 broadcast_in_dim.8
  29.0 0.1 broadcast_in_dim_reshape.4.shift_ref
  29.2 3.0 %shard_map.92 = f32[8,40,640]{2,1,0:T(8,128)S(1)} custom-call(f32[1,128]{1,0:T(1,128)S(1)} %get-tuple-element.15.norm_ref, bf16[300,2560]{1,0:T(8,128)(2,1)S(1)} %copy-done, f32[300,256]{1,0:T(8,128)S(1)} %collective-permute-done.rim_ref, bf16[128,768]{1,0:T(8,128)(2,1)S(1)} %reshape.20.weights_ref, s32[300,1]{1,0:T(8,128)S(1)} %broadcast_in_dim_reshape.4.shift_ref), custom_call_target="tpu_custom_call" | custom-call | flops 419430400 | bytes 4194304 | tf_op jit(solution)/shard_map/pallas_call | solution.py:249
  32.2 22.2 %all_to_all.34.trace_ref = f32[8,40,640]{2,1,0:T(8,128)S(1)} all-to-all(f32[8,40,640]{2,1,0:T(8,128)S(1)} %shard_map.92), channel_id=1, replica_groups=mesh['xh'=2,'y'=4,'xl'=2,'zq'=8,'zp'=2,'core'=2] {'y','xl'}, dimensions={0} | all-to-all | bytes 1638400 | tf_op jit(solution)/shard_map/all_to_all | solution.py:257
  54.4 0.1 slice_reduce_fusion.2
  54.5 0.2 slice_reduce_fusion
  54.8 0.1 pad_maximum_fusion
  54.8 19.2 %all_to_all.35 = f32[16,1,128]{2,1,0:T(1,128)S(1)} all-to-all(f32[16,1,128]{2,1,0:T(1,128)S(1)} %broadcast_in_dim.19), channel_id=1, replica_groups=mesh['xh'=2,'y'=4,'xl'=2,'zq'=8,'zp'=2,'core'=2] {'zq','zp'}, dimensions={0} | all-to-all | bytes 16384 | tf_op jit(solution)/shard_map/all_to_all | solution.py:264
  74.0 0.1 slice_bitcast_fusion
  74.1 0.1 copy.18
  74.2 0.7 reshape.22
  74.8 9.0 %all-to-all-start.3 = ((f32[4,1,32]{2,1,0:T(1,128)}), f32[4,1,32]{2,1,0:T(1,128)S(1)}, u32[]{:S(2)}, u32[]{:S(2)}) async-start(f32[4,1,32]{2,1,0:T(1,128)} %bitcast.3), calls=%async_computation.3 | async-start | bytes 4096 | tf_op jit(solution)/shard_map/all_to_all | solution.py:268
  83.8 4.6 %all-to-all-done.3 = f32[4,1,32]{2,1,0:T(1,128)S(1)} async-done(((f32[4,1,32]{2,1,0:T(1,128)}), f32[4,1,32]{2,1,0:T(1,128)S(1)}, u32[]{:S(2)}, u32[]{:S(2)}) %all-to-all-start.3) | async-done | bytes 544 | tf_op jit(solution)/shard_map/all_to_all | solution.py:268
  88.5 0.1 copy.20.root_ref
  88.6 1.3 copy-done.3
  89.9 9.3 %shard_map.93 = f32[2,2,8,32,512]{4,3,2,1,0:T(8,128)S(1)} custom-call(bf16[1024,640]{1,0:T(8,128)(2,1)S(1)} %bitcast.7, bf16[128,128]{1,0:T(8,128)(2,1)S(1)} %copy-done.5, bf16[128,128]{1,0:T(8,128)(2,1)S(1)} %copy-done.4, f32[8,40,640]{2,1,0:T(8,128)S(1)} %all_to_all.34.trace_ref, f32[40,1]{1,0:T(8,128)S(1)} %copy.20.root_ref), custom_call_target="tpu_custom_call" | custom-call | flops 6710886400 | bytes 4194304 | tf_op jit(solution)/shard_map/pallas_call | solution.py:197
  99.2 6.7 %all_to_all.36 = f32[2,2,8,32,512]{4,3,2,1,0:T(8,128)S(1)} all-to-all(f32[2,2,8,32,512]{4,3,2,1,0:T(8,128)S(1)} %shard_map.93), channel_id=1, replica_groups=mesh['xh'=2,'y'=4,'xl'=2,'zq'=8,'zp'=2,'core'=2] {'core'}, dimensions={0} | all-to-all | bytes 4194304 | tf_op jit(solution)/shard_map/all_to_all | solution.py:272
  105.9 1.1 reduce_sum.48
  107.0 7.4 %all-to-all-start.5 = ((bf16[16,32,512]{2,1,0:T(8,128)(2,1)}), bf16[16,32,512]{2,1,0:T(8,128)(2,1)S(1)}, u32[]{:S(2)}, u32[]{:S(2)}) async-start(bf16[16,32,512]{2,1,0:T(8,128)(2,1)} %bitcast.5), calls=%async_computation.5 | async-start | bytes 1048576 | tf_op jit(solution)/shard_map/all_to_all | solution.py:274
  114.4 10.7 %all-to-all-done.5 = bf16[16,32,512]{2,1,0:T(8,128)(2,1)S(1)} async-done(((bf16[16,32,512]{2,1,0:T(8,128)(2,1)}), bf16[16,32,512]{2,1,0:T(8,128)(2,1)S(1)}, u32[]{:S(2)}, u32[]{:S(2)}) %all-to-all-start.5) | async-done | bytes 524320 | tf_op jit(solution)/shard_map/all_to_all | solution.py:274
  125.1 0.1 convert_reduce_fusion
  125.2 0.7 broadcast_divide_fusion
  (28 shorter events, 0.2 us)
Async XLA Ops:
  6.5 3.4 %copy-start.2 = (bf16[128,128]{1,0:T(8,128)(2,1)S(1)}, bf16[128,128]{1,0:T(8,128)(2,1)}, u32[]{:S(2)}) copy-start(bf16[128,128]{1,0:T(8,128)(2,1)} %constant.20.clone.order_ref) | copy-start | bytes 98308
  6.5 3.3 %copy-start.7 = (s32[1,300]{1,0:T(1,128)S(1)}, s32[1,300]{1,0:T(1,128)}, u32[]{:S(2)}) copy-start(s32[1,300]{1,0:T(1,128)} %param.13) | copy-start | bytes 3604
  6.5 3.4 %copy-start.1 = (bf16[1,300,256]{2,1,0:T(8,128)(2,1)S(1)}, bf16[1,300,256]{2,1,0:T(8,128)(2,1)}, u32[]{:S(2)}) copy-start(bf16[1,300,256]{2,1,0:T(8,128)(2,1)} %template_ref.1) | copy-start | bytes 460804
  8.3 20.6 %copy-start.8 = (s32[100]{0:T(128)S(1)}, s32[100]{0:T(128)}, u32[]{:S(2)}) copy-start(s32[100]{0:T(128)} %param.14) | copy-start | bytes 1204
  8.3 20.8 %copy-start = (bf16[300,2560]{1,0:T(8,128)(2,1)S(1)}, bf16[300,2560]{1,0:T(8,128)(2,1)}, u32[]{:S(2)}) copy-start(bf16[300,2560]{1,0:T(8,128)(2,1)} %raw_ref.1) | copy-start | bytes 4608004
  11.2 17.0 %all-to-all-start = ((bf16[16,8,640]{2,1,0:T(8,128)(2,1)}), bf16[16,8,640]{2,1,0:T(8,128)(2,1)S(1)}, u32[]{:S(2)}, u32[]{:S(2)}) async-start(bf16[16,8,640]{2,1,0:T(8,128)(2,1)} %get-tuple-element.12), calls=%async_computation | async-start | bytes 327680 | tf_op jit(solution)/shard_map/all_to_all | solution.py:244
  18.6 69.9 %all-gather.2.cloned.1.call-start = ((), (), s32[]{:S(2)}) async-start(), calls=%async_computation.6 | async-start | bytes 1474560 | tf_op jit(solution)/shard_map/all_gather | solution.py:246
  18.7 9.5 %collective-permute-start = (f32[300,256]{1,0:T(8,128)S(1)}, f32[300,256]{1,0:T(8,128)S(1)}, u32[]{:S(2)}, u32[]{:S(2)}) collective-permute-start(f32[300,256]{1,0:T(8,128)S(1)} %get-tuple-element.13), channel_id=1, source_target_pairs={{2,0},{4,2},{6,4},{8,6},{10,8},{12,10},{14,12},{16,14},{18,16},{20... | collective-permute-start | bytes 921608 | tf_op jit(solution)/shard_map/ppermute | solution.py:36
  28.2 0.7 copy-start.6
  29.1 59.4 %copy-start.4 = (bf16[128,128]{1,0:T(8,128)(2,1)S(1)}, bf16[128,128]{1,0:T(8,128)(2,1)}, u32[]{:S(2)}) copy-start(bf16[128,128]{1,0:T(8,128)(2,1)} %constant.22.clone.second_ref) | copy-start | bytes 98308
  29.1 59.4 %copy-start.5 = (bf16[128,128]{1,0:T(8,128)(2,1)S(1)}, bf16[128,128]{1,0:T(8,128)(2,1)}, u32[]{:S(2)}) copy-start(bf16[128,128]{1,0:T(8,128)(2,1)} %constant.21.clone.first_ref) | copy-start | bytes 98308
  74.8 13.6 %all-to-all-start.3 = ((f32[4,1,32]{2,1,0:T(1,128)}), f32[4,1,32]{2,1,0:T(1,128)S(1)}, u32[]{:S(2)}, u32[]{:S(2)}) async-start(f32[4,1,32]{2,1,0:T(1,128)} %bitcast.3), calls=%async_computation.3 | async-start | bytes 4096 | tf_op jit(solution)/shard_map/all_to_all | solution.py:268
  88.6 1.3 copy-start.3
  107.0 18.1 %all-to-all-start.5 = ((bf16[16,32,512]{2,1,0:T(8,128)(2,1)}), bf16[16,32,512]{2,1,0:T(8,128)(2,1)S(1)}, u32[]{:S(2)}, u32[]{:S(2)}) async-start(bf16[16,32,512]{2,1,0:T(8,128)(2,1)} %bitcast.5), calls=%async_computation.5 | async-start | bytes 1048576 | tf_op jit(solution)/shard_map/all_to_all | solution.py:274
Sparse Core Ops, SparseCore 0:
  29.0 58.8 all-gather.1

commit v7 on v6

--- a/solution.py
+++ b/solution.py
@@ -36,23 +36,21 @@
     return lax.ppermute(value, BLK, [(i + 1, i) for i in range(count - 1)])
 
 
-def tap_matrix(fir_taps):
-    depth = DECIM * LANES + LANES
-    pattern = jnp.concatenate([fir_taps, jnp.zeros((depth + DECIM - NTAP,), fir_taps.dtype)])
-    flat = jnp.tile(pattern, LANES)[: LANES * depth]
-    return flat.reshape(LANES, depth)
-
-
 def product(left, right):
     dims = (((1,), (1,)), ((), ()))
     return lax.dot_general(left, right, dims, preferred_element_type=jnp.float32)
 
 
 def front_kernel(
-    start_ref, template_ref, mask_ref, order_ref, raw_ref, weights_ref,
-    message_ref, rim_ref, norm_ref,
+    start_ref, taps_ref, template_ref, mask_ref, order_ref, raw_ref,
+    message_ref, rim_ref, norm_ref, weights_ref,
 ):
     step = DECIM * LANES
+    taps = jnp.broadcast_to(taps_ref[...].astype(jnp.float32), (8, LANES))
+    taps = pltpu.roll(taps, 0, 1, stride=DECIM, stride_axis=0)
+    taps = jnp.concatenate([taps, jnp.zeros((8, step), jnp.float32)], axis=1)
+    tiles = [taps] + [pltpu.roll(taps, 8 * DECIM * i, 1) for i in range(1, LANES // 8)]
+    weights_ref[...] = jnp.concatenate(tiles, axis=0).astype(jnp.bfloat16)
     rim_ref[:, :LANES] = product(raw_ref[:, : step + LANES], weights_ref[...])
     later = product(raw_ref[:, step : 2 * step + LANES], weights_ref[...])
     raw = pltpu.roll(raw_ref[:, :LANES].astype(jnp.float32), RIM % LANES, 1)
@@ -220,26 +218,40 @@
     channels, raw_len = raw_traces.shape
     lags = raw_len // DECIM
     blocks = lax.axis_size(BLK)
-    weights = tap_matrix(fir_taps)
     order = np.zeros((TLEN, TLEN), np.float32)
     for r in range(ROWS):
         for s in range(SUB):
             order[s * ROWS + r, r * SUB + s] = 1
-    message, rim, norm = pl.pallas_call(
+    depth = DECIM * LANES + LANES
+    taps = jnp.pad(fir_taps, (0, LANES - NTAP))[None]
+    mask = jnp.pad(channel_mask, ((0, 0), (0, -channels % LANES)))
+    near = (channels, 2 * DECIM * LANES + LANES)
+    message, rim, norm, weights = pl.pallas_call(
         front_kernel,
-        in_specs=[pl.BlockSpec(memory_space=pltpu.SMEM)] + [vmem()] * 5,
-        out_specs=[vmem()] * 3,
+        grid=(1,),
+        in_specs=[
+            pl.BlockSpec(memory_space=pltpu.SMEM),
+            whole(taps.shape),
+            whole(templates.shape),
+            whole(mask.shape),
+            whole(order.shape),
+            whole(near),
+        ],
+        out_specs=[
+            whole((2 * GROUPS, ROWS, WIDE)),
+            whole((channels, 2 * LANES)),
+            whole((1, LANES)),
+            whole((LANES, depth)),
+        ],
         out_shape=[
             jax.ShapeDtypeStruct((2 * GROUPS, ROWS, WIDE), jnp.bfloat16),
             jax.ShapeDtypeStruct((channels, 2 * LANES), jnp.float32),
             jax.ShapeDtypeStruct((1, LANES), jnp.float32),
+            jax.ShapeDtypeStruct((LANES, depth), jnp.bfloat16),
         ],
         compiler_params=params(32),
         cost_estimate=pl.CostEstimate(flops=128 << 20, bytes_accessed=2 << 20, transcendentals=0),
-    )(
-        start_offsets, templates, jnp.pad(channel_mask, ((0, 0), (0, -channels % LANES))),
-        jnp.asarray(order, jnp.bfloat16), raw_traces[:, : 2 * DECIM * LANES + LANES], weights,
-    )
+    )(start_offsets, taps, templates, mask, jnp.asarray(order, jnp.bfloat16), raw_traces)
     rim = from_next_block(rim)
     exchanged = lax.all_to_all(message, ("y", "xl", "zp"), 0, 0, tiled=True)
     exchanged, rim = lax.optimization_barrier((exchanged, rim))

time: 133 us -> 136 us (1.023)
  local copies, waits for them, and re-layouts: 5.85 us -> 7.66 us
  starting transfers between devices: 25.1 us -> 26.5 us
    unnamed x18, local copies, waits for them, and re-layouts: 2.03 us -> 5.09 us
    all_to_all x1, starting transfers between devices: 7.39 us -> 8.86 us  [local(): sums = lax.all_to_all(sums, ('xh', 'y', 'xl'), 0, 0, tiled=True)]
where the time goes in v7:
time: 136 us; the launch traced here: 135 us
  blocking collectives  47.3 us (35%)
  starting transfers between devices  26.5 us (19%)
  waiting for transfers between devices  23.8 us (18%)
  between operations  14.2 us (10%)
  Pallas kernels  13.7 us (10%)
  local copies, waits for them, and re-layouts  7.66 us (6%)
  other arithmetic  2.25 us (2%)
    all_to_all x1, blocking collectives, local(): traces = lax.all_to_all(traces, ('y', 'xl'), 0, 0, tiled=True)  22.2 us
    all_to_all x1, blocking collectives, local(): facts = lax.all_to_all(facts, ('zq', 'zp'), 0, 0, tiled=True)  19.2 us
    all_to_all x1, waiting for transfers between devices, local(): sums = lax.all_to_all(sums, ('xh', 'y', 'xl'), 0, 0, tiled=True)  10.7 us
    pallas_call x1, Pallas kernels, correlate(): pl.pallas_call(corr_kernel, grid=(GROUPS // PIECES,), in_specs=[whole(gat...  9.25 us
    all_to_all x1, starting transfers between devices, local(): lax.all_to_all(norms, ('xh', 'core'), 0, 0, tiled=True)  8.88 us
    all_to_all x1, starting transfers between devices, local(): sums = lax.all_to_all(sums, ('xh', 'y', 'xl'), 0, 0, tiled=True)  8.86 us
    ppermute x1, waiting for transfers between devices, from_next_block(): return lax.ppermute(value, BLK, [(i + 1, i) for i in range(count - 1)])  8.21 us
    all_to_all x1, starting transfers between devices, local(): exchanged = lax.all_to_all(message, ('y', 'xl', 'zp'), 0, 0, tiled=True)  7.41 us
  transfers between devices with their start and end apart: 5, of which 3 were waited for; matrix products, arithmetic and copies ran while one was open for 1% of the time, Pallas kernels for 2%

profile of v7, /device:TPU:1, one launch (start us, length us, event | category | flops | bytes accessed | tf_op | source)
XLA Modules:
  0.0 135.4 jit_solution(9773847261619701507)
XLA Ops:
  7.2 0.7 pad_bitcast_fusion.taps_ref
  7.9 0.7 pad.9.mask_ref
  8.6 1.4 %copy-done = bf16[300,2560]{1,0:T(8,128)(2,1)S(1)} copy-done((bf16[300,2560]{1,0:T(8,128)(2,1)S(1)}, bf16[300,2560]{1,0:T(8,128)(2,1)}, u32[]{:S(2)}) %copy-start) | copy-done | bytes 1536024
  10.0 0.9 copy-done.2
  10.9 0.8 copy-done.3
  11.6 1.5 %shard_map.91 = (bf16[16,8,640]{2,1,0:T(8,128)(2,1)}, f32[300,256]{1,0:T(8,128)S(1)}, f32[1,128]{1,0:T(1,128)S(1)}, bf16[128,768]{1,0:T(8,128)(2,1)S(1)}) custom-call(s32[1]{0:T(128)S(6)} %copy.21.start_ref, bf16[1,128]{1,0:T(2,128)(2,1)S(1)} %pad_bitcast_fusion.taps_ref, bf16[1,300,256]{2,1,0:T(8,128)(2,1)S(1)} %copy-done.2, s32[1,384]{1,0:T(1,128)S(1)} %pad.9.mask_ref, ...), custom_call_target="tpu_custom_call" | custom-call | flops 134217728 | bytes 2097152 | tf_op jit(solution)/shard_map/pallas_call | solution.py:229
  13.1 7.4 %all-to-all-start = ((bf16[16,8,640]{2,1,0:T(8,128)(2,1)}), bf16[16,8,640]{2,1,0:T(8,128)(2,1)S(1)}, u32[]{:S(2)}, u32[]{:S(2)}) async-start(bf16[16,8,640]{2,1,0:T(8,128)(2,1)} %get-tuple-element.13), calls=%async_computation | async-start | bytes 327680 | tf_op jit(solution)/shard_map/all_to_all | solution.py:256
  20.6 1.3 collective-permute-start
  21.9 8.2 %collective-permute-done.rim_ref = f32[300,256]{1,0:T(8,128)S(1)} collective-permute-done((f32[300,256]{1,0:T(8,128)S(1)}, f32[300,256]{1,0:T(8,128)S(1)}, u32[]{:S(2)}, u32[]{:S(2)}) %collective-permute-start) | collective-permute-done | bytes 307232 | tf_op jit(solution)/shard_map/ppermute | solution.py:36
  30.1 0.7 copy-done.7
  30.8 0.1 broadcast_in_dim.20
  30.9 0.1 broadcast_in_dim_reshape.4.shift_ref
  31.0 3.0 %shard_map.92 = f32[8,40,640]{2,1,0:T(8,128)S(1)} custom-call(f32[1,128]{1,0:T(1,128)S(1)} %get-tuple-element.16.norm_ref, bf16[300,2560]{1,0:T(8,128)(2,1)S(1)} %copy-done.1, f32[300,256]{1,0:T(8,128)S(1)} %collective-permute-done.rim_ref, bf16[128,768]{1,0:T(8,128)(2,1)S(1)} %get-tuple-element.18.weights_ref, s32[300,1]{1,0:T(8,128)S(1)} %broadcast_in_dim_reshape.4.shift_ref), custom_call_target="tpu_custom_call" | custom-call | flops 419430400 | bytes 4194304 | tf_op jit(solution)/shard_map/pallas_call | solution.py:261
  34.0 22.2 %all_to_all.34.trace_ref = f32[8,40,640]{2,1,0:T(8,128)S(1)} all-to-all(f32[8,40,640]{2,1,0:T(8,128)S(1)} %shard_map.92), channel_id=1, replica_groups=mesh['xh'=2,'y'=4,'xl'=2,'zq'=8,'zp'=2,'core'=2] {'y','xl'}, dimensions={0} | all-to-all | bytes 1638400 | tf_op jit(solution)/shard_map/all_to_all | solution.py:269
  56.3 0.1 slice_reduce_fusion.2
  56.4 0.2 slice_reduce_fusion
  56.6 0.1 pad_maximum_fusion
  56.7 19.2 %all_to_all.35 = f32[16,1,128]{2,1,0:T(1,128)S(1)} all-to-all(f32[16,1,128]{2,1,0:T(1,128)S(1)} %broadcast_in_dim.22), channel_id=1, replica_groups=mesh['xh'=2,'y'=4,'xl'=2,'zq'=8,'zp'=2,'core'=2] {'zq','zp'}, dimensions={0} | all-to-all | bytes 16384 | tf_op jit(solution)/shard_map/all_to_all | solution.py:276
  75.9 0.1 slice_bitcast_fusion
  76.0 0.1 copy.18
  76.0 0.7 reshape.17
  76.7 8.9 %all-to-all-start.3 = ((f32[4,1,32]{2,1,0:T(1,128)}), f32[4,1,32]{2,1,0:T(1,128)S(1)}, u32[]{:S(2)}, u32[]{:S(2)}) async-start(f32[4,1,32]{2,1,0:T(1,128)} %bitcast.4), calls=%async_computation.3 | async-start | bytes 4096 | tf_op jit(solution)/shard_map/all_to_all | solution.py:280
  85.6 4.9 %all-to-all-done.3 = f32[4,1,32]{2,1,0:T(1,128)S(1)} async-done(((f32[4,1,32]{2,1,0:T(1,128)}), f32[4,1,32]{2,1,0:T(1,128)S(1)}, u32[]{:S(2)}, u32[]{:S(2)}) %all-to-all-start.3) | async-done | bytes 544 | tf_op jit(solution)/shard_map/all_to_all | solution.py:280
  90.5 0.1 copy.20.root_ref
  90.6 1.3 copy-done.4
  91.9 9.3 %shard_map.93 = f32[2,2,8,32,512]{4,3,2,1,0:T(8,128)S(1)} custom-call(bf16[1024,640]{1,0:T(8,128)(2,1)S(1)} %bitcast.9, bf16[128,128]{1,0:T(8,128)(2,1)S(1)} %copy-done.6, bf16[128,128]{1,0:T(8,128)(2,1)S(1)} %copy-done.5, f32[8,40,640]{2,1,0:T(8,128)S(1)} %all_to_all.34.trace_ref, f32[40,1]{1,0:T(8,128)S(1)} %copy.20.root_ref), custom_call_target="tpu_custom_call" | custom-call | flops 6710886400 | bytes 4194304 | tf_op jit(solution)/shard_map/pallas_call | solution.py:195
  101.2 5.9 %all_to_all.36 = f32[2,2,8,32,512]{4,3,2,1,0:T(8,128)S(1)} all-to-all(f32[2,2,8,32,512]{4,3,2,1,0:T(8,128)S(1)} %shard_map.93), channel_id=1, replica_groups=mesh['xh'=2,'y'=4,'xl'=2,'zq'=8,'zp'=2,'core'=2] {'core'}, dimensions={0} | all-to-all | bytes 4194304 | tf_op jit(solution)/shard_map/all_to_all | solution.py:284
  107.1 1.1 reduce_sum.48
  108.2 8.9 %all-to-all-start.5 = ((bf16[16,32,512]{2,1,0:T(8,128)(2,1)}), bf16[16,32,512]{2,1,0:T(8,128)(2,1)S(1)}, u32[]{:S(2)}, u32[]{:S(2)}) async-start(bf16[16,32,512]{2,1,0:T(8,128)(2,1)} %bitcast.6), calls=%async_computation.5 | async-start | bytes 1048576 | tf_op jit(solution)/shard_map/all_to_all | solution.py:286
  117.1 10.7 %all-to-all-done.5 = bf16[16,32,512]{2,1,0:T(8,128)(2,1)S(1)} async-done(((bf16[16,32,512]{2,1,0:T(8,128)(2,1)}), bf16[16,32,512]{2,1,0:T(8,128)(2,1)S(1)}, u32[]{:S(2)}, u32[]{:S(2)}) %all-to-all-start.5) | async-done | bytes 524320 | tf_op jit(solution)/shard_map/all_to_all | solution.py:286
  127.8 0.1 convert_reduce_fusion
  127.9 0.7 broadcast_divide_fusion
  (23 shorter events, 0.2 us)
Async XLA Ops:
  6.5 24.2 %copy-start.8 = (s32[100]{0:T(128)S(1)}, s32[100]{0:T(128)}, u32[]{:S(2)}) copy-start(s32[100]{0:T(128)} %param.14) | copy-start | bytes 1204
  8.5 1.4 %copy-start = (bf16[300,2560]{1,0:T(8,128)(2,1)S(1)}, bf16[300,2560]{1,0:T(8,128)(2,1)}, u32[]{:S(2)}) copy-start(bf16[300,2560]{1,0:T(8,128)(2,1)} %raw_ref.3) | copy-start | bytes 4608004
  10.0 0.9 copy-start.2
  10.9 0.8 copy-start.3
  11.6 19.4 %copy-start.1 = (bf16[300,2560]{1,0:T(8,128)(2,1)S(1)}, bf16[300,2560]{1,0:T(8,128)(2,1)}, u32[]{:S(2)}) copy-start(bf16[300,2560]{1,0:T(8,128)(2,1)} %raw_ref.3) | copy-start | bytes 4608004
  13.1 17.0 %all-to-all-start = ((bf16[16,8,640]{2,1,0:T(8,128)(2,1)}), bf16[16,8,640]{2,1,0:T(8,128)(2,1)S(1)}, u32[]{:S(2)}, u32[]{:S(2)}) async-start(bf16[16,8,640]{2,1,0:T(8,128)(2,1)} %get-tuple-element.13), calls=%async_computation | async-start | bytes 327680 | tf_op jit(solution)/shard_map/all_to_all | solution.py:256
  20.5 70.1 %all-gather.2.cloned.1.call-start = ((), (), s32[]{:S(2)}) async-start(), calls=%async_computation.6 | async-start | bytes 1474560 | tf_op jit(solution)/shard_map/all_gather | solution.py:258
  20.6 9.5 %collective-permute-start = (f32[300,256]{1,0:T(8,128)S(1)}, f32[300,256]{1,0:T(8,128)S(1)}, u32[]{:S(2)}, u32[]{:S(2)}) collective-permute-start(f32[300,256]{1,0:T(8,128)S(1)} %get-tuple-element.14), channel_id=1, source_target_pairs={{2,0},{4,2},{6,4},{8,6},{10,8},{12,10},{14,12},{16,14},{18,16},{20... | collective-permute-start | bytes 921608 | tf_op jit(solution)/shard_map/ppermute | solution.py:36
  30.1 0.7 copy-start.7
  31.0 59.6 %copy-start.5 = (bf16[128,128]{1,0:T(8,128)(2,1)S(1)}, bf16[128,128]{1,0:T(8,128)(2,1)}, u32[]{:S(2)}) copy-start(bf16[128,128]{1,0:T(8,128)(2,1)} %constant.22.clone.second_ref) | copy-start | bytes 98308
  31.0 59.6 %copy-start.6 = (bf16[128,128]{1,0:T(8,128)(2,1)S(1)}, bf16[128,128]{1,0:T(8,128)(2,1)}, u32[]{:S(2)}) copy-start(bf16[128,128]{1,0:T(8,128)(2,1)} %constant.21.clone.first_ref) | copy-start | bytes 98308
  76.7 13.8 %all-to-all-start.3 = ((f32[4,1,32]{2,1,0:T(1,128)}), f32[4,1,32]{2,1,0:T(1,128)S(1)}, u32[]{:S(2)}, u32[]{:S(2)}) async-start(f32[4,1,32]{2,1,0:T(1,128)} %bitcast.4), calls=%async_computation.3 | async-start | bytes 4096 | tf_op jit(solution)/shard_map/all_to_all | solution.py:280
  90.6 1.3 copy-start.4
  108.2 19.6 %all-to-all-start.5 = ((bf16[16,32,512]{2,1,0:T(8,128)(2,1)}), bf16[16,32,512]{2,1,0:T(8,128)(2,1)S(1)}, u32[]{:S(2)}, u32[]{:S(2)}) async-start(bf16[16,32,512]{2,1,0:T(8,128)(2,1)} %bitcast.6), calls=%async_computation.5 | async-start | bytes 1048576 | tf_op jit(solution)/shard_map/all_to_all | solution.py:286
Sparse Core Ops, SparseCore 0:
  30.9 59.3 all-gather.1

commit v8 on v6

--- a/solution.py
+++ b/solution.py
@@ -166,7 +166,7 @@
         for c in range(2):
             for x in range(2):
                 g = c * 2 + x
-                out_ref[c, x, t] = total[g * 32 : (g + 1) * 32, :]
+                out_ref[c, x, t] = total[g * 32 : (g + 1) * 32, :].astype(jnp.bfloat16)
 
 
 def orders():
@@ -205,7 +205,7 @@
             whole(root_power.shape),
         ],
         out_specs=pl.BlockSpec((2, 2, PIECES, 32, lags), lambda i: (0, 0, i, 0, 0)),
-        out_shape=jax.ShapeDtypeStruct((2, 2, GROUPS, 32, lags), jnp.float32),
+        out_shape=jax.ShapeDtypeStruct((2, 2, GROUPS, 32, lags), jnp.bfloat16),
         scratch_shapes=[
             pltpu.VMEM((ROWS, LANES, WIDE), jnp.bfloat16),
             pltpu.VMEM((ROWS // PAIR * LANES, depth), jnp.bfloat16),
@@ -269,9 +269,8 @@
     root_power, norms = lax.optimization_barrier((root_power, norms))
 
     sums = correlate(gathered, traces, root_power[:, None], lags)
-    sums = jnp.sum(lax.all_to_all(sums, "core", 0, 0, tiled=True), axis=0)
-    sums = sums.astype(jnp.bfloat16).reshape(2 * GROUPS, 32, lags)
-    sums = lax.all_to_all(sums, ("xh", "y", "xl"), 0, 0, tiled=True)
+    sums = sums.reshape(4 * GROUPS, 32, lags)
+    sums = lax.all_to_all(sums, ("core", "xh", "y", "xl"), 0, 0, tiled=True)
     sums = jnp.sum(sums.astype(jnp.float32), axis=0)
     return sums / jnp.sqrt(norms + 1e-05)[:, None]
 

time: 133 us -> 135 us (1.015)
  waiting for transfers between devices: 23.5 us -> 30.4 us
  blocking collectives: 48.1 us -> 41.4 us
  starting transfers between devices: 25.1 us -> 27.2 us
    all_to_all x1 -> x0, blocking collectives: 6.72 us -> none  [local(): sums = jnp.sum(lax.all_to_all(sums, 'core', 0, 0, tiled=True), axis=0)]
    all_to_all x1, waiting for transfers between devices: 10.7 us -> 17.3 us  [local(): sums = lax.all_to_all(sums, ('core', 'xh', 'y', 'xl'), 0, 0, tiled=True)]
    all_to_all x1, starting transfers between devices: 7.39 us -> 9.57 us  [local(): sums = lax.all_to_all(sums, ('core', 'xh', 'y', 'xl'), 0, 0, tiled=True)]
where the time goes in v8:
time: 135 us
  blocking collectives  41.4 us (31%)
  waiting for transfers between devices  30.4 us (23%)
  starting transfers between devices  27.2 us (20%)
  Pallas kernels  14.3 us (11%)
  between operations  14.2 us (11%)
  local copies, waits for them, and re-layouts  5.85 us (4%)
    all_to_all x1, blocking collectives, local(): traces = lax.all_to_all(traces, ('y', 'xl'), 0, 0, tiled=True)  22.2 us
    all_to_all x1, blocking collectives, local(): facts = lax.all_to_all(facts, ('zq', 'zp'), 0, 0, tiled=True)  19.2 us
    all_to_all x1, waiting for transfers between devices, local(): sums = lax.all_to_all(sums, ('core', 'xh', 'y', 'xl'), 0, 0, tiled=True)  17.3 us
    pallas_call x1, Pallas kernels, correlate(): pl.pallas_call(corr_kernel, grid=(GROUPS // PIECES,), in_specs=[whole(gat...  9.96 us
    all_to_all x1, starting transfers between devices, local(): sums = lax.all_to_all(sums, ('core', 'xh', 'y', 'xl'), 0, 0, tiled=True)  9.57 us
    all_to_all x1, starting transfers between devices, local(): lax.all_to_all(norms, ('xh', 'core'), 0, 0, tiled=True)  8.85 us
    ppermute x1, waiting for transfers between devices, from_next_block(): return lax.ppermute(value, BLK, [(i + 1, i) for i in range(count - 1)])  8.22 us
    all_to_all x1, starting transfers between devices, local(): exchanged = lax.all_to_all(message, ('y', 'xl', 'zp'), 0, 0, tiled=True)  7.4 us
  transfers between devices with their start and end apart: 5, of which 3 were waited for; matrix products, arithmetic and copies ran while one was open for 1% of the time, Pallas kernels for 2%

profile of v8, /device:TPU:1, one launch (start us, length us, event | category | flops | bytes accessed | tf_op | source)
XLA Modules:
  0.0 134.6 jit_solution(15440950544398122215)
XLA Ops:
  7.2 0.7 concatenate.6
  7.9 0.4 tile.10
  8.3 0.2 reshape.20.weights_ref
  8.5 1.3 slice.18.raw_ref
  9.9 1.3 shard_map.91
  11.2 7.4 %all-to-all-start = ((bf16[16,8,640]{2,1,0:T(8,128)(2,1)}), bf16[16,8,640]{2,1,0:T(8,128)(2,1)S(1)}, u32[]{:S(2)}, u32[]{:S(2)}) async-start(bf16[16,8,640]{2,1,0:T(8,128)(2,1)} %get-tuple-element.12), calls=%async_computation | async-start | bytes 327680 | tf_op jit(solution)/shard_map/all_to_all | solution.py:244
  18.6 0.0 all-gather.2.cloned.1.call-start
  18.7 1.3 collective-permute-start
  20.0 8.2 %collective-permute-done.rim_ref = f32[300,256]{1,0:T(8,128)S(1)} collective-permute-done((f32[300,256]{1,0:T(8,128)S(1)}, f32[300,256]{1,0:T(8,128)S(1)}, u32[]{:S(2)}, u32[]{:S(2)}) %collective-permute-start) | collective-permute-done | bytes 307232 | tf_op jit(solution)/shard_map/ppermute | solution.py:36
  28.2 0.7 copy-done.6
  28.9 0.0 all-gather.2.cloned.1.call-update
  28.9 0.1 broadcast_in_dim.8
  29.0 0.1 broadcast_in_dim_reshape.4.shift_ref
  29.1 3.0 %shard_map.92 = f32[8,40,640]{2,1,0:T(8,128)S(1)} custom-call(f32[1,128]{1,0:T(1,128)S(1)} %get-tuple-element.15.norm_ref, bf16[300,2560]{1,0:T(8,128)(2,1)S(1)} %copy-done, f32[300,256]{1,0:T(8,128)S(1)} %collective-permute-done.rim_ref, bf16[128,768]{1,0:T(8,128)(2,1)S(1)} %reshape.20.weights_ref, s32[300,1]{1,0:T(8,128)S(1)} %broadcast_in_dim_reshape.4.shift_ref), custom_call_target="tpu_custom_call" | custom-call | flops 419430400 | bytes 4194304 | tf_op jit(solution)/shard_map/pallas_call | solution.py:249
  32.1 0.0 copy-start.5
  32.1 22.2 %all_to_all.29.trace_ref = f32[8,40,640]{2,1,0:T(8,128)S(1)} all-to-all(f32[8,40,640]{2,1,0:T(8,128)S(1)} %shard_map.92), channel_id=1, replica_groups=mesh['xh'=2,'y'=4,'xl'=2,'zq'=8,'zp'=2,'core'=2] {'y','xl'}, dimensions={0} | all-to-all | bytes 1638400 | tf_op jit(solution)/shard_map/all_to_all | solution.py:257
  54.4 0.1 slice_reduce_fusion.2
  54.5 0.2 slice_reduce_fusion
  54.7 0.1 pad_maximum_fusion
  54.8 19.2 %all_to_all.30 = f32[16,1,128]{2,1,0:T(1,128)S(1)} all-to-all(f32[16,1,128]{2,1,0:T(1,128)S(1)} %broadcast_in_dim.19), channel_id=1, replica_groups=mesh['xh'=2,'y'=4,'xl'=2,'zq'=8,'zp'=2,'core'=2] {'zq','zp'}, dimensions={0} | all-to-all | bytes 16384 | tf_op jit(solution)/shard_map/all_to_all | solution.py:264
  74.0 0.1 slice_bitcast_fusion
  74.1 0.1 copy.14
  74.2 0.7 reshape.22
  74.8 8.9 %all-to-all-start.3 = ((f32[4,1,32]{2,1,0:T(1,128)}), f32[4,1,32]{2,1,0:T(1,128)S(1)}, u32[]{:S(2)}, u32[]{:S(2)}) async-start(f32[4,1,32]{2,1,0:T(1,128)} %bitcast.3), calls=%async_computation.3 | async-start | bytes 4096 | tf_op jit(solution)/shard_map/all_to_all | solution.py:268
  83.7 4.9 %all-to-all-done.3 = f32[4,1,32]{2,1,0:T(1,128)S(1)} async-done(((f32[4,1,32]{2,1,0:T(1,128)}), f32[4,1,32]{2,1,0:T(1,128)S(1)}, u32[]{:S(2)}, u32[]{:S(2)}) %all-to-all-start.3) | async-done | bytes 544 | tf_op jit(solution)/shard_map/all_to_all | solution.py:268
  88.6 0.1 copy.16.root_ref
  88.7 1.3 copy-done.3
  90.0 10.0 %shard_map.93 = bf16[2,2,8,32,512]{4,3,2,1,0:T(8,128)(2,1)} custom-call(bf16[1024,640]{1,0:T(8,128)(2,1)S(1)} %bitcast.7, bf16[128,128]{1,0:T(8,128)(2,1)S(1)} %copy-done.5, bf16[128,128]{1,0:T(8,128)(2,1)S(1)} %copy-done.4, f32[8,40,640]{2,1,0:T(8,128)S(1)} %all_to_all.29.trace_ref, f32[40,1]{1,0:T(8,128)S(1)} %copy.16.root_ref), custom_call_target="tpu_custom_call" | custom-call | flops 6710886400 | bytes 4194304 | tf_op jit(solution)/shard_map/pallas_call | solution.py:197
  100.0 9.6 %all-to-all-start.4 = ((bf16[32,32,512]{2,1,0:T(8,128)(2,1)}), bf16[32,32,512]{2,1,0:T(8,128)(2,1)S(1)}, u32[]{:S(2)}, u32[]{:S(2)}) async-start(bf16[32,32,512]{2,1,0:T(8,128)(2,1)} %bitcast.5), calls=%async_computation.4 | async-start | bytes 2097152 | tf_op jit(solution)/shard_map/all_to_all | solution.py:273
  109.5 17.3 %all-to-all-done.4 = bf16[32,32,512]{2,1,0:T(8,128)(2,1)S(1)} async-done(((bf16[32,32,512]{2,1,0:T(8,128)(2,1)}), bf16[32,32,512]{2,1,0:T(8,128)(2,1)S(1)}, u32[]{:S(2)}, u32[]{:S(2)}) %all-to-all-start.4) | async-done | bytes 1048608 | tf_op jit(solution)/shard_map/all_to_all | solution.py:273
  126.9 0.2 convert_reduce_fusion
  127.0 0.7 broadcast_divide_fusion
  (26 shorter events, 0.2 us)
Async XLA Ops:
  7.8 2.0 %copy-start.7 = (s32[1,300]{1,0:T(1,128)S(1)}, s32[1,300]{1,0:T(1,128)}, u32[]{:S(2)}) copy-start(s32[1,300]{1,0:T(1,128)} %param.13) | copy-start | bytes 3604
  7.9 2.0 %copy-start.1 = (bf16[1,300,256]{2,1,0:T(8,128)(2,1)S(1)}, bf16[1,300,256]{2,1,0:T(8,128)(2,1)}, u32[]{:S(2)}) copy-start(bf16[1,300,256]{2,1,0:T(8,128)(2,1)} %template_ref.1) | copy-start | bytes 460804
  7.9 2.0 %copy-start.2 = (bf16[128,128]{1,0:T(8,128)(2,1)S(1)}, bf16[128,128]{1,0:T(8,128)(2,1)}, u32[]{:S(2)}) copy-start(bf16[128,128]{1,0:T(8,128)(2,1)} %constant.20.clone.order_ref) | copy-start | bytes 98308
  8.5 20.4 %copy-start.8 = (s32[100]{0:T(128)S(1)}, s32[100]{0:T(128)}, u32[]{:S(2)}) copy-start(s32[100]{0:T(128)} %param.14) | copy-start | bytes 1204
  8.5 20.6 %copy-start = (bf16[300,2560]{1,0:T(8,128)(2,1)S(1)}, bf16[300,2560]{1,0:T(8,128)(2,1)}, u32[]{:S(2)}) copy-start(bf16[300,2560]{1,0:T(8,128)(2,1)} %raw_ref.1) | copy-start | bytes 4608004
  11.2 17.0 %all-to-all-start = ((bf16[16,8,640]{2,1,0:T(8,128)(2,1)}), bf16[16,8,640]{2,1,0:T(8,128)(2,1)S(1)}, u32[]{:S(2)}, u32[]{:S(2)}) async-start(bf16[16,8,640]{2,1,0:T(8,128)(2,1)} %get-tuple-element.12), calls=%async_computation | async-start | bytes 327680 | tf_op jit(solution)/shard_map/all_to_all | solution.py:244
  18.6 70.0 %all-gather.2.cloned.1.call-start = ((), (), s32[]{:S(2)}) async-start(), calls=%async_computation.5 | async-start | bytes 1474560 | tf_op jit(solution)/shard_map/all_gather | solution.py:246
  18.7 9.5 %collective-permute-start = (f32[300,256]{1,0:T(8,128)S(1)}, f32[300,256]{1,0:T(8,128)S(1)}, u32[]{:S(2)}, u32[]{:S(2)}) collective-permute-start(f32[300,256]{1,0:T(8,128)S(1)} %get-tuple-element.13), channel_id=1, source_target_pairs={{2,0},{4,2},{6,4},{8,6},{10,8},{12,10},{14,12},{16,14},{18,16},{20... | collective-permute-start | bytes 921608 | tf_op jit(solution)/shard_map/ppermute | solution.py:36
  28.2 0.7 copy-start.6
  32.1 56.6 %copy-start.4 = (bf16[128,128]{1,0:T(8,128)(2,1)S(1)}, bf16[128,128]{1,0:T(8,128)(2,1)}, u32[]{:S(2)}) copy-start(bf16[128,128]{1,0:T(8,128)(2,1)} %constant.22.clone.second_ref) | copy-start | bytes 98308
  32.1 56.5 %copy-start.5 = (bf16[128,128]{1,0:T(8,128)(2,1)S(1)}, bf16[128,128]{1,0:T(8,128)(2,1)}, u32[]{:S(2)}) copy-start(bf16[128,128]{1,0:T(8,128)(2,1)} %constant.21.clone.first_ref) | copy-start | bytes 98308
  74.8 13.7 %all-to-all-start.3 = ((f32[4,1,32]{2,1,0:T(1,128)}), f32[4,1,32]{2,1,0:T(1,128)S(1)}, u32[]{:S(2)}, u32[]{:S(2)}) async-start(f32[4,1,32]{2,1,0:T(1,128)} %bitcast.3), calls=%async_computation.3 | async-start | bytes 4096 | tf_op jit(solution)/shard_map/all_to_all | solution.py:268
  88.7 1.3 copy-start.3
  100.0 26.9 %all-to-all-start.4 = ((bf16[32,32,512]{2,1,0:T(8,128)(2,1)}), bf16[32,32,512]{2,1,0:T(8,128)(2,1)S(1)}, u32[]{:S(2)}, u32[]{:S(2)}) async-start(bf16[32,32,512]{2,1,0:T(8,128)(2,1)} %bitcast.5), calls=%async_computation.4 | async-start | bytes 2097152 | tf_op jit(solution)/shard_map/all_to_all | solution.py:273
Sparse Core Ops, SparseCore 0:
  29.0 59.3 all-gather.1

commit v9 on v7

--- a/solution.py
+++ b/solution.py
@@ -60,8 +60,11 @@
     stored = template_ref[0].astype(jnp.float32)
     channels, width = stored.shape
     window = pltpu.roll(stored, lax.rem(width - start_ref[0], width), 1)[:, :TLEN]
-    rest = jnp.zeros((mask_ref.shape[1] - channels, TLEN), jnp.float32)
-    panel = jnp.concatenate([window, rest], axis=0).T * mask_ref[...].astype(jnp.float32)
+    spare = -channels % LANES
+    window = jnp.concatenate([window, jnp.zeros((spare, TLEN), jnp.float32)], axis=0)
+    mask = mask_ref[...].astype(jnp.float32)
+    mask = jnp.concatenate([mask, jnp.zeros((1, spare), jnp.float32)], axis=1)
+    panel = window.T * mask
     norm = jnp.sum(jnp.sum(panel * panel, axis=0, keepdims=True), axis=1, keepdims=True)
     norm_ref[...] = jnp.broadcast_to(norm, norm_ref.shape)
 
@@ -224,7 +227,6 @@
             order[s * ROWS + r, r * SUB + s] = 1
     depth = DECIM * LANES + LANES
     taps = jnp.pad(fir_taps, (0, LANES - NTAP))[None]
-    mask = jnp.pad(channel_mask, ((0, 0), (0, -channels % LANES)))
     near = (channels, 2 * DECIM * LANES + LANES)
     message, rim, norm, weights = pl.pallas_call(
         front_kernel,
@@ -233,7 +235,7 @@
             pl.BlockSpec(memory_space=pltpu.SMEM),
             whole(taps.shape),
             whole(templates.shape),
-            whole(mask.shape),
+            whole(channel_mask.shape),
             whole(order.shape),
             whole(near),
         ],
@@ -249,9 +251,9 @@
             jax.ShapeDtypeStruct((1, LANES), jnp.float32),
             jax.ShapeDtypeStruct((LANES, depth), jnp.bfloat16),
         ],
-        compiler_params=params(32),
+        compiler_params=params(63),
         cost_estimate=pl.CostEstimate(flops=128 << 20, bytes_accessed=2 << 20, transcendentals=0),
-    )(start_offsets, taps, templates, mask, jnp.asarray(order, jnp.bfloat16), raw_traces)
+    )(start_offsets, taps, templates, channel_mask, jnp.asarray(order, jnp.bfloat16), raw_traces)
     rim = from_next_block(rim)
     exchanged = lax.all_to_all(message, ("y", "xl", "zp"), 0, 0, tiled=True)
     exchanged, rim = lax.optimization_barrier((exchanged, rim))

time: 136 us -> 133 us (0.978)
  starting transfers between devices: 26.5 us -> 23.3 us
  Pallas kernels: 13.7 us -> 15.1 us
    all_to_all x1, starting transfers between devices: 8.86 us -> 5.63 us  [local(): sums = lax.all_to_all(sums, ('xh', 'y', 'xl'), 0, 0, tiled=True)]
    pallas_call x1, Pallas kernels: 1.46 us -> 2.87 us  [local(): pl.pallas_call(front_kernel, grid=(1,), in_specs=[pl.BlockSpec(memory_spa...]
    unnamed x18 -> x16, local copies, waits for them, and re-layouts: 5.09 us -> 4.92 us
where the time goes in v9:
time: 133 us
  blocking collectives  46.9 us (35%)
  waiting for transfers between devices  23.6 us (18%)
  starting transfers between devices  23.3 us (18%)
  Pallas kernels  15.1 us (11%)
  between operations  14.2 us (11%)
  local copies, waits for them, and re-layouts  7.32 us (6%)
  other arithmetic  2.24 us (2%)
    all_to_all x1, blocking collectives, local(): traces = lax.all_to_all(traces, ('y', 'xl'), 0, 0, tiled=True)  22.5 us
    all_to_all x1, blocking collectives, local(): facts = lax.all_to_all(facts, ('zq', 'zp'), 0, 0, tiled=True)  18.7 us
    all_to_all x1, waiting for transfers between devices, local(): sums = lax.all_to_all(sums, ('xh', 'y', 'xl'), 0, 0, tiled=True)  10.7 us
    pallas_call x1, Pallas kernels, correlate(): pl.pallas_call(corr_kernel, grid=(GROUPS // PIECES,), in_specs=[whole(gat...  9.23 us
    all_to_all x1, starting transfers between devices, local(): lax.all_to_all(norms, ('xh', 'core'), 0, 0, tiled=True)  8.88 us
    ppermute x1, waiting for transfers between devices, from_next_block(): return lax.ppermute(value, BLK, [(i + 1, i) for i in range(count - 1)])  8.42 us
    all_to_all x1, starting transfers between devices, local(): exchanged = lax.all_to_all(message, ('y', 'xl', 'zp'), 0, 0, tiled=True)  7.41 us
    all_to_all x1, blocking collectives, local(): sums = jnp.sum(lax.all_to_all(sums, 'core', 0, 0, tiled=True), axis=0)  5.74 us
  transfers between devices with their start and end apart: 5, of which 3 were waited for; matrix products, arithmetic and copies ran while one was open for 1% of the time, Pallas kernels for 2%

profile of v9, /device:TPU:1, one launch (start us, length us, event | category | flops | bytes accessed | tf_op | source)
XLA Modules:
  0.0 132.6 jit_solution(5235919007909239143)
XLA Ops:
  7.2 1.2 pad_bitcast_fusion.taps_ref
  8.4 2.9 %shard_map.91 = (bf16[16,8,640]{2,1,0:T(8,128)(2,1)}, f32[300,256]{1,0:T(8,128)}, f32[1,128]{1,0:T(1,128)}, bf16[128,768]{1,0:T(8,128)(2,1)}) custom-call(s32[1]{0:T(128)S(6)} %copy.21.start_ref, bf16[1,128]{1,0:T(2,128)(2,1)} %pad_bitcast_fusion.taps_ref, bf16[1,300,256]{2,1,0:T(8,128)(2,1)} %template_ref.1, s32[1,300]{1,0:T(1,128)} %mask_ref.1, ...), custom_call_target="tpu_custom_call" | custom-call | flops 134217728 | bytes 2097152 | tf_op jit(solution)/shard_map/pallas_call | solution.py:231
  11.2 7.4 %all-to-all-start = ((bf16[16,8,640]{2,1,0:T(8,128)(2,1)}), bf16[16,8,640]{2,1,0:T(8,128)(2,1)S(1)}, u32[]{:S(2)}, u32[]{:S(2)}) async-start(bf16[16,8,640]{2,1,0:T(8,128)(2,1)} %get-tuple-element.13), calls=%async_computation | async-start | bytes 327680 | tf_op jit(solution)/shard_map/all_to_all | solution.py:258
  18.7 0.0 all-gather.2.cloned.1.call-start
  18.7 1.3 collective-permute-start
  20.0 8.4 %collective-permute-done.rim_ref = f32[300,256]{1,0:T(8,128)S(1)} collective-permute-done((f32[300,256]{1,0:T(8,128)}, f32[300,256]{1,0:T(8,128)S(1)}, u32[]{:S(2)}, u32[]{:S(2)}) %collective-permute-start) | collective-permute-done | bytes 307232 | tf_op jit(solution)/shard_map/ppermute | solution.py:36
  28.4 0.7 copy-done.6
  29.1 0.1 broadcast_in_dim.20
  29.2 0.1 broadcast_in_dim_reshape.4.shift_ref
  29.3 1.4 %copy-done = bf16[300,2560]{1,0:T(8,128)(2,1)S(1)} copy-done((bf16[300,2560]{1,0:T(8,128)(2,1)S(1)}, bf16[300,2560]{1,0:T(8,128)(2,1)}, u32[]{:S(2)}) %copy-start) | copy-done | bytes 1536024
  30.7 0.9 copy-done.1
  31.7 0.6 copy-done.2
  32.3 3.0 %shard_map.92 = f32[8,40,640]{2,1,0:T(8,128)S(1)} custom-call(f32[1,128]{1,0:T(1,128)S(1)} %copy-done.2, bf16[300,2560]{1,0:T(8,128)(2,1)S(1)} %copy-done, f32[300,256]{1,0:T(8,128)S(1)} %collective-permute-done.rim_ref, bf16[128,768]{1,0:T(8,128)(2,1)S(1)} %copy-done.1, s32[300,1]{1,0:T(8,128)S(1)} %broadcast_in_dim_reshape.4.shift_ref), custom_call_target="tpu_custom_call" | custom-call | flops 419430400 | bytes 4194304 | tf_op jit(solution)/shard_map/pallas_call | solution.py:263
  35.3 22.5 %all_to_all.34.trace_ref = f32[8,40,640]{2,1,0:T(8,128)S(1)} all-to-all(f32[8,40,640]{2,1,0:T(8,128)S(1)} %shard_map.92), channel_id=1, replica_groups=mesh['xh'=2,'y'=4,'xl'=2,'zq'=8,'zp'=2,'core'=2] {'y','xl'}, dimensions={0} | all-to-all | bytes 1638400 | tf_op jit(solution)/shard_map/all_to_all | solution.py:271
  57.8 0.1 slice_reduce_fusion.2
  57.9 0.2 slice_reduce_fusion
  58.1 0.1 pad_maximum_fusion
  58.2 18.7 %all_to_all.35 = f32[16,1,128]{2,1,0:T(1,128)S(1)} all-to-all(f32[16,1,128]{2,1,0:T(1,128)S(1)} %broadcast_in_dim.22), channel_id=1, replica_groups=mesh['xh'=2,'y'=4,'xl'=2,'zq'=8,'zp'=2,'core'=2] {'zq','zp'}, dimensions={0} | all-to-all | bytes 16384 | tf_op jit(solution)/shard_map/all_to_all | solution.py:278
  76.9 0.1 slice_bitcast_fusion
  77.0 0.1 copy.18
  77.0 0.7 reshape.17
  77.7 8.9 %all-to-all-start.3 = ((f32[4,1,32]{2,1,0:T(1,128)}), f32[4,1,32]{2,1,0:T(1,128)S(1)}, u32[]{:S(2)}, u32[]{:S(2)}) async-start(f32[4,1,32]{2,1,0:T(1,128)} %bitcast.4), calls=%async_computation.3 | async-start | bytes 4096 | tf_op jit(solution)/shard_map/all_to_all | solution.py:282
  86.6 4.5 %all-to-all-done.3 = f32[4,1,32]{2,1,0:T(1,128)S(1)} async-done(((f32[4,1,32]{2,1,0:T(1,128)}), f32[4,1,32]{2,1,0:T(1,128)S(1)}, u32[]{:S(2)}, u32[]{:S(2)}) %all-to-all-start.3) | async-done | bytes 544 | tf_op jit(solution)/shard_map/all_to_all | solution.py:282
  91.1 0.1 copy.20.root_ref
  91.2 1.3 copy-done.3
  92.5 9.2 %shard_map.93 = f32[2,2,8,32,512]{4,3,2,1,0:T(8,128)S(1)} custom-call(bf16[1024,640]{1,0:T(8,128)(2,1)S(1)} %bitcast.9, bf16[128,128]{1,0:T(8,128)(2,1)S(1)} %copy-done.5, bf16[128,128]{1,0:T(8,128)(2,1)S(1)} %copy-done.4, f32[8,40,640]{2,1,0:T(8,128)S(1)} %all_to_all.34.trace_ref, f32[40,1]{1,0:T(8,128)S(1)} %copy.20.root_ref), custom_call_target="tpu_custom_call" | custom-call | flops 6710886400 | bytes 4194304 | tf_op jit(solution)/shard_map/pallas_call | solution.py:198
  101.7 5.7 %all_to_all.36 = f32[2,2,8,32,512]{4,3,2,1,0:T(8,128)S(1)} all-to-all(f32[2,2,8,32,512]{4,3,2,1,0:T(8,128)S(1)} %shard_map.93), channel_id=1, replica_groups=mesh['xh'=2,'y'=4,'xl'=2,'zq'=8,'zp'=2,'core'=2] {'core'}, dimensions={0} | all-to-all | bytes 4194304 | tf_op jit(solution)/shard_map/all_to_all | solution.py:286
  107.5 1.1 reduce_sum.48
  108.6 5.6 %all-to-all-start.5 = ((bf16[16,32,512]{2,1,0:T(8,128)(2,1)}), bf16[16,32,512]{2,1,0:T(8,128)(2,1)S(1)}, u32[]{:S(2)}, u32[]{:S(2)}) async-start(bf16[16,32,512]{2,1,0:T(8,128)(2,1)} %bitcast.6), calls=%async_computation.5 | async-start | bytes 1048576 | tf_op jit(solution)/shard_map/all_to_all | solution.py:288
  114.2 10.7 %all-to-all-done.5 = bf16[16,32,512]{2,1,0:T(8,128)(2,1)S(1)} async-done(((bf16[16,32,512]{2,1,0:T(8,128)(2,1)}), bf16[16,32,512]{2,1,0:T(8,128)(2,1)S(1)}, u32[]{:S(2)}, u32[]{:S(2)}) %all-to-all-start.5) | async-done | bytes 524320 | tf_op jit(solution)/shard_map/all_to_all | solution.py:288
  124.9 0.1 convert_reduce_fusion
  125.0 0.7 broadcast_divide_fusion
  (20 shorter events, 0.1 us)
Async XLA Ops:
  6.5 22.6 %copy-start.7 = (s32[100]{0:T(128)S(1)}, s32[100]{0:T(128)}, u32[]{:S(2)}) copy-start(s32[100]{0:T(128)} %param.14) | copy-start | bytes 1204
  11.2 17.2 %all-to-all-start = ((bf16[16,8,640]{2,1,0:T(8,128)(2,1)}), bf16[16,8,640]{2,1,0:T(8,128)(2,1)S(1)}, u32[]{:S(2)}, u32[]{:S(2)}) async-start(bf16[16,8,640]{2,1,0:T(8,128)(2,1)} %get-tuple-element.13), calls=%async_computation | async-start | bytes 327680 | tf_op jit(solution)/shard_map/all_to_all | solution.py:258
  18.7 72.5 %all-gather.2.cloned.1.call-start = ((), (), s32[]{:S(2)}) async-start(), calls=%async_computation.6 | async-start | bytes 1474560 | tf_op jit(solution)/shard_map/all_gather | solution.py:260
  18.7 9.7 %collective-permute-start = (f32[300,256]{1,0:T(8,128)}, f32[300,256]{1,0:T(8,128)S(1)}, u32[]{:S(2)}, u32[]{:S(2)}) collective-permute-start(f32[300,256]{1,0:T(8,128)} %get-tuple-element.14), channel_id=1, source_target_pairs={{2,0},{4,2},{6,4},{8,6},{10,8},{12,10},{14,12},{16,14},{18,16},{20... | collective-permute-start | bytes 921608 | tf_op jit(solution)/shard_map/ppermute | solution.py:36
  28.4 0.7 copy-start.6
  29.3 1.4 %copy-start = (bf16[300,2560]{1,0:T(8,128)(2,1)S(1)}, bf16[300,2560]{1,0:T(8,128)(2,1)}, u32[]{:S(2)}) copy-start(bf16[300,2560]{1,0:T(8,128)(2,1)} %raw_ref.3) | copy-start | bytes 4608004
  30.7 0.9 copy-start.1
  31.6 0.6 copy-start.2
  32.3 58.9 %copy-start.4 = (bf16[128,128]{1,0:T(8,128)(2,1)S(1)}, bf16[128,128]{1,0:T(8,128)(2,1)}, u32[]{:S(2)}) copy-start(bf16[128,128]{1,0:T(8,128)(2,1)} %constant.21.clone.second_ref) | copy-start | bytes 98308
  32.3 58.9 %copy-start.5 = (bf16[128,128]{1,0:T(8,128)(2,1)S(1)}, bf16[128,128]{1,0:T(8,128)(2,1)}, u32[]{:S(2)}) copy-start(bf16[128,128]{1,0:T(8,128)(2,1)} %constant.20.clone.first_ref) | copy-start | bytes 98308
  77.7 13.4 %all-to-all-start.3 = ((f32[4,1,32]{2,1,0:T(1,128)}), f32[4,1,32]{2,1,0:T(1,128)S(1)}, u32[]{:S(2)}, u32[]{:S(2)}) async-start(f32[4,1,32]{2,1,0:T(1,128)} %bitcast.4), calls=%async_computation.3 | async-start | bytes 4096 | tf_op jit(solution)/shard_map/all_to_all | solution.py:282
  91.2 1.3 copy-start.3
  108.6 16.4 %all-to-all-start.5 = ((bf16[16,32,512]{2,1,0:T(8,128)(2,1)}), bf16[16,32,512]{2,1,0:T(8,128)(2,1)S(1)}, u32[]{:S(2)}, u32[]{:S(2)}) async-start(bf16[16,32,512]{2,1,0:T(8,128)(2,1)} %bitcast.6), calls=%async_computation.5 | async-start | bytes 1048576 | tf_op jit(solution)/shard_map/all_to_all | solution.py:288
Sparse Core Ops, SparseCore 0:
  29.2 59.1 all-gather.1

commit v10 on v9

--- a/solution.py
+++ b/solution.py
@@ -46,7 +46,8 @@
     message_ref, rim_ref, norm_ref, weights_ref,
 ):
     step = DECIM * LANES
-    taps = jnp.broadcast_to(taps_ref[...].astype(jnp.float32), (8, LANES))
+    taps = jnp.broadcast_to(taps_ref[...].astype(jnp.float32), (8, NTAP))
+    taps = jnp.concatenate([taps, jnp.zeros((8, LANES - NTAP), jnp.float32)], axis=1)
     taps = pltpu.roll(taps, 0, 1, stride=DECIM, stride_axis=0)
     taps = jnp.concatenate([taps, jnp.zeros((8, step), jnp.float32)], axis=1)
     tiles = [taps] + [pltpu.roll(taps, 8 * DECIM * i, 1) for i in range(1, LANES // 8)]
@@ -226,7 +227,7 @@
         for s in range(SUB):
             order[s * ROWS + r, r * SUB + s] = 1
     depth = DECIM * LANES + LANES
-    taps = jnp.pad(fir_taps, (0, LANES - NTAP))[None]
+    taps = fir_taps[None]
     near = (channels, 2 * DECIM * LANES + LANES)
     message, rim, norm, weights = pl.pallas_call(
         front_kernel,

time: 133 us -> 132 us (level)
  no operation moved by 1% of the time
where the time goes in v10:
time: 132 us; the launch traced here: 131 us
  blocking collectives  46.9 us (36%)
  waiting for transfers between devices  23.6 us (18%)
  starting transfers between devices  23.1 us (18%)
  Pallas kernels  15.1 us (11%)
  between operations  14.2 us (11%)
  local copies, waits for them, and re-layouts  6.18 us (5%)
  other arithmetic  2.24 us (2%)
    all_to_all x1, blocking collectives, local(): traces = lax.all_to_all(traces, ('y', 'xl'), 0, 0, tiled=True)  22.5 us
    all_to_all x1, blocking collectives, local(): facts = lax.all_to_all(facts, ('zq', 'zp'), 0, 0, tiled=True)  18.7 us
    all_to_all x1, waiting for transfers between devices, local(): sums = lax.all_to_all(sums, ('xh', 'y', 'xl'), 0, 0, tiled=True)  10.7 us
    pallas_call x1, Pallas kernels, correlate(): pl.pallas_call(corr_kernel, grid=(GROUPS // PIECES,), in_specs=[whole(gat...  9.24 us
    all_to_all x1, starting transfers between devices, local(): lax.all_to_all(norms, ('xh', 'core'), 0, 0, tiled=True)  9.02 us
    ppermute x1, waiting for transfers between devices, from_next_block(): return lax.ppermute(value, BLK, [(i + 1, i) for i in range(count - 1)])  8.42 us
    all_to_all x1, starting transfers between devices, local(): exchanged = lax.all_to_all(message, ('y', 'xl', 'zp'), 0, 0, tiled=True)  7.41 us
    all_to_all x1, blocking collectives, local(): sums = jnp.sum(lax.all_to_all(sums, 'core', 0, 0, tiled=True), axis=0)  5.75 us
  transfers between devices with their start and end apart: 5, of which 3 were waited for; matrix products, arithmetic and copies ran while one was open for 1% of the time, Pallas kernels for 2%

profile of v10, /device:TPU:1, one launch (start us, length us, event | category | flops | bytes accessed | tf_op | source)
XLA Modules:
  0.0 131.3 jit_solution(1525521643581414325)
XLA Ops:
  7.2 2.9 %shard_map.91 = (bf16[16,8,640]{2,1,0:T(8,128)(2,1)}, f32[300,256]{1,0:T(8,128)}, f32[1,128]{1,0:T(1,128)}, bf16[128,768]{1,0:T(8,128)(2,1)}) custom-call(s32[1]{0:T(128)S(6)} %copy.21.start_ref, bf16[1,60]{1,0:T(2,128)(2,1)} %bitcast.11, bf16[1,300,256]{2,1,0:T(8,128)(2,1)} %template_ref.1, s32[1,300]{1,0:T(1,128)} %mask_ref.1, ...), custom_call_target="tpu_custom_call" | custom-call | flops 134217728 | bytes 2097152 | tf_op jit(solution)/shard_map/pallas_call | solution.py:232
  10.1 7.4 %all-to-all-start = ((bf16[16,8,640]{2,1,0:T(8,128)(2,1)}), bf16[16,8,640]{2,1,0:T(8,128)(2,1)S(1)}, u32[]{:S(2)}, u32[]{:S(2)}) async-start(bf16[16,8,640]{2,1,0:T(8,128)(2,1)} %get-tuple-element.13), calls=%async_computation | async-start | bytes 327680 | tf_op jit(solution)/shard_map/all_to_all | solution.py:259
  17.5 0.0 all-gather.2.cloned.1.call-start
  17.5 1.3 collective-permute-start
  18.8 8.4 %collective-permute-done.rim_ref = f32[300,256]{1,0:T(8,128)S(1)} collective-permute-done((f32[300,256]{1,0:T(8,128)}, f32[300,256]{1,0:T(8,128)S(1)}, u32[]{:S(2)}, u32[]{:S(2)}) %collective-permute-start) | collective-permute-done | bytes 307232 | tf_op jit(solution)/shard_map/ppermute | solution.py:36
  27.3 0.7 copy-done.6
  27.9 0.0 all-gather.2.cloned.1.call-update
  27.9 0.1 broadcast_in_dim.20
  28.0 0.1 broadcast_in_dim_reshape.4.shift_ref
  28.1 1.4 %copy-done = bf16[300,2560]{1,0:T(8,128)(2,1)S(1)} copy-done((bf16[300,2560]{1,0:T(8,128)(2,1)S(1)}, bf16[300,2560]{1,0:T(8,128)(2,1)}, u32[]{:S(2)}) %copy-start) | copy-done | bytes 1536024
  29.5 0.9 copy-done.1
  30.5 0.7 copy-done.2
  31.1 3.0 %shard_map.92 = f32[8,40,640]{2,1,0:T(8,128)S(1)} custom-call(f32[1,128]{1,0:T(1,128)S(1)} %copy-done.2, bf16[300,2560]{1,0:T(8,128)(2,1)S(1)} %copy-done, f32[300,256]{1,0:T(8,128)S(1)} %collective-permute-done.rim_ref, bf16[128,768]{1,0:T(8,128)(2,1)S(1)} %copy-done.1, s32[300,1]{1,0:T(8,128)S(1)} %broadcast_in_dim_reshape.4.shift_ref), custom_call_target="tpu_custom_call" | custom-call | flops 419430400 | bytes 4194304 | tf_op jit(solution)/shard_map/pallas_call | solution.py:264
  34.1 22.5 %all_to_all.34.trace_ref = f32[8,40,640]{2,1,0:T(8,128)S(1)} all-to-all(f32[8,40,640]{2,1,0:T(8,128)S(1)} %shard_map.92), channel_id=1, replica_groups=mesh['xh'=2,'y'=4,'xl'=2,'zq'=8,'zp'=2,'core'=2] {'y','xl'}, dimensions={0} | all-to-all | bytes 1638400 | tf_op jit(solution)/shard_map/all_to_all | solution.py:272
  56.6 0.1 slice_reduce_fusion.2
  56.7 0.2 slice_reduce_fusion
  57.0 0.1 pad_maximum_fusion
  57.1 18.7 %all_to_all.35 = f32[16,1,128]{2,1,0:T(1,128)S(1)} all-to-all(f32[16,1,128]{2,1,0:T(1,128)S(1)} %broadcast_in_dim.22), channel_id=1, replica_groups=mesh['xh'=2,'y'=4,'xl'=2,'zq'=8,'zp'=2,'core'=2] {'zq','zp'}, dimensions={0} | all-to-all | bytes 16384 | tf_op jit(solution)/shard_map/all_to_all | solution.py:279
  75.7 0.1 slice_bitcast_fusion
  75.8 0.1 copy.18
  75.9 0.7 reshape.17
  76.5 9.0 %all-to-all-start.3 = ((f32[4,1,32]{2,1,0:T(1,128)}), f32[4,1,32]{2,1,0:T(1,128)S(1)}, u32[]{:S(2)}, u32[]{:S(2)}) async-start(f32[4,1,32]{2,1,0:T(1,128)} %bitcast.4), calls=%async_computation.3 | async-start | bytes 4096 | tf_op jit(solution)/shard_map/all_to_all | solution.py:283
  85.6 4.5 %all-to-all-done.3 = f32[4,1,32]{2,1,0:T(1,128)S(1)} async-done(((f32[4,1,32]{2,1,0:T(1,128)}), f32[4,1,32]{2,1,0:T(1,128)S(1)}, u32[]{:S(2)}, u32[]{:S(2)}) %all-to-all-start.3) | async-done | bytes 544 | tf_op jit(solution)/shard_map/all_to_all | solution.py:283
  90.0 0.1 copy.20.root_ref
  90.2 1.3 copy-done.3
  91.5 9.2 %shard_map.93 = f32[2,2,8,32,512]{4,3,2,1,0:T(8,128)S(1)} custom-call(bf16[1024,640]{1,0:T(8,128)(2,1)S(1)} %bitcast.8, bf16[128,128]{1,0:T(8,128)(2,1)S(1)} %copy-done.5, bf16[128,128]{1,0:T(8,128)(2,1)S(1)} %copy-done.4, f32[8,40,640]{2,1,0:T(8,128)S(1)} %all_to_all.34.trace_ref, f32[40,1]{1,0:T(8,128)S(1)} %copy.20.root_ref), custom_call_target="tpu_custom_call" | custom-call | flops 6710886400 | bytes 4194304 | tf_op jit(solution)/shard_map/pallas_call | solution.py:199
  100.7 5.7 %all_to_all.36 = f32[2,2,8,32,512]{4,3,2,1,0:T(8,128)S(1)} all-to-all(f32[2,2,8,32,512]{4,3,2,1,0:T(8,128)S(1)} %shard_map.93), channel_id=1, replica_groups=mesh['xh'=2,'y'=4,'xl'=2,'zq'=8,'zp'=2,'core'=2] {'core'}, dimensions={0} | all-to-all | bytes 4194304 | tf_op jit(solution)/shard_map/all_to_all | solution.py:287
  106.5 1.1 reduce_sum.48
  107.6 5.4 %all-to-all-start.5 = ((bf16[16,32,512]{2,1,0:T(8,128)(2,1)}), bf16[16,32,512]{2,1,0:T(8,128)(2,1)S(1)}, u32[]{:S(2)}, u32[]{:S(2)}) async-start(bf16[16,32,512]{2,1,0:T(8,128)(2,1)} %bitcast.6), calls=%async_computation.5 | async-start | bytes 1048576 | tf_op jit(solution)/shard_map/all_to_all | solution.py:289
  112.9 10.7 %all-to-all-done.5 = bf16[16,32,512]{2,1,0:T(8,128)(2,1)S(1)} async-done(((bf16[16,32,512]{2,1,0:T(8,128)(2,1)}), bf16[16,32,512]{2,1,0:T(8,128)(2,1)S(1)}, u32[]{:S(2)}, u32[]{:S(2)}) %all-to-all-start.5) | async-done | bytes 524320 | tf_op jit(solution)/shard_map/all_to_all | solution.py:289
  123.6 0.1 convert_reduce_fusion
  123.7 0.7 broadcast_divide_fusion
  (19 shorter events, 0.1 us)
Async XLA Ops:
  6.5 21.4 %copy-start.7 = (s32[100]{0:T(128)S(1)}, s32[100]{0:T(128)}, u32[]{:S(2)}) copy-start(s32[100]{0:T(128)} %param.14) | copy-start | bytes 1204
  10.1 17.2 %all-to-all-start = ((bf16[16,8,640]{2,1,0:T(8,128)(2,1)}), bf16[16,8,640]{2,1,0:T(8,128)(2,1)S(1)}, u32[]{:S(2)}, u32[]{:S(2)}) async-start(bf16[16,8,640]{2,1,0:T(8,128)(2,1)} %get-tuple-element.13), calls=%async_computation | async-start | bytes 327680 | tf_op jit(solution)/shard_map/all_to_all | solution.py:259
  17.5 72.7 %all-gather.2.cloned.1.call-start = ((), (), s32[]{:S(2)}) async-start(), calls=%async_computation.6 | async-start | bytes 1474560 | tf_op jit(solution)/shard_map/all_gather | solution.py:261
  17.5 9.7 %collective-permute-start = (f32[300,256]{1,0:T(8,128)}, f32[300,256]{1,0:T(8,128)S(1)}, u32[]{:S(2)}, u32[]{:S(2)}) collective-permute-start(f32[300,256]{1,0:T(8,128)} %get-tuple-element.14), channel_id=1, source_target_pairs={{2,0},{4,2},{6,4},{8,6},{10,8},{12,10},{14,12},{16,14},{18,16},{20... | collective-permute-start | bytes 921608 | tf_op jit(solution)/shard_map/ppermute | solution.py:36
  27.3 0.7 copy-start.6
  28.1 1.4 %copy-start = (bf16[300,2560]{1,0:T(8,128)(2,1)S(1)}, bf16[300,2560]{1,0:T(8,128)(2,1)}, u32[]{:S(2)}) copy-start(bf16[300,2560]{1,0:T(8,128)(2,1)} %raw_ref.3) | copy-start | bytes 4608004
  29.5 0.9 copy-start.1
  30.5 0.7 copy-start.2
  31.1 59.0 %copy-start.4 = (bf16[128,128]{1,0:T(8,128)(2,1)S(1)}, bf16[128,128]{1,0:T(8,128)(2,1)}, u32[]{:S(2)}) copy-start(bf16[128,128]{1,0:T(8,128)(2,1)} %constant.18.clone.second_ref) | copy-start | bytes 98308
  31.1 59.0 %copy-start.5 = (bf16[128,128]{1,0:T(8,128)(2,1)S(1)}, bf16[128,128]{1,0:T(8,128)(2,1)}, u32[]{:S(2)}) copy-start(bf16[128,128]{1,0:T(8,128)(2,1)} %constant.17.clone.first_ref) | copy-start | bytes 98308
  76.5 13.5 %all-to-all-start.3 = ((f32[4,1,32]{2,1,0:T(1,128)}), f32[4,1,32]{2,1,0:T(1,128)S(1)}, u32[]{:S(2)}, u32[]{:S(2)}) async-start(f32[4,1,32]{2,1,0:T(1,128)} %bitcast.4), calls=%async_computation.3 | async-start | bytes 4096 | tf_op jit(solution)/shard_map/all_to_all | solution.py:283
  90.2 1.3 %copy-start.3 = (bf16[128,8,640]{2,1,0:T(8,128)(2,1)S(1)}, bf16[128,8,640]{2,1,0:T(8,128)(2,1)}, u32[]{:S(2)}) copy-start(bf16[128,8,640]{2,1,0:T(8,128)(2,1)} %all-gather.2.cloned.1.call-done) | copy-start | bytes 3932164
  107.6 16.1 %all-to-all-start.5 = ((bf16[16,32,512]{2,1,0:T(8,128)(2,1)}), bf16[16,32,512]{2,1,0:T(8,128)(2,1)S(1)}, u32[]{:S(2)}, u32[]{:S(2)}) async-start(bf16[16,32,512]{2,1,0:T(8,128)(2,1)} %bitcast.6), calls=%async_computation.5 | async-start | bytes 1048576 | tf_op jit(solution)/shard_map/all_to_all | solution.py:289
Sparse Core Ops, SparseCore 0:
  28.1 59.2 all-gather.1

commit v11 on v10

--- a/solution.py
+++ b/solution.py
@@ -213,7 +213,7 @@
             pltpu.VMEM((ROWS // PAIR * LANES, depth), jnp.bfloat16),
             pltpu.VMEM((depth, PIECES * WIDE), jnp.bfloat16),
         ],
-        compiler_params=params(48),
+        compiler_params=params(63),
         cost_estimate=pl.CostEstimate(flops=flops, bytes_accessed=4 << 20, transcendentals=0),
     )(gathered, first, second, traces, root_power)
 

time: 132 us -> 135 us (1.023)
  Pallas kernels: 15.1 us -> 17.4 us
    pallas_call x1, Pallas kernels: 9.24 us -> 11.6 us  [correlate(): pl.pallas_call(corr_kernel, grid=(GROUPS // PIECES,), in_specs=[whole(gat...]
    unnamed x16 -> x12, local copies, waits for them, and re-layouts: 4.95 us -> 3.64 us
  transfers between devices with their start and end apart: 5 -> 5, of which waited for: 3 -> 3; matrix products, arithmetic and copies ran while one was open for 1% -> 2% of each run, Pallas kernels for 2% -> 2%
where the time goes in v11:
time: 135 us; the launch traced here: 134 us
  blocking collectives  48 us (36%)
  waiting for transfers between devices  23.6 us (17%)
  starting transfers between devices  22.9 us (17%)
  Pallas kernels  17.4 us (13%)
  between operations  14.2 us (11%)
  local copies, waits for them, and re-layouts  5.47 us (4%)
  other arithmetic  2.25 us (2%)
    all_to_all x1, blocking collectives, local(): traces = lax.all_to_all(traces, ('y', 'xl'), 0, 0, tiled=True)  22.5 us
    all_to_all x1, blocking collectives, local(): facts = lax.all_to_all(facts, ('zq', 'zp'), 0, 0, tiled=True)  18.6 us
    pallas_call x1, Pallas kernels, correlate(): pl.pallas_call(corr_kernel, grid=(GROUPS // PIECES,), in_specs=[whole(gat...  11.6 us
    all_to_all x1, waiting for transfers between devices, local(): sums = lax.all_to_all(sums, ('xh', 'y', 'xl'), 0, 0, tiled=True)  10.7 us
    all_to_all x1, starting transfers between devices, local(): lax.all_to_all(norms, ('xh', 'core'), 0, 0, tiled=True)  9.17 us
    ppermute x1, waiting for transfers between devices, from_next_block(): return lax.ppermute(value, BLK, [(i + 1, i) for i in range(count - 1)])  8.42 us
    all_to_all x1, starting transfers between devices, local(): exchanged = lax.all_to_all(message, ('y', 'xl', 'zp'), 0, 0, tiled=True)  7.41 us
    all_to_all x1, blocking collectives, local(): sums = jnp.sum(lax.all_to_all(sums, 'core', 0, 0, tiled=True), axis=0)  6.93 us
  transfers between devices with their start and end apart: 5, of which 3 were waited for; matrix products, arithmetic and copies ran while one was open for 2% of the time, Pallas kernels for 2%

profile of v11, /device:TPU:1, one launch (start us, length us, event | category | flops | bytes accessed | tf_op | source)
XLA Modules:
  0.0 133.9 jit_solution(11878060562320235899)
XLA Ops:
  7.2 2.9 %shard_map.91 = (bf16[16,8,640]{2,1,0:T(8,128)(2,1)}, f32[300,256]{1,0:T(8,128)}, f32[1,128]{1,0:T(1,128)}, bf16[128,768]{1,0:T(8,128)(2,1)}) custom-call(s32[1]{0:T(128)S(6)} %copy.21.start_ref, bf16[1,60]{1,0:T(2,128)(2,1)} %bitcast.10, bf16[1,300,256]{2,1,0:T(8,128)(2,1)} %template_ref.1, s32[1,300]{1,0:T(1,128)} %mask_ref.1, ...), custom_call_target="tpu_custom_call" | custom-call | flops 134217728 | bytes 2097152 | tf_op jit(solution)/shard_map/pallas_call | solution.py:232
  10.1 7.4 %all-to-all-start = ((bf16[16,8,640]{2,1,0:T(8,128)(2,1)}), bf16[16,8,640]{2,1,0:T(8,128)(2,1)S(1)}, u32[]{:S(2)}, u32[]{:S(2)}) async-start(bf16[16,8,640]{2,1,0:T(8,128)(2,1)} %get-tuple-element.13), calls=%async_computation | async-start | bytes 327680 | tf_op jit(solution)/shard_map/all_to_all | solution.py:259
  17.5 0.0 all-gather.2.cloned.1.call-start
  17.5 1.3 collective-permute-start
  18.8 8.4 %collective-permute-done.rim_ref = f32[300,256]{1,0:T(8,128)S(1)} collective-permute-done((f32[300,256]{1,0:T(8,128)}, f32[300,256]{1,0:T(8,128)S(1)}, u32[]{:S(2)}, u32[]{:S(2)}) %collective-permute-start) | collective-permute-done | bytes 307232 | tf_op jit(solution)/shard_map/ppermute | solution.py:36
  27.3 0.7 copy-done.4
  27.9 0.0 all-gather.2.cloned.1.call-update
  28.0 0.1 broadcast_in_dim.20
  28.0 0.1 broadcast_in_dim_reshape.4.shift_ref
  28.1 0.0 copy-start
  28.2 1.4 %copy-done = bf16[300,2560]{1,0:T(8,128)(2,1)S(1)} copy-done((bf16[300,2560]{1,0:T(8,128)(2,1)S(1)}, bf16[300,2560]{1,0:T(8,128)(2,1)}, u32[]{:S(2)}) %copy-start) | copy-done | bytes 1536024
  29.5 0.9 copy-done.1
  30.5 0.7 copy-done.2
  31.1 3.0 %shard_map.92 = f32[8,40,640]{2,1,0:T(8,128)S(1)} custom-call(f32[1,128]{1,0:T(1,128)S(1)} %copy-done.2, bf16[300,2560]{1,0:T(8,128)(2,1)S(1)} %copy-done, f32[300,256]{1,0:T(8,128)S(1)} %collective-permute-done.rim_ref, bf16[128,768]{1,0:T(8,128)(2,1)S(1)} %copy-done.1, s32[300,1]{1,0:T(8,128)S(1)} %broadcast_in_dim_reshape.4.shift_ref), custom_call_target="tpu_custom_call" | custom-call | flops 419430400 | bytes 4194304 | tf_op jit(solution)/shard_map/pallas_call | solution.py:264
  34.1 22.5 %all_to_all.34.trace_ref = f32[8,40,640]{2,1,0:T(8,128)S(1)} all-to-all(f32[8,40,640]{2,1,0:T(8,128)S(1)} %shard_map.92), channel_id=1, replica_groups=mesh['xh'=2,'y'=4,'xl'=2,'zq'=8,'zp'=2,'core'=2] {'y','xl'}, dimensions={0} | all-to-all | bytes 1638400 | tf_op jit(solution)/shard_map/all_to_all | solution.py:272
  56.6 0.1 slice_reduce_fusion.2
  56.7 0.2 slice_reduce_fusion
  57.0 0.1 pad_maximum_fusion
  57.1 18.6 %all_to_all.35 = f32[16,1,128]{2,1,0:T(1,128)S(1)} all-to-all(f32[16,1,128]{2,1,0:T(1,128)S(1)} %broadcast_in_dim.22), channel_id=1, replica_groups=mesh['xh'=2,'y'=4,'xl'=2,'zq'=8,'zp'=2,'core'=2] {'zq','zp'}, dimensions={0} | all-to-all | bytes 16384 | tf_op jit(solution)/shard_map/all_to_all | solution.py:279
  75.7 0.1 slice_bitcast_fusion
  75.7 0.1 copy.18
  75.8 0.7 reshape.17
  76.5 9.2 %all-to-all-start.3 = ((f32[4,1,32]{2,1,0:T(1,128)}), f32[4,1,32]{2,1,0:T(1,128)S(1)}, u32[]{:S(2)}, u32[]{:S(2)}) async-start(f32[4,1,32]{2,1,0:T(1,128)} %bitcast.4), calls=%async_computation.3 | async-start | bytes 4096 | tf_op jit(solution)/shard_map/all_to_all | solution.py:283
  85.7 4.5 %all-to-all-done.3 = f32[4,1,32]{2,1,0:T(1,128)S(1)} async-done(((f32[4,1,32]{2,1,0:T(1,128)}), f32[4,1,32]{2,1,0:T(1,128)S(1)}, u32[]{:S(2)}, u32[]{:S(2)}) %all-to-all-start.3) | async-done | bytes 544 | tf_op jit(solution)/shard_map/all_to_all | solution.py:283
  90.2 0.7 copy.20.root_ref
  90.9 11.6 %shard_map.93 = f32[2,2,8,32,512]{4,3,2,1,0:T(8,128)} custom-call(bf16[1024,640]{1,0:T(8,128)(2,1)} %bitcast.12, bf16[128,128]{1,0:T(8,128)(2,1)} %constant.17.clone.first_ref, bf16[128,128]{1,0:T(8,128)(2,1)} %constant.18.clone.second_ref, f32[8,40,640]{2,1,0:T(8,128)} %copy-done.3, f32[40,1]{1,0:T(8,128)} %copy.20.root_ref), custom_call_target="tpu_custom_call" | custom-call | flops 6710886400 | bytes 4194304 | tf_op jit(solution)/shard_map/pallas_call | solution.py:199
  102.5 6.9 %all_to_all.36 = f32[2,2,8,32,512]{4,3,2,1,0:T(8,128)S(1)} all-to-all(f32[2,2,8,32,512]{4,3,2,1,0:T(8,128)} %shard_map.93), channel_id=1, replica_groups=mesh['xh'=2,'y'=4,'xl'=2,'zq'=8,'zp'=2,'core'=2] {'core'}, dimensions={0} | all-to-all | bytes 4194304 | tf_op jit(solution)/shard_map/all_to_all | solution.py:287
  109.4 1.1 reduce_sum.48
  110.5 5.0 %all-to-all-start.5 = ((bf16[16,32,512]{2,1,0:T(8,128)(2,1)}), bf16[16,32,512]{2,1,0:T(8,128)(2,1)S(1)}, u32[]{:S(2)}, u32[]{:S(2)}) async-start(bf16[16,32,512]{2,1,0:T(8,128)(2,1)} %bitcast.6), calls=%async_computation.5 | async-start | bytes 1048576 | tf_op jit(solution)/shard_map/all_to_all | solution.py:289
  115.5 10.7 %all-to-all-done.5 = bf16[16,32,512]{2,1,0:T(8,128)(2,1)S(1)} async-done(((bf16[16,32,512]{2,1,0:T(8,128)(2,1)}), bf16[16,32,512]{2,1,0:T(8,128)(2,1)S(1)}, u32[]{:S(2)}, u32[]{:S(2)}) %all-to-all-start.5) | async-done | bytes 524320 | tf_op jit(solution)/shard_map/all_to_all | solution.py:289
  126.2 0.1 convert_reduce_fusion
  126.3 0.7 broadcast_divide_fusion
  (15 shorter events, 0.1 us)
Async XLA Ops:
  6.5 21.4 %copy-start.5 = (s32[100]{0:T(128)S(1)}, s32[100]{0:T(128)}, u32[]{:S(2)}) copy-start(s32[100]{0:T(128)} %param.14) | copy-start | bytes 1204
  10.1 17.2 %all-to-all-start = ((bf16[16,8,640]{2,1,0:T(8,128)(2,1)}), bf16[16,8,640]{2,1,0:T(8,128)(2,1)S(1)}, u32[]{:S(2)}, u32[]{:S(2)}) async-start(bf16[16,8,640]{2,1,0:T(8,128)(2,1)} %get-tuple-element.13), calls=%async_computation | async-start | bytes 327680 | tf_op jit(solution)/shard_map/all_to_all | solution.py:259
  17.5 73.4 %all-gather.2.cloned.1.call-start = ((), (), s32[]{:S(2)}) async-start(), calls=%async_computation.6 | async-start | bytes 1474560 | tf_op jit(solution)/shard_map/all_gather | solution.py:261
  17.5 9.7 %collective-permute-start = (f32[300,256]{1,0:T(8,128)}, f32[300,256]{1,0:T(8,128)S(1)}, u32[]{:S(2)}, u32[]{:S(2)}) collective-permute-start(f32[300,256]{1,0:T(8,128)} %get-tuple-element.14), channel_id=1, source_target_pairs={{2,0},{4,2},{6,4},{8,6},{10,8},{12,10},{14,12},{16,14},{18,16},{20... | collective-permute-start | bytes 921608 | tf_op jit(solution)/shard_map/ppermute | solution.py:36
  27.3 0.7 copy-start.4
  28.1 1.4 %copy-start = (bf16[300,2560]{1,0:T(8,128)(2,1)S(1)}, bf16[300,2560]{1,0:T(8,128)(2,1)}, u32[]{:S(2)}) copy-start(bf16[300,2560]{1,0:T(8,128)(2,1)} %raw_ref.3) | copy-start | bytes 4608004
  29.5 0.9 copy-start.1
  30.5 0.7 copy-start.2
  56.6 34.3 %copy-start.3 = (f32[8,40,640]{2,1,0:T(8,128)}, f32[8,40,640]{2,1,0:T(8,128)S(1)}, u32[]{:S(2)}) copy-start(f32[8,40,640]{2,1,0:T(8,128)S(1)} %all_to_all.34.trace_ref) | copy-start | bytes 2457604
  76.5 13.7 %all-to-all-start.3 = ((f32[4,1,32]{2,1,0:T(1,128)}), f32[4,1,32]{2,1,0:T(1,128)S(1)}, u32[]{:S(2)}, u32[]{:S(2)}) async-start(f32[4,1,32]{2,1,0:T(1,128)} %bitcast.4), calls=%async_computation.3 | async-start | bytes 4096 | tf_op jit(solution)/shard_map/all_to_all | solution.py:283
  110.5 15.7 %all-to-all-start.5 = ((bf16[16,32,512]{2,1,0:T(8,128)(2,1)}), bf16[16,32,512]{2,1,0:T(8,128)(2,1)S(1)}, u32[]{:S(2)}, u32[]{:S(2)}) async-start(bf16[16,32,512]{2,1,0:T(8,128)(2,1)} %bitcast.6), calls=%async_computation.5 | async-start | bytes 1048576 | tf_op jit(solution)/shard_map/all_to_all | solution.py:289
Sparse Core Ops, SparseCore 0:
  28.1 59.0 all-gather.1
